TPU v7x, 32 devices: a whole 2x2x4 slice. The times are simulated.
32 devices in a mesh: seq: 8 (over y, x, core), head: 4 (over z).
Axes of the slice: x: 2, y: 2, z: 4, core: 2. Of those that a mesh axis runs over, the one named last changes fastest.
Arguments:
- tokens: bfloat16 [8192, 512], P(('seq', 'head')), may hold values from -6 to 6
- w_proj: bfloat16 [512, 2048], replicated, may hold values from -0.25 to 0.25
- w_out: bfloat16 [512, 512], replicated, may hold values from -0.25 to 0.25
- tile_user: int32 [64], replicated, may hold values from 0 to 15, never falling along the last dimension, each value on 1 to 40 neighbouring positions
Outputs:
- mixed: bfloat16 [8192, 512], P(('seq', 'head'))
Inputs may be any that keep to these rules, and one draw needn't show every extreme that they name: `tile_user`: tile users never fall along the tiles; each user covers 1 to 40 tiles, one exactly 40; every number of 0 to 15 occurs.
All inputs are finite; a program needn't handle non-finite values.
Results may differ from a plain program's by a relative error of at most 0.0052.
Values may be sent and summed in bfloat16 or wider, within the bound.
No kernel may reach another device: no remote copies, remote signals or barrier semaphores. Data moves between devices by JAX's collectives and lax.ppermute only.
A program may use at most 128 MiB of HBM per device.

v0:
```python
import functools

import jax
import jax.numpy as jnp
from jax import lax
from jax.experimental import pallas as pl
from jax.experimental.pallas import tpu as pltpu
from jax.sharding import PartitionSpec as P

H = 8
DH = 64
TILE = 128
LANES = 2 * DH
TEAM = H // 2

epsilon = 1e-05

f32 = jnp.float32
bf16 = jnp.bfloat16


def layer_norm(values):
    center = values - jnp.mean(values, axis=-1, keepdims=True)
    spread = jnp.mean(center * center, axis=-1, keepdims=True)
    return center * lax.rsqrt(spread + epsilon)


def silu(values):
    half = values * 0.5
    return half + half * jnp.tanh(half)


def swap_halves(values):
    return pltpu.roll(values, DH, 1)


def low_lanes(rows):
    return lax.broadcasted_iota(jnp.int32, (rows, LANES), 1) < DH


def project_keys(me_ref, tokens_ref, value_weights, key_weights, *refs):
    outs, held = refs[:-1], refs[-1]
    rows = tokens_ref.shape[0]
    normed = layer_norm(tokens_ref[...].astype(f32)).astype(bf16)
    low = low_lanes(rows)
    for pair in range(H // 2):
        at = slice(pair * LANES, (pair + 1) * LANES)
        values = silu(jnp.dot(normed, value_weights[:, at], preferred_element_type=f32))
        keys = silu(jnp.dot(normed, key_weights[:, at], preferred_element_type=f32))
        held[2 * pair] = jnp.where(low, keys, swap_halves(values)).astype(bf16)
        held[2 * pair + 1] = jnp.where(low, swap_halves(keys), values).astype(bf16)
    for k, out in enumerate(outs):
        out[...] = held[jnp.bitwise_xor(me_ref[0], k)]


def project_queries(me_ref, tokens_ref, query_weights, gating_weights, *refs):
    outs, gating, held = refs[:-2], refs[-2], refs[-1]
    rows = tokens_ref.shape[0]
    half = rows // 2
    normed = layer_norm(tokens_ref[...].astype(f32)).astype(bf16)
    low = low_lanes(half)
    scale = 0.5 * DH ** (-0.5)
    for pair in range(H // 2):
        at = slice(pair * LANES, (pair + 1) * LANES)
        queries = silu(jnp.dot(normed, query_weights[:, at], preferred_element_type=f32)) * scale
        upper, lower = queries[:half], queries[half:]
        held[2 * pair] = jnp.where(low, upper, swap_halves(lower)).astype(bf16)
        held[2 * pair + 1] = jnp.where(low, swap_halves(upper), lower).astype(bf16)
        gating[:, at] = silu(
            jnp.dot(normed, gating_weights[:, at], preferred_element_type=f32)
        ).astype(bf16)
    for k, out in enumerate(outs):
        out[...] = held[jnp.bitwise_xor(me_ref[0], k)]


def attend(
    opens, closes, reach_ref, start_ref, inverse_ref, block_ref, slot_ref, queries_ref, *refs
):
    step = pl.program_id(0)
    held, total, queries, sems = refs[-4:]
    out_ref = refs[-5]
    parts = refs[: -5 if opens else -6]
    rows = held.shape[1]
    half = rows // 2
    tiles = rows // TILE

    @pl.when(step == 0)
    def _():
        copies, at = [], 0
        for i, part in enumerate(parts):
            copies.append(
                pltpu.make_async_copy(part, held.at[pl.ds(at, part.shape[0])], sems.at[i])
            )
            at += part.shape[0]
        for copy in copies:
            copy.start()
        for copy in copies:
            copy.wait()

    low = low_lanes(half)
    blocks = [block_ref[reach_ref[2] + step * TEAM + i] for i in range(TEAM)]
    for i in range(TEAM):
        packed = queries_ref[i].astype(f32)
        queries[i * rows : i * rows + half] = jnp.where(low, packed, 0.0).astype(bf16)
        queries[i * rows + half : (i + 1) * rows] = jnp.where(
            low, swap_halves(packed), 0.0
        ).astype(bf16)
    starts = [start_ref[block * tiles + j] for block in blocks for j in range(tiles)]
    least, low_start, high_start = blocks[0], starts[0], starts[0]
    for block in blocks[1:]:
        least = jnp.minimum(least, block)
    for start in starts[1:]:
        low_start = jnp.minimum(low_start, start)
        high_start = jnp.maximum(high_start, start)
    total[...] = jnp.zeros_like(total) if opens else refs[-6][...]

    def add(key_block, count, masked):
        key_rows = [held[slot_ref[key_block + i]] for i in range(count)]
        key_rows = key_rows[0] if count == 1 else jnp.concatenate(key_rows, axis=0)
        if masked:
            column = lax.broadcasted_iota(jnp.int32, (TILE, count * rows), 1)
            ahead = column - lax.broadcasted_iota(jnp.int32, (TILE, count * rows), 0)
        for i in range(TEAM):
            at = slice(i * rows, (i + 1) * rows)
            score = lax.dot_general(
                queries[at], key_rows, (((1,), (1,)), ((), ())), preferred_element_type=f32
            )
            weights = score + score * jnp.tanh(score)
            if masked:
                pieces = []
                for j in range(tiles):
                    from_start = starts[i * tiles + j] * TILE - key_block * rows
                    to_row = (blocks[i] - key_block) * rows + j * TILE
                    allowed = (column >= from_start) & (ahead <= to_row)
                    pieces.append(jnp.where(allowed, weights[j * TILE : (j + 1) * TILE], 0.0))
                weights = jnp.concatenate(pieces, axis=0)
            total[at] += jnp.dot(weights.astype(bf16), key_rows, preferred_element_type=f32)

    def loop(begin, end, count, masked):
        def body(index, carry):
            add(begin + index * count, count, masked)
            return carry

        lax.fori_loop(0, jnp.maximum(end - begin, 0) // count, body, 0)

    reach_low, reach_high = reach_ref[0], jnp.minimum(reach_ref[1], least)
    first = jnp.maximum(low_start // tiles, reach_low)
    whole = jnp.maximum(first, jnp.minimum((high_start + tiles - 1) // tiles, reach_high))
    even = jnp.maximum(whole, jnp.minimum((whole + TEAM - 1) // TEAM * TEAM, reach_high))
    loop(first, whole, 1, True)
    loop(whole, even, 1, False)
    loop(even, reach_high, TEAM, False)

    @pl.when(least < reach_ref[1])
    def _():
        add(least, TEAM, True)

    if not closes:
        out_ref[...] = total[...]
        return
    for i in range(TEAM):
        at = i * rows
        upper = total[at : at + half] * inverse_ref[blocks[i] * tiles]
        lower = total[at + half : at + rows] * inverse_ref[blocks[i] * tiles + tiles - 1]
        out_ref[i] = jnp.where(low, swap_halves(upper), lower).astype(bf16)


def attend_call(tables, reach, queries, parts, before=None, closes=True):
    half, rows = queries.shape[1], 2 * queries.shape[1]
    steps = queries.shape[0] // TEAM
    held_blocks = sum(array.shape[0] for array in parts)
    totals = pl.BlockSpec((TEAM * rows, LANES), lambda i, *_: (i, 0))
    packed = pl.BlockSpec((TEAM, half, LANES), lambda i, *_: (i, 0, 0))
    extra = [] if before is None else [before]
    return pl.pallas_call(
        functools.partial(attend, before is None, closes),
        grid_spec=pltpu.PrefetchScalarGridSpec(
            num_scalar_prefetch=5,
            grid=(steps,),
            in_specs=[packed] + [ANY] * len(parts) + [totals] * len(extra),
            out_specs=packed if closes else totals,
            scratch_shapes=[
                pltpu.VMEM((held_blocks, rows, LANES), bf16),
                pltpu.VMEM((TEAM * rows, LANES), f32),
                pltpu.VMEM((TEAM * rows, LANES), bf16),
                pltpu.SemaphoreType.DMA((len(parts),)),
            ],
        ),
        out_shape=jax.ShapeDtypeStruct(queries.shape, bf16)
        if closes
        else jax.ShapeDtypeStruct((steps * TEAM * rows, LANES), f32),
        compiler_params=pltpu.CompilerParams(vmem_limit_bytes=40 << 20),
        cost_estimate=pl.CostEstimate(
            flops=steps * 2_000_000_000, bytes_accessed=4_000_000, transcendentals=4_000_000
        ),
        name="attend",
    )(reach, *tables, queries, *parts, *extra)


def finish(me_ref, tokens_ref, attention_ref, gating_ref, weights_ref, out_ref):
    rows = tokens_ref.shape[0]
    half = rows // 2
    low = low_lanes(half)
    uppers, lowers = [], []
    for pair in range(H // 2):
        one = attention_ref[jnp.bitwise_xor(me_ref[0], 2 * pair)].astype(f32)
        two = attention_ref[jnp.bitwise_xor(me_ref[0], 2 * pair + 1)].astype(f32)
        uppers.append(jnp.where(low, one, swap_halves(two)))
        lowers.append(jnp.where(low, swap_halves(one), two))
    attention = jnp.concatenate(
        [jnp.concatenate(uppers, axis=1), jnp.concatenate(lowers, axis=1)], axis=0
    )
    gated = (layer_norm(attention) * gating_ref[...].astype(f32)).astype(bf16)
    mixed = tokens_ref[...].astype(f32) + jnp.dot(
        gated, weights_ref[...], preferred_element_type=f32
    )
    out_ref[...] = mixed.astype(bf16)


VMEM = pl.BlockSpec(memory_space=pltpu.VMEM)
SMEM = pl.BlockSpec(memory_space=pltpu.SMEM)
ANY = pl.BlockSpec(memory_space=pl.ANY)


def columns_of(width, block):
    return pl.BlockSpec((width, H * DH), lambda i: (0, block))


def per_device(seq_size, head_size, tokens, w_proj, w_out, tile_user):
    rows, width = tokens.shape
    half = rows // 2
    tiles = rows // TILE
    blocks = seq_size * head_size
    seq, head = lax.axis_index("seq"), lax.axis_index("head")
    fold = H // head_size
    share = fold
    groups = seq_size // (fold * share)
    group, part, core = seq // (fold * share), (seq // share) % fold, seq % share
    me = part * head_size + head
    me_array = me.reshape(1).astype(jnp.int32)

    def partner(array, k):
        if k == 0:
            return array
        pairs = []
        for s in range(seq_size):
            for h in range(head_size):
                g, p, c = s // (fold * share), (s // share) % fold, s % share
                other = (p * head_size + h) ^ k
                t = (g * fold + other // head_size) * share + c
                pairs.append((s * head_size + h, t * head_size + other % head_size))
        return lax.ppermute(array, ("seq", "head"), pairs)

    def seq_flip(array, bit):
        return lax.ppermute(array, "seq", [(s, s ^ bit) for s in range(seq_size)])

    keys_sent = pl.pallas_call(
        project_keys,
        out_shape=[jax.ShapeDtypeStruct((rows, LANES), bf16)] * H,
        grid=(1,),
        in_specs=[SMEM, VMEM, columns_of(width, 1), columns_of(width, 3)],
        out_specs=[VMEM] * H,
        scratch_shapes=[pltpu.VMEM((H, rows, LANES), bf16)],
        name="project_keys",
    )(me_array, tokens, w_proj, w_proj)
    queries_sent = pl.pallas_call(
        project_queries,
        out_shape=[jax.ShapeDtypeStruct((half, LANES), bf16)] * H
        + [jax.ShapeDtypeStruct((rows, H * DH), bf16)],
        grid=(1,),
        in_specs=[SMEM, VMEM, columns_of(width, 2), columns_of(width, 0)],
        out_specs=[VMEM] * (H + 1),
        scratch_shapes=[pltpu.VMEM((H, half, LANES), bf16)],
        name="project_queries",
    )(me_array, tokens, w_proj, w_proj)
    gating = queries_sent[-1]

    index = jnp.arange(blocks, dtype=jnp.int32)
    block_head, block_seq = index % head_size, index // head_size
    block_core = block_seq % share
    block_me = (block_seq // share % fold) * head_size + block_head
    block_group = block_seq // (share * fold)
    from_me = jnp.bitwise_xor(block_me, me)
    asked = jnp.arange(H, dtype=jnp.int32) ^ me
    query_block = (
        (group * fold + asked // head_size) * share + core
    ) * head_size + asked % head_size
    start = jnp.sum((tile_user[None, :] < tile_user[:, None]).astype(jnp.int32), axis=1)
    length = jnp.sum((tile_user[None, :] == tile_user[:, None]).astype(f32), axis=1) * TILE

    def reach(first, last, query):
        return jnp.stack([jnp.asarray(v, jnp.int32) for v in (first, last, query)])

    arrived = [partner(keys_sent[k], k) for k in range(H)]
    last = arrived[-1]
    to_send, _ = lax.optimization_barrier((tuple(queries_sent[:H]), last))
    queries = jnp.stack([partner(to_send[k], k) for k in range(H)])
    if groups == 2 and share == 2:
        lots = [jnp.stack(arrived[:TEAM]), jnp.stack(arrived[TEAM:])]
        far = [seq_flip(lot, fold * share) for lot in lots]
        near = lots + [seq_flip(lot, 1) for lot in lots]
        far = far + [seq_flip(lot, 1) for lot in far]
        slot = jnp.bitwise_xor(block_core, core) * H + from_me
        tables = (start, 1.0 / length, query_block, slot)
        bound = group * (blocks // groups)
        totals = attend_call(tables, reach(bound, blocks, 0), queries, near, closes=False)
        size = totals.shape[0] // 2
        attention = [None] * H
        for begin in (TEAM, 0):
            team = attend_call(
                tables,
                reach(0, bound, begin),
                queries[begin : begin + TEAM],
                far,
                before=totals[size * (begin // TEAM) : size * (begin // TEAM + 1)],
            )
            for k in range(TEAM):
                attention[begin + k] = team[k]
    else:
        everything = lax.all_gather(jnp.stack(arrived), "seq", axis=0, tiled=True)
        tables = (start, 1.0 / length, query_block, block_seq * H + from_me)
        attention = attend_call(tables, reach(0, blocks, 0), queries, [everything])
    returned = jnp.stack([partner(attention[k], k) for k in range(H)])
    return pl.pallas_call(
        finish,
        out_shape=jax.ShapeDtypeStruct((rows, width), bf16),
        in_specs=[SMEM, VMEM, VMEM, VMEM, VMEM],
        out_specs=VMEM,
        name="finish",
    )(me_array, tokens, returned, gating, w_out)


def solution(mesh):
    placed = (P(("seq", "head"), None), P(), P(), P())
    return jax.shard_map(
        functools.partial(per_device, mesh.shape["seq"], mesh.shape["head"]),
        mesh=mesh,
        in_specs=placed,
        out_specs=P(("seq", "head"), None),
        check_vma=False,
    )
```

profile of v0, /device:TPU:5, one launch (start us, length us, event | category | flops | bytes accessed | tf_op | source)
XLA Modules:
  0.0 79.5 jit_solution(4014801668940396406)
XLA Ops:
  0.0 3.1 %project_keys.1 = (bf16[256,128]{1,0:T(8,128)(2,1)}, bf16[256,128]{1,0:T(8,128)(2,1)}, bf16[256,128]{1,0:T(8,128)(2,1)}, bf16[256,128]{1,0:T(8,128)(2,1)}, bf16[...) custom-call(s32[1]{0:T(128)} %bitcast.me_ref, ...), custom_call_target="tpu_custom_call" | custom-call | tf_op jit(solution)/shard_map/project_keys/pallas_call | solution.py:257
  3.1 4.2 %collective-permute-start = (bf16[256,128]{1,0:T(8,128)(2,1)}, bf16[256,128]{1,0:T(8,128)(2,1)S(1)}, u32[]{:S(2)}, u32[]{:S(2)}) collective-permute-start(bf16[256,128]{1,0:T(8,128)(2,1)} %get-tuple-element.38), channel_id=1, source_target_pairs={{0,11},{1,10},{2,9},{3,8},{4,15},{5,14},{6,13},{7,12},{8,3},{9,2},... | collective-permute-start | bytes 196616 | tf_op jit(solution)/shard_map/ppermute | solution.py:252
  7.8 1.0 %collective-permute-start.10 = (bf16[256,128]{1,0:T(8,128)(2,1)}, bf16[256,128]{1,0:T(8,128)(2,1)S(1)}, u32[]{:S(2)}, u32[]{:S(2)}) collective-permute-start(bf16[256,128]{1,0:T(8,128)(2,1)} %get-tuple-element.49), channel_id=1, source_target_pairs={{0,10},{1,11},{2,8},{3,9},{4,14},{5,15},{6,12},{7,13},{8,2},{9,3},... | collective-permute-start | bytes 196616 | tf_op jit(solution)/shard_map/ppermute | solution.py:252
  8.8 1.2 %collective-permute-start.4 = (bf16[256,128]{1,0:T(8,128)(2,1)}, bf16[256,128]{1,0:T(8,128)(2,1)S(1)}, u32[]{:S(2)}, u32[]{:S(2)}) collective-permute-start(bf16[256,128]{1,0:T(8,128)(2,1)} %get-tuple-element.44), channel_id=1, source_target_pairs={{0,1},{1,0},{2,3},{3,2},{4,5},{5,4},{6,7},{7,6},{8,9},{9,8},{10,11... | collective-permute-start | bytes 196616 | tf_op jit(solution)/shard_map/ppermute | solution.py:252
  10.0 3.0 %project_queries.1 = (bf16[128,128]{1,0:T(8,128)(2,1)}, bf16[128,128]{1,0:T(8,128)(2,1)}, bf16[128,128]{1,0:T(8,128)(2,1)}, bf16[128,128]{1,0:T(8,128)(2,1)}, bf...) custom-call(s32[1]{0:T(128)} %bitcast.me_ref, ...), custom_call_target="tpu_custom_call" | custom-call | tf_op jit(solution)/shard_map/project_queries/pallas_call | solution.py:266
  13.8 2.4 %collective-permute-start.5 = (bf16[256,128]{1,0:T(8,128)(2,1)S(1)}, bf16[256,128]{1,0:T(8,128)(2,1)S(1)}, u32[]{:S(2)}, u32[]{:S(2)}) collective-permute-start(bf16[256,128]{1,0:T(8,128)(2,1)S(1)} %copy-done.3), channel_id=1, source_target_pairs={{0,2},{1,3},{2,0},{3,1},{4,6},{5,7},{6,4},{7,5},{8,10},{9,11},{10,... | collective-permute-start | bytes 196616 | tf_op jit(solution)/shard_map/ppermute | solution.py:252
  17.3 3.2 %collective-permute-start.2 = (bf16[128,128]{1,0:T(8,128)(2,1)}, bf16[128,128]{1,0:T(8,128)(2,1)S(1)}, u32[]{:S(2)}, u32[]{:S(2)}) collective-permute-start(bf16[128,128]{1,0:T(8,128)(2,1)} %get-tuple-element.41), channel_id=1, source_target_pairs={{0,2},{1,3},{2,0},{3,1},{4,6},{5,7},{6,4},{7,5},{8,10},{9,11},{10,... | collective-permute-start | bytes 98312 | tf_op jit(solution)/shard_map/ppermute | solution.py:252
  20.5 1.3 %collective-permute-start.14 = (bf16[128,128]{1,0:T(8,128)(2,1)}, bf16[128,128]{1,0:T(8,128)(2,1)S(1)}, u32[]{:S(2)}, u32[]{:S(2)}) collective-permute-start(bf16[128,128]{1,0:T(8,128)(2,1)} %get-tuple-element.50), channel_id=1, source_target_pairs={{0,8},{1,9},{2,10},{3,11},{4,12},{5,13},{6,14},{7,15},{8,0},{9,1},... | collective-permute-start | bytes 98312 | tf_op jit(solution)/shard_map/ppermute | solution.py:252
  21.9 1.2 %collective-permute-start.16 = (bf16[128,128]{1,0:T(8,128)(2,1)}, bf16[128,128]{1,0:T(8,128)(2,1)S(1)}, u32[]{:S(2)}, u32[]{:S(2)}) collective-permute-start(bf16[128,128]{1,0:T(8,128)(2,1)} %get-tuple-element.52), channel_id=1, source_target_pairs={{0,10},{1,11},{2,8},{3,9},{4,14},{5,15},{6,12},{7,13},{8,2},{9,3},... | collective-permute-start | bytes 98312 | tf_op jit(solution)/shard_map/ppermute | solution.py:252
  23.2 3.2 %collective-permute-start.17 = (bf16[128,128]{1,0:T(8,128)(2,1)}, bf16[128,128]{1,0:T(8,128)(2,1)S(1)}, u32[]{:S(2)}, u32[]{:S(2)}) collective-permute-start(bf16[128,128]{1,0:T(8,128)(2,1)} %get-tuple-element.53), channel_id=1, source_target_pairs={{0,11},{1,10},{2,9},{3,8},{4,15},{5,14},{6,13},{7,12},{8,3},{9,2},... | collective-permute-start | bytes 98312 | tf_op jit(solution)/shard_map/ppermute | solution.py:252
  26.4 4.4 %collective-permute-start.19 = (bf16[4,256,128]{2,1,0:T(8,128)(2,1)S(1)}, bf16[4,256,128]{2,1,0:T(8,128)(2,1)S(1)}, u32[]{:S(2)}, u32[]{:S(2)}) collective-permute-start(bf16[4,256,128]{2,1,0:T(8,128)(2,1)S(1)} %pad_maximum_fusion.1.refs_1_), channel_id=1, source_target_pairs={{0,4},{4,0},{8,12},{12,8},{16,20},{20,16},{24,28},{28,24},{1,5},{5... | collective-permute-start | bytes 786440 | tf_op jit(solution)/shard_map/ppermute | solution.py:255
  31.4 1.2 %collective-permute-start.7 = (bf16[4,256,128]{2,1,0:T(8,128)(2,1)S(1)}, bf16[4,256,128]{2,1,0:T(8,128)(2,1)S(1)}, u32[]{:S(2)}, u32[]{:S(2)}) collective-permute-start(bf16[4,256,128]{2,1,0:T(8,128)(2,1)S(1)} %pad_maximum_fusion.refs_0_), channel_id=1, source_target_pairs={{0,16},{4,20},{8,24},{12,28},{16,0},{20,4},{24,8},{28,12},{1,17},{... | collective-permute-start | bytes 786440 | tf_op jit(solution)/shard_map/ppermute | solution.py:255
  32.8 4.6 %collective-permute-done.3 = bf16[128,128]{1,0:T(8,128)(2,1)S(1)} collective-permute-done((bf16[128,128]{1,0:T(8,128)(2,1)}, bf16[128,128]{1,0:T(8,128)(2,1)S(1)}, u32[]{:S(2)}, u32[]{:S(2)}) %collective-permute-start.3) | collective-permute-done | bytes 32800 | tf_op jit(solution)/shard_map/ppermute | solution.py:252
  38.8 2.0 %collective-permute-start.13 = (bf16[4,256,128]{2,1,0:T(8,128)(2,1)S(1)}, bf16[4,256,128]{2,1,0:T(8,128)(2,1)S(1)}, u32[]{:S(2)}, u32[]{:S(2)}) collective-permute-start(bf16[4,256,128]{2,1,0:T(8,128)(2,1)S(1)} %collective-permute-done.11.refs_1_), channel_id=1, source_target_pairs={{0,4},{4,0},{8,12},{12,8},{16,20},{20,16},{24,28},{28,24},{1,5},{5... | collective-permute-start | bytes 786440 | tf_op jit(solution)/shard_map/ppermute | solution.py:255
  40.8 3.6 %collective-permute-done.7.refs_0_ = bf16[4,256,128]{2,1,0:T(8,128)(2,1)S(1)} collective-permute-done((bf16[4,256,128]{2,1,0:T(8,128)(2,1)S(1)}, bf16[4,256,128]{2,1,0:T(8,128)(2,1)S(1)}, u32[]{:S(2)}, u32[]{:S(2)}) %collective-permute-start.7) | collective-permute-done | bytes 262176 | tf_op jit(solution)/shard_map/ppermute | solution.py:255
  45.2 7.5 %attend.3 = f32[2048,128]{1,0:T(8,128)S(1)} custom-call(s32[3]{0:T(128)S(1)} %pad_add_fusion.reach_ref, s32[64]{0:T(128)S(1)} %convert_reduce_fusion.1.start_ref, f32[64]{0:T(128)S(1)} %multiply_divide_fusion.inverse_ref, s32[8]{0:T(128)S(1)} %fusion.1.block_ref, s32[32]{0:T(128)S(1)} %fusion.3.slot_ref, ...), custom_call_target="tpu_custom_call" | custom-call | flops 4000000000 | bytes 4000000 | tf_op jit(solution)/shard_map/attend/pallas_call | solution.py:175
  52.8 10.7 %attend.4 = bf16[4,128,128]{2,1,0:T(8,128)(2,1)S(1)} custom-call(s32[3]{0:T(128)S(1)} %pad_add_fusion.1.reach_ref, s32[64]{0:T(128)S(1)} %convert_reduce_fusion.1.start_ref, f32[64]{0:T(128)S(1)} %multiply_divide_fusion.inverse_ref, s32[8]{0:T(128)S(1)} %fusion.1.block_ref, s32[32]{0:T(128)S(1)} %fusion.3.slot_ref, ...), custom_call_target="tpu_custom_call" | custom-call | flops 2000000000 | bytes 4000000 | tf_op jit(solution)/shard_map/attend/pallas_call | solution.py:175
  63.6 1.0 %attend.5 = bf16[4,128,128]{2,1,0:T(8,128)(2,1)S(1)} custom-call(s32[3]{0:T(128)S(1)} %pad_add_fusion.3.reach_ref, s32[64]{0:T(128)S(1)} %convert_reduce_fusion.1.start_ref, f32[64]{0:T(128)S(1)} %multiply_divide_fusion.inverse_ref, s32[8]{0:T(128)S(1)} %fusion.1.block_ref, s32[32]{0:T(128)S(1)} %fusion.3.slot_ref, ...), custom_call_target="tpu_custom_call" | custom-call | flops 2000000000 | bytes 4000000 | tf_op jit(solution)/shard_map/attend/pallas_call | solution.py:175
  64.6 1.3 %collective-permute-start.23 = (bf16[128,128]{1,0:T(8,128)(2,1)S(1)}, bf16[128,128]{1,0:T(8,128)(2,1)S(1)}, u32[]{:S(2)}, u32[]{:S(2)}) collective-permute-start(bf16[128,128]{1,0:T(8,128)(2,1)S(1)} %get-tuple-element.60), channel_id=1, source_target_pairs={{0,8},{1,9},{2,10},{3,11},{4,12},{5,13},{6,14},{7,15},{8,0},{9,1},... | collective-permute-start | bytes 98312 | tf_op jit(solution)/shard_map/ppermute | solution.py:252
  66.1 3.3 %collective-permute-start.22 = (bf16[128,128]{1,0:T(8,128)(2,1)S(1)}, bf16[128,128]{1,0:T(8,128)(2,1)S(1)}, u32[]{:S(2)}, u32[]{:S(2)}) collective-permute-start(bf16[128,128]{1,0:T(8,128)(2,1)S(1)} %get-tuple-element.61), channel_id=1, source_target_pairs={{0,3},{1,2},{2,1},{3,0},{4,7},{5,6},{6,5},{7,4},{8,11},{9,10},{10,... | collective-permute-start | bytes 98312 | tf_op jit(solution)/shard_map/ppermute | solution.py:252
  69.4 1.2 %collective-permute-start.25 = (bf16[128,128]{1,0:T(8,128)(2,1)S(1)}, bf16[128,128]{1,0:T(8,128)(2,1)S(1)}, u32[]{:S(2)}, u32[]{:S(2)}) collective-permute-start(bf16[128,128]{1,0:T(8,128)(2,1)S(1)} %get-tuple-element.58), channel_id=1, source_target_pairs={{0,10},{1,11},{2,8},{3,9},{4,14},{5,15},{6,12},{7,13},{8,2},{9,3},... | collective-permute-start | bytes 98312 | tf_op jit(solution)/shard_map/ppermute | solution.py:252
  70.6 3.2 %collective-permute-start.26 = (bf16[128,128]{1,0:T(8,128)(2,1)S(1)}, bf16[128,128]{1,0:T(8,128)(2,1)S(1)}, u32[]{:S(2)}, u32[]{:S(2)}) collective-permute-start(bf16[128,128]{1,0:T(8,128)(2,1)S(1)} %get-tuple-element.57), channel_id=1, source_target_pairs={{0,11},{1,10},{2,9},{3,8},{4,15},{5,14},{6,13},{7,12},{8,3},{9,2},... | collective-permute-start | bytes 98312 | tf_op jit(solution)/shard_map/ppermute | solution.py:252
  74.0 2.1 %collective-permute-done.26 = bf16[128,128]{1,0:T(8,128)(2,1)S(1)} collective-permute-done((bf16[128,128]{1,0:T(8,128)(2,1)S(1)}, bf16[128,128]{1,0:T(8,128)(2,1)S(1)}, u32[]{:S(2)}, u32[]{:S(2)}) %collective-permute-start.26) | collective-permute-done | bytes 32800 | tf_op jit(solution)/shard_map/ppermute | solution.py:252
  76.9 2.7 %finish.1 = bf16[256,512]{1,0:T(8,128)(2,1)} custom-call(s32[1]{0:T(128)} %bitcast.me_ref, bf16[256,512]{1,0:T(8,128)(2,1)} %tokens_ref.5, bf16[8,128,128]{2,1,0:T(8,128)(2,1)} %copy-done, bf16[256,512]{1,0:T(8,128)(2,1)} %get-tuple-element.54.gating_ref, bf16[512,512]{1,0:T(8,128)(2,1)} %weights_ref.1), custom_call_target="tpu_custom_call" | custom-call | tf_op jit(solution)/shard_map/finish/pallas_call | solution.py:324
  (76 shorter events, 6.6 us)
Async XLA Ops:
  3.1 10.7 %collective-permute-start = (bf16[256,128]{1,0:T(8,128)(2,1)}, bf16[256,128]{1,0:T(8,128)(2,1)S(1)}, u32[]{:S(2)}, u32[]{:S(2)}) collective-permute-start(bf16[256,128]{1,0:T(8,128)(2,1)} %get-tuple-element.38), channel_id=1, source_target_pairs={{0,11},{1,10},{2,9},{3,8},{4,15},{5,14},{6,13},{7,12},{8,3},{9,2},... | collective-permute-start | bytes 196616 | tf_op jit(solution)/shard_map/ppermute | solution.py:252
  7.3 9.6 %collective-permute-start.8 = (bf16[256,128]{1,0:T(8,128)(2,1)}, bf16[256,128]{1,0:T(8,128)(2,1)S(1)}, u32[]{:S(2)}, u32[]{:S(2)}) collective-permute-start(bf16[256,128]{1,0:T(8,128)(2,1)} %get-tuple-element.47), channel_id=1, source_target_pairs={{0,8},{1,9},{2,10},{3,11},{4,12},{5,13},{6,14},{7,15},{8,0},{9,1},... | collective-permute-start | bytes 196616 | tf_op jit(solution)/shard_map/ppermute | solution.py:252
  7.6 9.5 %collective-permute-start.9 = (bf16[256,128]{1,0:T(8,128)(2,1)}, bf16[256,128]{1,0:T(8,128)(2,1)S(1)}, u32[]{:S(2)}, u32[]{:S(2)}) collective-permute-start(bf16[256,128]{1,0:T(8,128)(2,1)} %get-tuple-element.48), channel_id=1, source_target_pairs={{0,9},{1,8},{2,11},{3,10},{4,13},{5,12},{6,15},{7,14},{8,1},{9,0},... | collective-permute-start | bytes 196616 | tf_op jit(solution)/shard_map/ppermute | solution.py:252
  7.8 9.5 %collective-permute-start.10 = (bf16[256,128]{1,0:T(8,128)(2,1)}, bf16[256,128]{1,0:T(8,128)(2,1)S(1)}, u32[]{:S(2)}, u32[]{:S(2)}) collective-permute-start(bf16[256,128]{1,0:T(8,128)(2,1)} %get-tuple-element.49), channel_id=1, source_target_pairs={{0,10},{1,11},{2,8},{3,9},{4,14},{5,15},{6,12},{7,13},{8,2},{9,3},... | collective-permute-start | bytes 196616 | tf_op jit(solution)/shard_map/ppermute | solution.py:252
  8.8 11.7 %collective-permute-start.4 = (bf16[256,128]{1,0:T(8,128)(2,1)}, bf16[256,128]{1,0:T(8,128)(2,1)S(1)}, u32[]{:S(2)}, u32[]{:S(2)}) collective-permute-start(bf16[256,128]{1,0:T(8,128)(2,1)} %get-tuple-element.44), channel_id=1, source_target_pairs={{0,1},{1,0},{2,3},{3,2},{4,5},{5,4},{6,7},{7,6},{8,9},{9,8},{10,11... | collective-permute-start | bytes 196616 | tf_op jit(solution)/shard_map/ppermute | solution.py:252
  13.8 8.1 %collective-permute-start.5 = (bf16[256,128]{1,0:T(8,128)(2,1)S(1)}, bf16[256,128]{1,0:T(8,128)(2,1)S(1)}, u32[]{:S(2)}, u32[]{:S(2)}) collective-permute-start(bf16[256,128]{1,0:T(8,128)(2,1)S(1)} %copy-done.3), channel_id=1, source_target_pairs={{0,2},{1,3},{2,0},{3,1},{4,6},{5,7},{6,4},{7,5},{8,10},{9,11},{10,... | collective-permute-start | bytes 196616 | tf_op jit(solution)/shard_map/ppermute | solution.py:252
  16.9 5.1 %collective-permute-start.6 = (bf16[256,128]{1,0:T(8,128)(2,1)S(1)}, bf16[256,128]{1,0:T(8,128)(2,1)S(1)}, u32[]{:S(2)}, u32[]{:S(2)}) collective-permute-start(bf16[256,128]{1,0:T(8,128)(2,1)S(1)} %copy-done.2), channel_id=1, source_target_pairs={{0,3},{1,2},{2,1},{3,0},{4,7},{5,6},{6,5},{7,4},{8,11},{9,10},{10,... | collective-permute-start | bytes 196616 | tf_op jit(solution)/shard_map/ppermute | solution.py:252
  17.0 6.1 %collective-permute-start.1 = (bf16[128,128]{1,0:T(8,128)(2,1)}, bf16[128,128]{1,0:T(8,128)(2,1)S(1)}, u32[]{:S(2)}, u32[]{:S(2)}) collective-permute-start(bf16[128,128]{1,0:T(8,128)(2,1)} %get-tuple-element.40), channel_id=1, source_target_pairs={{0,1},{1,0},{2,3},{3,2},{4,5},{5,4},{6,7},{7,6},{8,9},{9,8},{10,11... | collective-permute-start | bytes 98312 | tf_op jit(solution)/shard_map/ppermute | solution.py:252
  17.3 9.1 %collective-permute-start.2 = (bf16[128,128]{1,0:T(8,128)(2,1)}, bf16[128,128]{1,0:T(8,128)(2,1)S(1)}, u32[]{:S(2)}, u32[]{:S(2)}) collective-permute-start(bf16[128,128]{1,0:T(8,128)(2,1)} %get-tuple-element.41), channel_id=1, source_target_pairs={{0,2},{1,3},{2,0},{3,1},{4,6},{5,7},{6,4},{7,5},{8,10},{9,11},{10,... | collective-permute-start | bytes 98312 | tf_op jit(solution)/shard_map/ppermute | solution.py:252
  20.5 10.2 %collective-permute-start.14 = (bf16[128,128]{1,0:T(8,128)(2,1)}, bf16[128,128]{1,0:T(8,128)(2,1)S(1)}, u32[]{:S(2)}, u32[]{:S(2)}) collective-permute-start(bf16[128,128]{1,0:T(8,128)(2,1)} %get-tuple-element.50), channel_id=1, source_target_pairs={{0,8},{1,9},{2,10},{3,11},{4,12},{5,13},{6,14},{7,15},{8,0},{9,1},... | collective-permute-start | bytes 98312 | tf_op jit(solution)/shard_map/ppermute | solution.py:252
  21.8 9.2 %collective-permute-start.15 = (bf16[128,128]{1,0:T(8,128)(2,1)}, bf16[128,128]{1,0:T(8,128)(2,1)S(1)}, u32[]{:S(2)}, u32[]{:S(2)}) collective-permute-start(bf16[128,128]{1,0:T(8,128)(2,1)} %get-tuple-element.51), channel_id=1, source_target_pairs={{0,9},{1,8},{2,11},{3,10},{4,13},{5,12},{6,15},{7,14},{8,1},{9,0},... | collective-permute-start | bytes 98312 | tf_op jit(solution)/shard_map/ppermute | solution.py:252
  21.9 9.4 %collective-permute-start.16 = (bf16[128,128]{1,0:T(8,128)(2,1)}, bf16[128,128]{1,0:T(8,128)(2,1)S(1)}, u32[]{:S(2)}, u32[]{:S(2)}) collective-permute-start(bf16[128,128]{1,0:T(8,128)(2,1)} %get-tuple-element.52), channel_id=1, source_target_pairs={{0,10},{1,11},{2,8},{3,9},{4,14},{5,15},{6,12},{7,13},{8,2},{9,3},... | collective-permute-start | bytes 98312 | tf_op jit(solution)/shard_map/ppermute | solution.py:252
  23.2 9.5 %collective-permute-start.17 = (bf16[128,128]{1,0:T(8,128)(2,1)}, bf16[128,128]{1,0:T(8,128)(2,1)S(1)}, u32[]{:S(2)}, u32[]{:S(2)}) collective-permute-start(bf16[128,128]{1,0:T(8,128)(2,1)} %get-tuple-element.53), channel_id=1, source_target_pairs={{0,11},{1,10},{2,9},{3,8},{4,15},{5,14},{6,13},{7,12},{8,3},{9,2},... | collective-permute-start | bytes 98312 | tf_op jit(solution)/shard_map/ppermute | solution.py:252
  26.4 18.8 %collective-permute-start.19 = (bf16[4,256,128]{2,1,0:T(8,128)(2,1)S(1)}, bf16[4,256,128]{2,1,0:T(8,128)(2,1)S(1)}, u32[]{:S(2)}, u32[]{:S(2)}) collective-permute-start(bf16[4,256,128]{2,1,0:T(8,128)(2,1)S(1)} %pad_maximum_fusion.1.refs_1_), channel_id=1, source_target_pairs={{0,4},{4,0},{8,12},{12,8},{16,20},{20,16},{24,28},{28,24},{1,5},{5... | collective-permute-start | bytes 786440 | tf_op jit(solution)/shard_map/ppermute | solution.py:255
  30.8 8.0 %collective-permute-start.11 = (bf16[4,256,128]{2,1,0:T(8,128)(2,1)S(1)}, bf16[4,256,128]{2,1,0:T(8,128)(2,1)S(1)}, u32[]{:S(2)}, u32[]{:S(2)}) collective-permute-start(bf16[4,256,128]{2,1,0:T(8,128)(2,1)S(1)} %pad_maximum_fusion.1.refs_1_), channel_id=1, source_target_pairs={{0,16},{4,20},{8,24},{12,28},{16,0},{20,4},{24,8},{28,12},{1,17},{... | collective-permute-start | bytes 786440 | tf_op jit(solution)/shard_map/ppermute | solution.py:255
  31.1 14.1 %collective-permute-start.18 = (bf16[4,256,128]{2,1,0:T(8,128)(2,1)S(1)}, bf16[4,256,128]{2,1,0:T(8,128)(2,1)S(1)}, u32[]{:S(2)}, u32[]{:S(2)}) collective-permute-start(bf16[4,256,128]{2,1,0:T(8,128)(2,1)S(1)} %pad_maximum_fusion.refs_0_), channel_id=1, source_target_pairs={{0,4},{4,0},{8,12},{12,8},{16,20},{20,16},{24,28},{28,24},{1,5},{5... | collective-permute-start | bytes 786440 | tf_op jit(solution)/shard_map/ppermute | solution.py:255
  31.4 13.0 %collective-permute-start.7 = (bf16[4,256,128]{2,1,0:T(8,128)(2,1)S(1)}, bf16[4,256,128]{2,1,0:T(8,128)(2,1)S(1)}, u32[]{:S(2)}, u32[]{:S(2)}) collective-permute-start(bf16[4,256,128]{2,1,0:T(8,128)(2,1)S(1)} %pad_maximum_fusion.refs_0_), channel_id=1, source_target_pairs={{0,16},{4,20},{8,24},{12,28},{16,0},{20,4},{24,8},{28,12},{1,17},{... | collective-permute-start | bytes 786440 | tf_op jit(solution)/shard_map/ppermute | solution.py:255
  32.6 4.8 %collective-permute-start.3 = (bf16[128,128]{1,0:T(8,128)(2,1)}, bf16[128,128]{1,0:T(8,128)(2,1)S(1)}, u32[]{:S(2)}, u32[]{:S(2)}) collective-permute-start(bf16[128,128]{1,0:T(8,128)(2,1)} %get-tuple-element.42), channel_id=1, source_target_pairs={{0,3},{1,2},{2,1},{3,0},{4,7},{5,6},{6,5},{7,4},{8,11},{9,10},{10,... | collective-permute-start | bytes 98312 | tf_op jit(solution)/shard_map/ppermute | solution.py:252
  38.8 14.0 %collective-permute-start.13 = (bf16[4,256,128]{2,1,0:T(8,128)(2,1)S(1)}, bf16[4,256,128]{2,1,0:T(8,128)(2,1)S(1)}, u32[]{:S(2)}, u32[]{:S(2)}) collective-permute-start(bf16[4,256,128]{2,1,0:T(8,128)(2,1)S(1)} %collective-permute-done.11.refs_1_), channel_id=1, source_target_pairs={{0,4},{4,0},{8,12},{12,8},{16,20},{20,16},{24,28},{28,24},{1,5},{5... | collective-permute-start | bytes 786440 | tf_op jit(solution)/shard_map/ppermute | solution.py:255
  44.4 8.4 %collective-permute-start.12 = (bf16[4,256,128]{2,1,0:T(8,128)(2,1)S(1)}, bf16[4,256,128]{2,1,0:T(8,128)(2,1)S(1)}, u32[]{:S(2)}, u32[]{:S(2)}) collective-permute-start(bf16[4,256,128]{2,1,0:T(8,128)(2,1)S(1)} %collective-permute-done.7.refs_0_), channel_id=1, source_target_pairs={{0,4},{4,0},{8,12},{12,8},{16,20},{20,16},{24,28},{28,24},{1,5},{5... | collective-permute-start | bytes 786440 | tf_op jit(solution)/shard_map/ppermute | solution.py:255
  63.5 5.9 %collective-permute-start.20 = (bf16[128,128]{1,0:T(8,128)(2,1)S(1)}, bf16[128,128]{1,0:T(8,128)(2,1)S(1)}, u32[]{:S(2)}, u32[]{:S(2)}) collective-permute-start(bf16[128,128]{1,0:T(8,128)(2,1)S(1)} %get-tuple-element.63), channel_id=1, source_target_pairs={{0,1},{1,0},{2,3},{3,2},{4,5},{5,4},{6,7},{7,6},{8,9},{9,8},{10,11... | collective-permute-start | bytes 98312 | tf_op jit(solution)/shard_map/ppermute | solution.py:252
  64.6 9.3 %collective-permute-start.23 = (bf16[128,128]{1,0:T(8,128)(2,1)S(1)}, bf16[128,128]{1,0:T(8,128)(2,1)S(1)}, u32[]{:S(2)}, u32[]{:S(2)}) collective-permute-start(bf16[128,128]{1,0:T(8,128)(2,1)S(1)} %get-tuple-element.60), channel_id=1, source_target_pairs={{0,8},{1,9},{2,10},{3,11},{4,12},{5,13},{6,14},{7,15},{8,0},{9,1},... | collective-permute-start | bytes 98312 | tf_op jit(solution)/shard_map/ppermute | solution.py:252
  66.1 7.8 %collective-permute-start.22 = (bf16[128,128]{1,0:T(8,128)(2,1)S(1)}, bf16[128,128]{1,0:T(8,128)(2,1)S(1)}, u32[]{:S(2)}, u32[]{:S(2)}) collective-permute-start(bf16[128,128]{1,0:T(8,128)(2,1)S(1)} %get-tuple-element.61), channel_id=1, source_target_pairs={{0,3},{1,2},{2,1},{3,0},{4,7},{5,6},{6,5},{7,4},{8,11},{9,10},{10,... | collective-permute-start | bytes 98312 | tf_op jit(solution)/shard_map/ppermute | solution.py:252
  70.6 5.5 %collective-permute-start.26 = (bf16[128,128]{1,0:T(8,128)(2,1)S(1)}, bf16[128,128]{1,0:T(8,128)(2,1)S(1)}, u32[]{:S(2)}, u32[]{:S(2)}) collective-permute-start(bf16[128,128]{1,0:T(8,128)(2,1)S(1)} %get-tuple-element.57), channel_id=1, source_target_pairs={{0,11},{1,10},{2,9},{3,8},{4,15},{5,14},{6,13},{7,12},{8,3},{9,2},... | collective-permute-start | bytes 98312 | tf_op jit(solution)/shard_map/ppermute | solution.py:252
  (8 other events, 46.1 us)
where the time goes:
time: 79.2 us; the launch traced here: 79.5 us
  starting transfers between devices  37.1 us (47%)
  Pallas kernels  27.9 us (35%)
  waiting for transfers between devices  11.1 us (14%)
  local copies, waits for them, and re-layouts  1.71 us (2%)
  other arithmetic  1.49 us (2%)
    ppermute x21, starting transfers between devices, partner(): return lax.ppermute(array, ('seq', 'head'), pairs)  28.1 us
    pallas_call x3, Pallas kernels, attend_call(): pl.pallas_call(functools.partial(attend, before is None, closes), grid_sp...  19.1 us
    ppermute x6, starting transfers between devices, seq_flip(): return lax.ppermute(array, 'seq', [(s, s ^ bit) for s in range(seq_size)])  9.06 us
    ppermute x21, waiting for transfers between devices, partner(): return lax.ppermute(array, ('seq', 'head'), pairs)  6.95 us
    ppermute x6, waiting for transfers between devices, seq_flip(): return lax.ppermute(array, 'seq', [(s, s ^ bit) for s in range(seq_size)])  4.11 us
    pallas_call x1, Pallas kernels, per_device(): pl.pallas_call(project_keys, out_shape=[jax.ShapeDtypeStruct((rows, LANES...  3.08 us
    pallas_call x1, Pallas kernels, per_device(): pl.pallas_call(project_queries, out_shape=[jax.ShapeDtypeStruct((half, LA...  3.05 us
    pallas_call x1, Pallas kernels, per_device(): pl.pallas_call(finish, out_shape=jax.ShapeDtypeStruct((rows, width), bf16...  2.67 us
  transfers between devices with their start and end apart: 27, of which 5 were waited for; matrix products, arithmetic and copies ran while one was open for 3% of the time, Pallas kernels for 14%

commit v1 on v0

--- a/solution.py
+++ b/solution.py
@@ -38,39 +38,31 @@
     return lax.broadcasted_iota(jnp.int32, (rows, LANES), 1) < DH
 
 
-def project_keys(me_ref, tokens_ref, value_weights, key_weights, *refs):
+def project(me_ref, tokens_ref, values_ref, queries_ref, keys_ref, *refs):
     outs, held = refs[:-1], refs[-1]
-    rows = tokens_ref.shape[0]
-    normed = layer_norm(tokens_ref[...].astype(f32)).astype(bf16)
-    low = low_lanes(rows)
-    for pair in range(H // 2):
-        at = slice(pair * LANES, (pair + 1) * LANES)
-        values = silu(jnp.dot(normed, value_weights[:, at], preferred_element_type=f32))
-        keys = silu(jnp.dot(normed, key_weights[:, at], preferred_element_type=f32))
-        held[2 * pair] = jnp.where(low, keys, swap_halves(values)).astype(bf16)
-        held[2 * pair + 1] = jnp.where(low, swap_halves(keys), values).astype(bf16)
-    for k, out in enumerate(outs):
-        out[...] = held[jnp.bitwise_xor(me_ref[0], k)]
-
-
-def project_queries(me_ref, tokens_ref, query_weights, gating_weights, *refs):
-    outs, gating, held = refs[:-2], refs[-2], refs[-1]
     rows = tokens_ref.shape[0]
     half = rows // 2
     normed = layer_norm(tokens_ref[...].astype(f32)).astype(bf16)
-    low = low_lanes(half)
+    low, half_low = low_lanes(rows), low_lanes(half)
     scale = 0.5 * DH ** (-0.5)
+    keys = silu(jnp.dot(normed, keys_ref[...], preferred_element_type=f32))
+    values = silu(jnp.dot(normed, values_ref[...], preferred_element_type=f32))
+    queries = silu(jnp.dot(normed, queries_ref[...], preferred_element_type=f32)) * scale
     for pair in range(H // 2):
         at = slice(pair * LANES, (pair + 1) * LANES)
-        queries = silu(jnp.dot(normed, query_weights[:, at], preferred_element_type=f32)) * scale
-        upper, lower = queries[:half], queries[half:]
-        held[2 * pair] = jnp.where(low, upper, swap_halves(lower)).astype(bf16)
-        held[2 * pair + 1] = jnp.where(low, swap_halves(upper), lower).astype(bf16)
-        gating[:, at] = silu(
-            jnp.dot(normed, gating_weights[:, at], preferred_element_type=f32)
-        ).astype(bf16)
+        key, value, upper, lower = keys[:, at], values[:, at], queries[:half, at], queries[half:, at]
+        held[2 * pair, :rows] = jnp.where(low, key, swap_halves(value)).astype(bf16)
+        held[2 * pair + 1, :rows] = jnp.where(low, swap_halves(key), value).astype(bf16)
+        held[2 * pair, rows:] = jnp.where(half_low, upper, swap_halves(lower)).astype(bf16)
+        held[2 * pair + 1, rows:] = jnp.where(half_low, swap_halves(upper), lower).astype(bf16)
     for k, out in enumerate(outs):
         out[...] = held[jnp.bitwise_xor(me_ref[0], k)]
+
+
+def project_gating(tokens_ref, gating_weights, out_ref):
+    normed = layer_norm(tokens_ref[...].astype(f32)).astype(bf16)
+    gating = silu(jnp.dot(normed, gating_weights[...], preferred_element_type=f32))
+    out_ref[...] = gating.astype(bf16)
 
 
 def attend(
@@ -116,11 +108,11 @@
 
     def add(key_block, count, masked):
         key_rows = [held[slot_ref[key_block + i]] for i in range(count)]
-        key_rows = key_rows[0] if count == 1 else jnp.concatenate(key_rows, axis=0)
+        key_rows = jnp.concatenate(key_rows, axis=0)
         if masked:
             column = lax.broadcasted_iota(jnp.int32, (TILE, count * rows), 1)
             ahead = column - lax.broadcasted_iota(jnp.int32, (TILE, count * rows), 0)
-        for i in range(TEAM):
+        def add_to(i):
             at = slice(i * rows, (i + 1) * rows)
             score = lax.dot_general(
                 queries[at], key_rows, (((1,), (1,)), ((), ())), preferred_element_type=f32
@@ -136,20 +128,26 @@
                 weights = jnp.concatenate(pieces, axis=0)
             total[at] += jnp.dot(weights.astype(bf16), key_rows, preferred_element_type=f32)
 
-    def loop(begin, end, count, masked):
+        for i in range(TEAM):
+            if masked:
+                needed = starts[i * tiles] < (key_block + count) * tiles
+                pl.when(needed)(functools.partial(add_to, i))
+            else:
+                add_to(i)
+
+    def loop(begin, end, masked):
         def body(index, carry):
-            add(begin + index * count, count, masked)
+            add(index * TEAM, TEAM, masked)
             return carry
 
-        lax.fori_loop(0, jnp.maximum(end - begin, 0) // count, body, 0)
+        lax.fori_loop(begin // TEAM, end // TEAM, body, 0)
 
     reach_low, reach_high = reach_ref[0], jnp.minimum(reach_ref[1], least)
-    first = jnp.maximum(low_start // tiles, reach_low)
-    whole = jnp.maximum(first, jnp.minimum((high_start + tiles - 1) // tiles, reach_high))
-    even = jnp.maximum(whole, jnp.minimum((whole + TEAM - 1) // TEAM * TEAM, reach_high))
-    loop(first, whole, 1, True)
-    loop(whole, even, 1, False)
-    loop(even, reach_high, TEAM, False)
+    first = jnp.maximum(low_start // (tiles * TEAM) * TEAM, reach_low)
+    whole = (high_start + tiles * TEAM - 1) // (tiles * TEAM) * TEAM
+    whole = jnp.maximum(first, jnp.minimum(whole, reach_high))
+    loop(first, jnp.minimum(whole, reach_high), True)
+    loop(whole, reach_high, False)
 
     @pl.when(least < reach_ref[1])
     def _():
@@ -254,26 +252,23 @@
     def seq_flip(array, bit):
         return lax.ppermute(array, "seq", [(s, s ^ bit) for s in range(seq_size)])
 
-    keys_sent = pl.pallas_call(
-        project_keys,
-        out_shape=[jax.ShapeDtypeStruct((rows, LANES), bf16)] * H,
+    sent = pl.pallas_call(
+        project,
+        out_shape=[jax.ShapeDtypeStruct((rows + half, LANES), bf16)] * H,
         grid=(1,),
-        in_specs=[SMEM, VMEM, columns_of(width, 1), columns_of(width, 3)],
+        in_specs=[SMEM, VMEM] + [columns_of(width, i) for i in (1, 2, 3)],
         out_specs=[VMEM] * H,
-        scratch_shapes=[pltpu.VMEM((H, rows, LANES), bf16)],
-        name="project_keys",
-    )(me_array, tokens, w_proj, w_proj)
-    queries_sent = pl.pallas_call(
-        project_queries,
-        out_shape=[jax.ShapeDtypeStruct((half, LANES), bf16)] * H
-        + [jax.ShapeDtypeStruct((rows, H * DH), bf16)],
+        scratch_shapes=[pltpu.VMEM((H, rows + half, LANES), bf16)],
+        name="project",
+    )(me_array, tokens, w_proj, w_proj, w_proj)
+    gating = pl.pallas_call(
+        project_gating,
+        out_shape=jax.ShapeDtypeStruct((rows, H * DH), bf16),
         grid=(1,),
-        in_specs=[SMEM, VMEM, columns_of(width, 2), columns_of(width, 0)],
-        out_specs=[VMEM] * (H + 1),
-        scratch_shapes=[pltpu.VMEM((H, half, LANES), bf16)],
-        name="project_queries",
-    )(me_array, tokens, w_proj, w_proj)
-    gating = queries_sent[-1]
+        in_specs=[VMEM, columns_of(width, 0)],
+        out_specs=VMEM,
+        name="project_gating",
+    )(tokens, w_proj)
 
     index = jnp.arange(blocks, dtype=jnp.int32)
     block_head, block_seq = index % head_size, index // head_size
@@ -291,10 +286,9 @@
     def reach(first, last, query):
         return jnp.stack([jnp.asarray(v, jnp.int32) for v in (first, last, query)])
 
-    arrived = [partner(keys_sent[k], k) for k in range(H)]
-    last = arrived[-1]
-    to_send, _ = lax.optimization_barrier((tuple(queries_sent[:H]), last))
-    queries = jnp.stack([partner(to_send[k], k) for k in range(H)])
+    arrived = [partner(sent[k], k) for k in range(H)]
+    queries = jnp.stack([array[rows:] for array in arrived])
+    arrived = [array[:rows] for array in arrived]
     if groups == 2 and share == 2:
         lots = [jnp.stack(arrived[:TEAM]), jnp.stack(arrived[TEAM:])]
         far = [seq_flip(lot, fold * share) for lot in lots]

time: 79.2 us -> 83.8 us (1.058)
  the two profiles are of different devices: /device:TPU:5 before, /device:TPU:4 now
where the time goes in v1:
time: 83.8 us; the launch traced here: 83.5 us
  starting transfers between devices  30.2 us (36%)
  Pallas kernels  25.7 us (31%)
  waiting for transfers between devices  23.2 us (28%)
  local copies, waits for them, and re-layouts  3.39 us (4%)
    ppermute x14, starting transfers between devices, partner(): return lax.ppermute(array, ('seq', 'head'), pairs)  27.8 us
    pallas_call x3, Pallas kernels, attend_call(): pl.pallas_call(functools.partial(attend, before is None, closes), grid_sp...  17.4 us
    ppermute x6, waiting for transfers between devices, seq_flip(): return lax.ppermute(array, 'seq', [(s, s ^ bit) for s in range(seq_size)])  11.7 us
    ppermute x14, waiting for transfers between devices, partner(): return lax.ppermute(array, ('seq', 'head'), pairs)  11.5 us
    pallas_call x1, Pallas kernels, per_device(): pl.pallas_call(project, out_shape=[jax.ShapeDtypeStruct((rows + half, LAN...  3.34 us
    pallas_call x1, Pallas kernels, per_device(): pl.pallas_call(finish, out_shape=jax.ShapeDtypeStruct((rows, width), bf16...  2.67 us
    ppermute x6, starting transfers between devices, seq_flip(): return lax.ppermute(array, 'seq', [(s, s ^ bit) for s in range(seq_size)])  2.4 us
    pallas_call x1, Pallas kernels, per_device(): pl.pallas_call(project_gating, out_shape=jax.ShapeDtypeStruct((rows, H *...  2.32 us
  transfers between devices with their start and end apart: 20, of which 6 were waited for; matrix products, arithmetic and copies ran while one was open for 4% of the time, Pallas kernels for 17%

profile of v1, /device:TPU:4, one launch (start us, length us, event | category | flops | bytes accessed | tf_op | source)
XLA Modules:
  0.0 83.5 jit_solution(16169655534596219716)
XLA Ops:
  0.0 3.3 %project.1 = (bf16[384,128]{1,0:T(8,128)(2,1)}, bf16[384,128]{1,0:T(8,128)(2,1)}, bf16[384,128]{1,0:T(8,128)(2,1)}, bf16[384,128]{1,0:T(8,128)(2,1)}, bf16[384,1...) custom-call(s32[1]{0:T(128)} %bitcast.me_ref, ...), custom_call_target="tpu_custom_call" | custom-call | tf_op jit(solution)/shard_map/project/pallas_call | solution.py:255
  3.3 1.6 %collective-permute-start = (bf16[384,128]{1,0:T(8,128)(2,1)}, bf16[384,128]{1,0:T(8,128)(2,1)S(1)}, u32[]{:S(2)}, u32[]{:S(2)}) collective-permute-start(bf16[384,128]{1,0:T(8,128)(2,1)} %get-tuple-element.14), channel_id=1, source_target_pairs={{0,1},{1,0},{2,3},{3,2},{4,5},{5,4},{6,7},{7,6},{8,9},{9,8},{10,11... | collective-permute-start | bytes 294920 | tf_op jit(solution)/shard_map/ppermute | solution.py:250
  5.0 2.6 %collective-permute-start.1 = (bf16[384,128]{1,0:T(8,128)(2,1)}, bf16[384,128]{1,0:T(8,128)(2,1)S(1)}, u32[]{:S(2)}, u32[]{:S(2)}) collective-permute-start(bf16[384,128]{1,0:T(8,128)(2,1)} %get-tuple-element.15), channel_id=1, source_target_pairs={{0,2},{1,3},{2,0},{3,1},{4,6},{5,7},{6,4},{7,5},{8,10},{9,11},{10,... | collective-permute-start | bytes 294920 | tf_op jit(solution)/shard_map/ppermute | solution.py:250
  7.8 1.5 %collective-permute-start.4 = (bf16[384,128]{1,0:T(8,128)(2,1)}, bf16[384,128]{1,0:T(8,128)(2,1)S(1)}, u32[]{:S(2)}, u32[]{:S(2)}) collective-permute-start(bf16[384,128]{1,0:T(8,128)(2,1)} %get-tuple-element.17), channel_id=1, source_target_pairs={{0,8},{1,9},{2,10},{3,11},{4,12},{5,13},{6,14},{7,15},{8,0},{9,1},... | collective-permute-start | bytes 294920 | tf_op jit(solution)/shard_map/ppermute | solution.py:250
  9.3 3.6 %collective-permute-start.7 = (bf16[384,128]{1,0:T(8,128)(2,1)}, bf16[384,128]{1,0:T(8,128)(2,1)S(1)}, u32[]{:S(2)}, u32[]{:S(2)}) collective-permute-start(bf16[384,128]{1,0:T(8,128)(2,1)} %get-tuple-element.20), channel_id=1, source_target_pairs={{0,11},{1,10},{2,9},{3,8},{4,15},{5,14},{6,13},{7,12},{8,3},{9,2},... | collective-permute-start | bytes 294920 | tf_op jit(solution)/shard_map/ppermute | solution.py:250
  15.6 2.3 %project_gating.1.gating_ref = bf16[256,512]{1,0:T(8,128)(2,1)} custom-call(bf16[256,512]{1,0:T(8,128)(2,1)} %tokens_ref.5, bf16[512,2048]{1,0:T(8,128)(2,1)} %gating_weights.1), custom_call_target="tpu_custom_call" | custom-call | tf_op jit(solution)/shard_map/project_gating/pallas_call | solution.py:264
  18.2 5.1 %collective-permute-start.6 = (bf16[384,128]{1,0:T(8,128)(2,1)S(1)}, bf16[384,128]{1,0:T(8,128)(2,1)S(1)}, u32[]{:S(2)}, u32[]{:S(2)}) collective-permute-start(bf16[384,128]{1,0:T(8,128)(2,1)S(1)} %copy-done.2), channel_id=1, source_target_pairs={{0,10},{1,11},{2,8},{3,9},{4,14},{5,15},{6,12},{7,13},{8,2},{9,3},... | collective-permute-start | bytes 294920 | tf_op jit(solution)/shard_map/ppermute | solution.py:250
  23.4 3.6 %collective-permute-done.6 = bf16[384,128]{1,0:T(8,128)(2,1)S(1)} collective-permute-done((bf16[384,128]{1,0:T(8,128)(2,1)S(1)}, bf16[384,128]{1,0:T(8,128)(2,1)S(1)}, u32[]{:S(2)}, u32[]{:S(2)}) %collective-permute-start.6) | collective-permute-done | bytes 98336 | tf_op jit(solution)/shard_map/ppermute | solution.py:250
  27.0 1.8 %collective-permute-start.5 = (bf16[384,128]{1,0:T(8,128)(2,1)S(1)}, bf16[384,128]{1,0:T(8,128)(2,1)S(1)}, u32[]{:S(2)}, u32[]{:S(2)}) collective-permute-start(bf16[384,128]{1,0:T(8,128)(2,1)S(1)} %copy-done.1), channel_id=1, source_target_pairs={{0,9},{1,8},{2,11},{3,10},{4,13},{5,12},{6,15},{7,14},{8,1},{9,0},... | collective-permute-start | bytes 294920 | tf_op jit(solution)/shard_map/ppermute | solution.py:250
  28.8 3.7 %collective-permute-done.5 = bf16[384,128]{1,0:T(8,128)(2,1)S(1)} collective-permute-done((bf16[384,128]{1,0:T(8,128)(2,1)S(1)}, bf16[384,128]{1,0:T(8,128)(2,1)S(1)}, u32[]{:S(2)}, u32[]{:S(2)}) %collective-permute-start.5) | collective-permute-done | bytes 98336 | tf_op jit(solution)/shard_map/ppermute | solution.py:250
  33.6 1.5 %collective-permute-start.3 = (bf16[4,256,128]{2,1,0:T(8,128)(2,1)S(1)}, bf16[4,256,128]{2,1,0:T(8,128)(2,1)S(1)}, u32[]{:S(2)}, u32[]{:S(2)}) collective-permute-start(bf16[4,256,128]{2,1,0:T(8,128)(2,1)S(1)} %pad_maximum_fusion.refs_0_), channel_id=1, source_target_pairs={{0,16},{4,20},{8,24},{12,28},{16,0},{20,4},{24,8},{28,12},{1,17},{... | collective-permute-start | bytes 786440 | tf_op jit(solution)/shard_map/ppermute | solution.py:253
  35.3 6.5 %collective-permute-done.8.refs_1_ = bf16[4,256,128]{2,1,0:T(8,128)(2,1)S(1)} collective-permute-done((bf16[4,256,128]{2,1,0:T(8,128)(2,1)S(1)}, bf16[4,256,128]{2,1,0:T(8,128)(2,1)S(1)}, u32[]{:S(2)}, u32[]{:S(2)}) %collective-permute-start.8) | collective-permute-done | bytes 262176 | tf_op jit(solution)/shard_map/ppermute | solution.py:253
  41.8 5.2 %collective-permute-done.3.refs_0_ = bf16[4,256,128]{2,1,0:T(8,128)(2,1)S(1)} collective-permute-done((bf16[4,256,128]{2,1,0:T(8,128)(2,1)S(1)}, bf16[4,256,128]{2,1,0:T(8,128)(2,1)S(1)}, u32[]{:S(2)}, u32[]{:S(2)}) %collective-permute-start.3) | collective-permute-done | bytes 262176 | tf_op jit(solution)/shard_map/ppermute | solution.py:253
  47.0 7.4 %attend.3 = f32[2048,128]{1,0:T(8,128)S(1)} custom-call(s32[3]{0:T(128)S(1)} %pad_add_fusion.reach_ref, s32[64]{0:T(128)S(1)} %convert_reduce_fusion.1.start_ref, f32[64]{0:T(128)S(1)} %multiply_divide_fusion.inverse_ref, s32[8]{0:T(128)S(1)} %fusion.1.block_ref, s32[32]{0:T(128)S(1)} %fusion.3.slot_ref, ...), custom_call_target="tpu_custom_call" | custom-call | flops 4000000000 | bytes 4000000 | tf_op jit(solution)/shard_map/attend/pallas_call | solution.py:173
  54.5 5.7 %attend.4 = bf16[4,128,128]{2,1,0:T(8,128)(2,1)S(1)} custom-call(s32[3]{0:T(128)S(1)} %pad_add_fusion.1.reach_ref, s32[64]{0:T(128)S(1)} %convert_reduce_fusion.1.start_ref, f32[64]{0:T(128)S(1)} %multiply_divide_fusion.inverse_ref, s32[8]{0:T(128)S(1)} %fusion.1.block_ref, s32[32]{0:T(128)S(1)} %fusion.3.slot_ref, ...), custom_call_target="tpu_custom_call" | custom-call | flops 2000000000 | bytes 4000000 | tf_op jit(solution)/shard_map/attend/pallas_call | solution.py:173
  60.3 1.9 %collective-permute-start.13 = (bf16[128,128]{1,0:T(8,128)(2,1)S(1)}, bf16[128,128]{1,0:T(8,128)(2,1)S(1)}, u32[]{:S(2)}, u32[]{:S(2)}) collective-permute-start(bf16[128,128]{1,0:T(8,128)(2,1)S(1)} %get-tuple-element.29), channel_id=1, source_target_pairs={{0,1},{1,0},{2,3},{3,2},{4,5},{5,4},{6,7},{7,6},{8,9},{9,8},{10,11... | collective-permute-start | bytes 98312 | tf_op jit(solution)/shard_map/ppermute | solution.py:250
  62.2 4.2 %attend.5 = bf16[4,128,128]{2,1,0:T(8,128)(2,1)S(1)} custom-call(s32[3]{0:T(128)S(1)} %pad_add_fusion.3.reach_ref, s32[64]{0:T(128)S(1)} %convert_reduce_fusion.1.start_ref, f32[64]{0:T(128)S(1)} %multiply_divide_fusion.inverse_ref, s32[8]{0:T(128)S(1)} %fusion.1.block_ref, s32[32]{0:T(128)S(1)} %fusion.3.slot_ref, ...), custom_call_target="tpu_custom_call" | custom-call | flops 2000000000 | bytes 4000000 | tf_op jit(solution)/shard_map/attend/pallas_call | solution.py:173
  68.1 1.5 %collective-permute-start.15 = (bf16[128,128]{1,0:T(8,128)(2,1)S(1)}, bf16[128,128]{1,0:T(8,128)(2,1)S(1)}, u32[]{:S(2)}, u32[]{:S(2)}) collective-permute-start(bf16[128,128]{1,0:T(8,128)(2,1)S(1)} %get-tuple-element.27), channel_id=1, source_target_pairs={{0,3},{1,2},{2,1},{3,0},{4,7},{5,6},{6,5},{7,4},{8,11},{9,10},{10,... | collective-permute-start | bytes 98312 | tf_op jit(solution)/shard_map/ppermute | solution.py:250
  69.6 1.8 %collective-permute-start.17 = (bf16[128,128]{1,0:T(8,128)(2,1)S(1)}, bf16[128,128]{1,0:T(8,128)(2,1)S(1)}, u32[]{:S(2)}, u32[]{:S(2)}) collective-permute-start(bf16[128,128]{1,0:T(8,128)(2,1)S(1)} %get-tuple-element.25), channel_id=1, source_target_pairs={{0,9},{1,8},{2,11},{3,10},{4,13},{5,12},{6,15},{7,14},{8,1},{9,0},... | collective-permute-start | bytes 98312 | tf_op jit(solution)/shard_map/ppermute | solution.py:250
  71.4 2.0 %collective-permute-start.18 = (bf16[128,128]{1,0:T(8,128)(2,1)S(1)}, bf16[128,128]{1,0:T(8,128)(2,1)S(1)}, u32[]{:S(2)}, u32[]{:S(2)}) collective-permute-start(bf16[128,128]{1,0:T(8,128)(2,1)S(1)} %get-tuple-element.24), channel_id=1, source_target_pairs={{0,10},{1,11},{2,8},{3,9},{4,14},{5,15},{6,12},{7,13},{8,2},{9,3},... | collective-permute-start | bytes 98312 | tf_op jit(solution)/shard_map/ppermute | solution.py:250
  73.4 2.5 %collective-permute-start.19 = (bf16[128,128]{1,0:T(8,128)(2,1)S(1)}, bf16[128,128]{1,0:T(8,128)(2,1)S(1)}, u32[]{:S(2)}, u32[]{:S(2)}) collective-permute-start(bf16[128,128]{1,0:T(8,128)(2,1)S(1)} %get-tuple-element.23), channel_id=1, source_target_pairs={{0,11},{1,10},{2,9},{3,8},{4,15},{5,14},{6,13},{7,12},{8,3},{9,2},... | collective-permute-start | bytes 98312 | tf_op jit(solution)/shard_map/ppermute | solution.py:250
  75.9 1.2 %collective-permute-done.18 = bf16[128,128]{1,0:T(8,128)(2,1)S(1)} collective-permute-done((bf16[128,128]{1,0:T(8,128)(2,1)S(1)}, bf16[128,128]{1,0:T(8,128)(2,1)S(1)}, u32[]{:S(2)}, u32[]{:S(2)}) %collective-permute-start.18) | collective-permute-done | bytes 32800 | tf_op jit(solution)/shard_map/ppermute | solution.py:250
  77.2 2.9 %collective-permute-done.19 = bf16[128,128]{1,0:T(8,128)(2,1)S(1)} collective-permute-done((bf16[128,128]{1,0:T(8,128)(2,1)S(1)}, bf16[128,128]{1,0:T(8,128)(2,1)S(1)}, u32[]{:S(2)}, u32[]{:S(2)}) %collective-permute-start.19) | collective-permute-done | bytes 32800 | tf_op jit(solution)/shard_map/ppermute | solution.py:250
  80.8 2.7 %finish.1 = bf16[256,512]{1,0:T(8,128)(2,1)} custom-call(s32[1]{0:T(128)} %bitcast.me_ref, bf16[256,512]{1,0:T(8,128)(2,1)} %tokens_ref.5, bf16[8,128,128]{2,1,0:T(8,128)(2,1)} %copy-done, bf16[256,512]{1,0:T(8,128)(2,1)} %project_gating.1.gating_ref, bf16[512,512]{1,0:T(8,128)(2,1)} %weights_ref.1), custom_call_target="tpu_custom_call" | custom-call | tf_op jit(solution)/shard_map/finish/pallas_call | solution.py:318
  (76 shorter events, 6.9 us)
Async XLA Ops:
  0.0 14.5 %copy-start.3 = (s32[64]{0:T(128)S(1)}, s32[64]{0:T(128)}, u32[]{:S(2)}) copy-start(s32[64]{0:T(128)} %param.7) | copy-start | bytes 772
  3.3 14.9 %copy-start.2 = (bf16[384,128]{1,0:T(8,128)(2,1)S(1)}, bf16[384,128]{1,0:T(8,128)(2,1)}, u32[]{:S(2)}) copy-start(bf16[384,128]{1,0:T(8,128)(2,1)} %get-tuple-element.19) | copy-start | bytes 294916
  3.3 23.6 %copy-start.1 = (bf16[384,128]{1,0:T(8,128)(2,1)S(1)}, bf16[384,128]{1,0:T(8,128)(2,1)}, u32[]{:S(2)}) copy-start(bf16[384,128]{1,0:T(8,128)(2,1)} %get-tuple-element.18) | copy-start | bytes 294916
  3.3 29.9 %collective-permute-start = (bf16[384,128]{1,0:T(8,128)(2,1)}, bf16[384,128]{1,0:T(8,128)(2,1)S(1)}, u32[]{:S(2)}, u32[]{:S(2)}) collective-permute-start(bf16[384,128]{1,0:T(8,128)(2,1)} %get-tuple-element.14), channel_id=1, source_target_pairs={{0,1},{1,0},{2,3},{3,2},{4,5},{5,4},{6,7},{7,6},{8,9},{9,8},{10,11... | collective-permute-start | bytes 294920 | tf_op jit(solution)/shard_map/ppermute | solution.py:250
  5.0 28.2 %collective-permute-start.1 = (bf16[384,128]{1,0:T(8,128)(2,1)}, bf16[384,128]{1,0:T(8,128)(2,1)S(1)}, u32[]{:S(2)}, u32[]{:S(2)}) collective-permute-start(bf16[384,128]{1,0:T(8,128)(2,1)} %get-tuple-element.15), channel_id=1, source_target_pairs={{0,2},{1,3},{2,0},{3,1},{4,6},{5,7},{6,4},{7,5},{8,10},{9,11},{10,... | collective-permute-start | bytes 294920 | tf_op jit(solution)/shard_map/ppermute | solution.py:250
  7.6 25.6 %collective-permute-start.2 = (bf16[384,128]{1,0:T(8,128)(2,1)}, bf16[384,128]{1,0:T(8,128)(2,1)S(1)}, u32[]{:S(2)}, u32[]{:S(2)}) collective-permute-start(bf16[384,128]{1,0:T(8,128)(2,1)} %get-tuple-element.16), channel_id=1, source_target_pairs={{0,3},{1,2},{2,1},{3,0},{4,7},{5,6},{6,5},{7,4},{8,11},{9,10},{10,... | collective-permute-start | bytes 294920 | tf_op jit(solution)/shard_map/ppermute | solution.py:250
  7.8 24.7 %collective-permute-start.4 = (bf16[384,128]{1,0:T(8,128)(2,1)}, bf16[384,128]{1,0:T(8,128)(2,1)S(1)}, u32[]{:S(2)}, u32[]{:S(2)}) collective-permute-start(bf16[384,128]{1,0:T(8,128)(2,1)} %get-tuple-element.17), channel_id=1, source_target_pairs={{0,8},{1,9},{2,10},{3,11},{4,12},{5,13},{6,14},{7,15},{8,0},{9,1},... | collective-permute-start | bytes 294920 | tf_op jit(solution)/shard_map/ppermute | solution.py:250
  9.3 8.9 %collective-permute-start.7 = (bf16[384,128]{1,0:T(8,128)(2,1)}, bf16[384,128]{1,0:T(8,128)(2,1)S(1)}, u32[]{:S(2)}, u32[]{:S(2)}) collective-permute-start(bf16[384,128]{1,0:T(8,128)(2,1)} %get-tuple-element.20), channel_id=1, source_target_pairs={{0,11},{1,10},{2,9},{3,8},{4,15},{5,14},{6,13},{7,12},{8,3},{9,2},... | collective-permute-start | bytes 294920 | tf_op jit(solution)/shard_map/ppermute | solution.py:250
  18.2 8.8 %collective-permute-start.6 = (bf16[384,128]{1,0:T(8,128)(2,1)S(1)}, bf16[384,128]{1,0:T(8,128)(2,1)S(1)}, u32[]{:S(2)}, u32[]{:S(2)}) collective-permute-start(bf16[384,128]{1,0:T(8,128)(2,1)S(1)} %copy-done.2), channel_id=1, source_target_pairs={{0,10},{1,11},{2,8},{3,9},{4,14},{5,15},{6,12},{7,13},{8,2},{9,3},... | collective-permute-start | bytes 294920 | tf_op jit(solution)/shard_map/ppermute | solution.py:250
  27.0 5.5 %collective-permute-start.5 = (bf16[384,128]{1,0:T(8,128)(2,1)S(1)}, bf16[384,128]{1,0:T(8,128)(2,1)S(1)}, u32[]{:S(2)}, u32[]{:S(2)}) collective-permute-start(bf16[384,128]{1,0:T(8,128)(2,1)S(1)} %copy-done.1), channel_id=1, source_target_pairs={{0,9},{1,8},{2,11},{3,10},{4,13},{5,12},{6,15},{7,14},{8,1},{9,0},... | collective-permute-start | bytes 294920 | tf_op jit(solution)/shard_map/ppermute | solution.py:250
  32.6 14.4 %collective-permute-start.12 = (bf16[4,256,128]{2,1,0:T(8,128)(2,1)S(1)}, bf16[4,256,128]{2,1,0:T(8,128)(2,1)S(1)}, u32[]{:S(2)}, u32[]{:S(2)}) collective-permute-start(bf16[4,256,128]{2,1,0:T(8,128)(2,1)S(1)} %pad_maximum_fusion.1.refs_1_), channel_id=1, source_target_pairs={{0,4},{4,0},{8,12},{12,8},{16,20},{20,16},{24,28},{28,24},{1,5},{5... | collective-permute-start | bytes 786440 | tf_op jit(solution)/shard_map/ppermute | solution.py:253
  32.6 9.2 %collective-permute-start.8 = (bf16[4,256,128]{2,1,0:T(8,128)(2,1)S(1)}, bf16[4,256,128]{2,1,0:T(8,128)(2,1)S(1)}, u32[]{:S(2)}, u32[]{:S(2)}) collective-permute-start(bf16[4,256,128]{2,1,0:T(8,128)(2,1)S(1)} %pad_maximum_fusion.1.refs_1_), channel_id=1, source_target_pairs={{0,16},{4,20},{8,24},{12,28},{16,0},{20,4},{24,8},{28,12},{1,17},{... | collective-permute-start | bytes 786440 | tf_op jit(solution)/shard_map/ppermute | solution.py:253
  33.3 13.7 %collective-permute-start.11 = (bf16[4,256,128]{2,1,0:T(8,128)(2,1)S(1)}, bf16[4,256,128]{2,1,0:T(8,128)(2,1)S(1)}, u32[]{:S(2)}, u32[]{:S(2)}) collective-permute-start(bf16[4,256,128]{2,1,0:T(8,128)(2,1)S(1)} %pad_maximum_fusion.refs_0_), channel_id=1, source_target_pairs={{0,4},{4,0},{8,12},{12,8},{16,20},{20,16},{24,28},{28,24},{1,5},{5... | collective-permute-start | bytes 786440 | tf_op jit(solution)/shard_map/ppermute | solution.py:253
  33.6 13.4 %collective-permute-start.3 = (bf16[4,256,128]{2,1,0:T(8,128)(2,1)S(1)}, bf16[4,256,128]{2,1,0:T(8,128)(2,1)S(1)}, u32[]{:S(2)}, u32[]{:S(2)}) collective-permute-start(bf16[4,256,128]{2,1,0:T(8,128)(2,1)S(1)} %pad_maximum_fusion.refs_0_), channel_id=1, source_target_pairs={{0,16},{4,20},{8,24},{12,28},{16,0},{20,4},{24,8},{28,12},{1,17},{... | collective-permute-start | bytes 786440 | tf_op jit(solution)/shard_map/ppermute | solution.py:253
  41.8 12.7 %collective-permute-start.10 = (bf16[4,256,128]{2,1,0:T(8,128)(2,1)S(1)}, bf16[4,256,128]{2,1,0:T(8,128)(2,1)S(1)}, u32[]{:S(2)}, u32[]{:S(2)}) collective-permute-start(bf16[4,256,128]{2,1,0:T(8,128)(2,1)S(1)} %collective-permute-done.8.refs_1_), channel_id=1, source_target_pairs={{0,4},{4,0},{8,12},{12,8},{16,20},{20,16},{24,28},{28,24},{1,5},{5... | collective-permute-start | bytes 786440 | tf_op jit(solution)/shard_map/ppermute | solution.py:253
  47.0 7.5 %collective-permute-start.9 = (bf16[4,256,128]{2,1,0:T(8,128)(2,1)S(1)}, bf16[4,256,128]{2,1,0:T(8,128)(2,1)S(1)}, u32[]{:S(2)}, u32[]{:S(2)}) collective-permute-start(bf16[4,256,128]{2,1,0:T(8,128)(2,1)S(1)} %collective-permute-done.3.refs_0_), channel_id=1, source_target_pairs={{0,4},{4,0},{8,12},{12,8},{16,20},{20,16},{24,28},{28,24},{1,5},{5... | collective-permute-start | bytes 786440 | tf_op jit(solution)/shard_map/ppermute | solution.py:253
  60.3 11.1 %collective-permute-start.13 = (bf16[128,128]{1,0:T(8,128)(2,1)S(1)}, bf16[128,128]{1,0:T(8,128)(2,1)S(1)}, u32[]{:S(2)}, u32[]{:S(2)}) collective-permute-start(bf16[128,128]{1,0:T(8,128)(2,1)S(1)} %get-tuple-element.29), channel_id=1, source_target_pairs={{0,1},{1,0},{2,3},{3,2},{4,5},{5,4},{6,7},{7,6},{8,9},{9,8},{10,11... | collective-permute-start | bytes 98312 | tf_op jit(solution)/shard_map/ppermute | solution.py:250
  66.4 9.5 %collective-permute-start.16 = (bf16[128,128]{1,0:T(8,128)(2,1)S(1)}, bf16[128,128]{1,0:T(8,128)(2,1)S(1)}, u32[]{:S(2)}, u32[]{:S(2)}) collective-permute-start(bf16[128,128]{1,0:T(8,128)(2,1)S(1)} %get-tuple-element.26), channel_id=1, source_target_pairs={{0,8},{1,9},{2,10},{3,11},{4,12},{5,13},{6,14},{7,15},{8,0},{9,1},... | collective-permute-start | bytes 98312 | tf_op jit(solution)/shard_map/ppermute | solution.py:250
  67.0 6.4 %collective-permute-start.14 = (bf16[128,128]{1,0:T(8,128)(2,1)S(1)}, bf16[128,128]{1,0:T(8,128)(2,1)S(1)}, u32[]{:S(2)}, u32[]{:S(2)}) collective-permute-start(bf16[128,128]{1,0:T(8,128)(2,1)S(1)} %get-tuple-element.28), channel_id=1, source_target_pairs={{0,2},{1,3},{2,0},{3,1},{4,6},{5,7},{6,4},{7,5},{8,10},{9,11},{10,... | collective-permute-start | bytes 98312 | tf_op jit(solution)/shard_map/ppermute | solution.py:250
  68.1 7.8 %collective-permute-start.15 = (bf16[128,128]{1,0:T(8,128)(2,1)S(1)}, bf16[128,128]{1,0:T(8,128)(2,1)S(1)}, u32[]{:S(2)}, u32[]{:S(2)}) collective-permute-start(bf16[128,128]{1,0:T(8,128)(2,1)S(1)} %get-tuple-element.27), channel_id=1, source_target_pairs={{0,3},{1,2},{2,1},{3,0},{4,7},{5,6},{6,5},{7,4},{8,11},{9,10},{10,... | collective-permute-start | bytes 98312 | tf_op jit(solution)/shard_map/ppermute | solution.py:250
  69.6 6.3 %collective-permute-start.17 = (bf16[128,128]{1,0:T(8,128)(2,1)S(1)}, bf16[128,128]{1,0:T(8,128)(2,1)S(1)}, u32[]{:S(2)}, u32[]{:S(2)}) collective-permute-start(bf16[128,128]{1,0:T(8,128)(2,1)S(1)} %get-tuple-element.25), channel_id=1, source_target_pairs={{0,9},{1,8},{2,11},{3,10},{4,13},{5,12},{6,15},{7,14},{8,1},{9,0},... | collective-permute-start | bytes 98312 | tf_op jit(solution)/shard_map/ppermute | solution.py:250
  71.4 5.7 %collective-permute-start.18 = (bf16[128,128]{1,0:T(8,128)(2,1)S(1)}, bf16[128,128]{1,0:T(8,128)(2,1)S(1)}, u32[]{:S(2)}, u32[]{:S(2)}) collective-permute-start(bf16[128,128]{1,0:T(8,128)(2,1)S(1)} %get-tuple-element.24), channel_id=1, source_target_pairs={{0,10},{1,11},{2,8},{3,9},{4,14},{5,15},{6,12},{7,13},{8,2},{9,3},... | collective-permute-start | bytes 98312 | tf_op jit(solution)/shard_map/ppermute | solution.py:250
  73.4 6.7 %collective-permute-start.19 = (bf16[128,128]{1,0:T(8,128)(2,1)S(1)}, bf16[128,128]{1,0:T(8,128)(2,1)S(1)}, u32[]{:S(2)}, u32[]{:S(2)}) collective-permute-start(bf16[128,128]{1,0:T(8,128)(2,1)S(1)} %get-tuple-element.23), channel_id=1, source_target_pairs={{0,11},{1,10},{2,9},{3,8},{4,15},{5,14},{6,13},{7,12},{8,3},{9,2},... | collective-permute-start | bytes 98312 | tf_op jit(solution)/shard_map/ppermute | solution.py:250
  80.1 0.7 copy-start

commit v2 on v1

--- a/solution.py
+++ b/solution.py
@@ -66,31 +66,23 @@
 
 
 def attend(
-    opens, closes, reach_ref, start_ref, inverse_ref, block_ref, slot_ref, queries_ref, *refs
+    opens, closes, start_ref, inverse_ref, block_ref, team_ref, slot_ref, queries_ref, *refs
 ):
     step = pl.program_id(0)
-    held, total, queries, sems = refs[-4:]
-    out_ref = refs[-5]
-    parts = refs[: -5 if opens else -6]
+    held, total, queries, sem = refs[-4:]
+    out_ref, keys_ref = refs[-5], refs[0]
     rows = held.shape[1]
     half = rows // 2
     tiles = rows // TILE
 
     @pl.when(step == 0)
     def _():
-        copies, at = [], 0
-        for i, part in enumerate(parts):
-            copies.append(
-                pltpu.make_async_copy(part, held.at[pl.ds(at, part.shape[0])], sems.at[i])
-            )
-            at += part.shape[0]
-        for copy in copies:
-            copy.start()
-        for copy in copies:
-            copy.wait()
+        copy = pltpu.make_async_copy(keys_ref, held, sem)
+        copy.start()
+        copy.wait()
 
     low = low_lanes(half)
-    blocks = [block_ref[reach_ref[2] + step * TEAM + i] for i in range(TEAM)]
+    blocks = [block_ref[step * TEAM + i] for i in range(TEAM)]
     for i in range(TEAM):
         packed = queries_ref[i].astype(f32)
         queries[i * rows : i * rows + half] = jnp.where(low, packed, 0.0).astype(bf16)
@@ -104,14 +96,14 @@
     for start in starts[1:]:
         low_start = jnp.minimum(low_start, start)
         high_start = jnp.maximum(high_start, start)
-    total[...] = jnp.zeros_like(total) if opens else refs[-6][...]
-
-    def add(key_block, count, masked):
-        key_rows = [held[slot_ref[key_block + i]] for i in range(count)]
-        key_rows = jnp.concatenate(key_rows, axis=0)
+    total[...] = jnp.zeros_like(total) if opens else refs[1][...]
+
+    def add(team, key_block, masked, chosen):
+        key_rows = jnp.concatenate([held[slot_ref[team * TEAM + i]] for i in range(TEAM)], axis=0)
         if masked:
-            column = lax.broadcasted_iota(jnp.int32, (TILE, count * rows), 1)
-            ahead = column - lax.broadcasted_iota(jnp.int32, (TILE, count * rows), 0)
+            column = lax.broadcasted_iota(jnp.int32, (TILE, TEAM * rows), 1)
+            ahead = column - lax.broadcasted_iota(jnp.int32, (TILE, TEAM * rows), 0)
+
         def add_to(i):
             at = slice(i * rows, (i + 1) * rows)
             score = lax.dot_general(
@@ -129,30 +121,22 @@
             total[at] += jnp.dot(weights.astype(bf16), key_rows, preferred_element_type=f32)
 
         for i in range(TEAM):
-            if masked:
-                needed = starts[i * tiles] < (key_block + count) * tiles
+            if chosen:
+                needed = starts[i * tiles] < (key_block + TEAM) * tiles
                 pl.when(needed)(functools.partial(add_to, i))
             else:
                 add_to(i)
 
-    def loop(begin, end, masked):
-        def body(index, carry):
-            add(index * TEAM, TEAM, masked)
-            return carry
-
-        lax.fori_loop(begin // TEAM, end // TEAM, body, 0)
-
-    reach_low, reach_high = reach_ref[0], jnp.minimum(reach_ref[1], least)
-    first = jnp.maximum(low_start // (tiles * TEAM) * TEAM, reach_low)
-    whole = (high_start + tiles * TEAM - 1) // (tiles * TEAM) * TEAM
-    whole = jnp.maximum(first, jnp.minimum(whole, reach_high))
-    loop(first, jnp.minimum(whole, reach_high), True)
-    loop(whole, reach_high, False)
-
-    @pl.when(least < reach_ref[1])
-    def _():
-        add(least, TEAM, True)
-
+    def one_team(team, carry):
+        key_block = team_ref[team]
+        before = (key_block < least) & ((key_block + TEAM) * tiles > low_start)
+        whole = key_block * tiles >= high_start
+        pl.when(before & whole)(lambda: add(team, key_block, False, False))
+        pl.when(before & ~whole)(lambda: add(team, key_block, True, True))
+        pl.when(key_block == least)(lambda: add(team, key_block, True, False))
+        return carry
+
+    lax.fori_loop(0, held.shape[0] // TEAM, one_team, 0)
     if not closes:
         out_ref[...] = total[...]
         return
@@ -160,39 +144,38 @@
         at = i * rows
         upper = total[at : at + half] * inverse_ref[blocks[i] * tiles]
         lower = total[at + half : at + rows] * inverse_ref[blocks[i] * tiles + tiles - 1]
-        out_ref[i] = jnp.where(low, swap_halves(upper), lower).astype(bf16)
-
-
-def attend_call(tables, reach, queries, parts, before=None, closes=True):
+        out_ref[i] = jnp.where(low, swap_halves(upper), lower).astype(out_ref.dtype)
+
+
+def attend_call(tables, queries, keys, before=None, gives=None):
     half, rows = queries.shape[1], 2 * queries.shape[1]
     steps = queries.shape[0] // TEAM
-    held_blocks = sum(array.shape[0] for array in parts)
     totals = pl.BlockSpec((TEAM * rows, LANES), lambda i, *_: (i, 0))
     packed = pl.BlockSpec((TEAM, half, LANES), lambda i, *_: (i, 0, 0))
     extra = [] if before is None else [before]
     return pl.pallas_call(
-        functools.partial(attend, before is None, closes),
+        functools.partial(attend, before is None, gives is not None),
         grid_spec=pltpu.PrefetchScalarGridSpec(
             num_scalar_prefetch=5,
             grid=(steps,),
-            in_specs=[packed] + [ANY] * len(parts) + [totals] * len(extra),
-            out_specs=packed if closes else totals,
+            in_specs=[packed, ANY] + [totals] * len(extra),
+            out_specs=totals if gives is None else packed,
             scratch_shapes=[
-                pltpu.VMEM((held_blocks, rows, LANES), bf16),
+                pltpu.VMEM(keys.shape, bf16),
                 pltpu.VMEM((TEAM * rows, LANES), f32),
                 pltpu.VMEM((TEAM * rows, LANES), bf16),
-                pltpu.SemaphoreType.DMA((len(parts),)),
+                pltpu.SemaphoreType.DMA,
             ],
         ),
-        out_shape=jax.ShapeDtypeStruct(queries.shape, bf16)
-        if closes
-        else jax.ShapeDtypeStruct((steps * TEAM * rows, LANES), f32),
+        out_shape=jax.ShapeDtypeStruct((steps * TEAM * rows, LANES), f32)
+        if gives is None
+        else jax.ShapeDtypeStruct(queries.shape, gives),
         compiler_params=pltpu.CompilerParams(vmem_limit_bytes=40 << 20),
         cost_estimate=pl.CostEstimate(
             flops=steps * 2_000_000_000, bytes_accessed=4_000_000, transcendentals=4_000_000
         ),
         name="attend",
-    )(reach, *tables, queries, *parts, *extra)
+    )(*tables, queries, keys, *extra)
 
 
 def finish(me_ref, tokens_ref, attention_ref, gating_ref, weights_ref, out_ref):
@@ -270,50 +253,46 @@
         name="project_gating",
     )(tokens, w_proj)
 
-    index = jnp.arange(blocks, dtype=jnp.int32)
-    block_head, block_seq = index % head_size, index // head_size
-    block_core = block_seq % share
-    block_me = (block_seq // share % fold) * head_size + block_head
-    block_group = block_seq // (share * fold)
-    from_me = jnp.bitwise_xor(block_me, me)
-    asked = jnp.arange(H, dtype=jnp.int32) ^ me
-    query_block = (
-        (group * fold + asked // head_size) * share + core
-    ) * head_size + asked % head_size
     start = jnp.sum((tile_user[None, :] < tile_user[:, None]).astype(jnp.int32), axis=1)
     length = jnp.sum((tile_user[None, :] == tile_user[:, None]).astype(f32), axis=1) * TILE
-
-    def reach(first, last, query):
-        return jnp.stack([jnp.asarray(v, jnp.int32) for v in (first, last, query)])
+    asked = jnp.arange(H, dtype=jnp.int32) ^ me
+
+    def blocks_of(places, in_group, in_core):
+        in_seq = (in_group * fold + places // head_size) * share + in_core
+        return in_seq * head_size + places % head_size
 
     arrived = [partner(sent[k], k) for k in range(H)]
     queries = jnp.stack([array[rows:] for array in arrived])
-    arrived = [array[:rows] for array in arrived]
+    keys = jnp.stack([array[:rows] for array in arrived])
+    first_places = jnp.arange(0, H, TEAM, dtype=jnp.int32)
+    mine = blocks_of(asked, group, core)
     if groups == 2 and share == 2:
-        lots = [jnp.stack(arrived[:TEAM]), jnp.stack(arrived[TEAM:])]
-        far = [seq_flip(lot, fold * share) for lot in lots]
-        near = lots + [seq_flip(lot, 1) for lot in lots]
-        far = far + [seq_flip(lot, 1) for lot in far]
-        slot = jnp.bitwise_xor(block_core, core) * H + from_me
-        tables = (start, 1.0 / length, query_block, slot)
-        bound = group * (blocks // groups)
-        totals = attend_call(tables, reach(bound, blocks, 0), queries, near, closes=False)
+        far_keys = seq_flip(keys, fold * share)
+        other_queries = seq_flip(queries, 1)
+        others = blocks_of(asked, group, 1 - core)
+
+        def tables(query_blocks, in_group):
+            return start, 1.0 / length, query_blocks, blocks_of(first_places, in_group, core), asked
+
+        totals = attend_call(
+            tables(jnp.concatenate([others, mine]), group),
+            jnp.concatenate([other_queries, queries]),
+            keys,
+        )
         size = totals.shape[0] // 2
-        attention = [None] * H
-        for begin in (TEAM, 0):
-            team = attend_call(
-                tables,
-                reach(0, bound, begin),
-                queries[begin : begin + TEAM],
-                far,
-                before=totals[size * (begin // TEAM) : size * (begin // TEAM + 1)],
-            )
-            for k in range(TEAM):
-                attention[begin + k] = team[k]
+        far_keys, totals = lax.optimization_barrier((far_keys, totals))
+        theirs = attend_call(
+            tables(others, 1 - group), other_queries, far_keys, totals[:size], bf16
+        )
+        theirs = seq_flip(theirs, 1)
+        ours = attend_call(tables(mine, 1 - group), queries, far_keys, totals[size:], f32)
+        attention = (ours + theirs.astype(f32)).astype(bf16)
     else:
-        everything = lax.all_gather(jnp.stack(arrived), "seq", axis=0, tiled=True)
-        tables = (start, 1.0 / length, query_block, block_seq * H + from_me)
-        attention = attend_call(tables, reach(0, blocks, 0), queries, [everything])
+        everything = lax.all_gather(keys, "seq", axis=0, tiled=True)
+        index = jnp.arange(blocks, dtype=jnp.int32)
+        slot = index // head_size * H + jnp.bitwise_xor(index % head_size, me)
+        tables = (start, 1.0 / length, mine, index[::TEAM], slot)
+        attention = attend_call(tables, queries, everything, gives=bf16)
     returned = jnp.stack([partner(attention[k], k) for k in range(H)])
     return pl.pallas_call(
         finish,

time: 83.8 us -> 70.4 us (0.84)
  waiting for transfers between devices: 23.2 us -> 16.9 us
  starting transfers between devices: 30.2 us -> 25.5 us
  Pallas kernels: 25.7 us -> 23.5 us
    ppermute x6 -> x3, waiting for transfers between devices: 11.7 us -> 6.85 us  [seq_flip(): return lax.ppermute(array, 'seq', [(s, s ^ bit) for s in range(seq_size)])]
    ppermute x14, starting transfers between devices: 27.8 us -> 24.8 us  [partner(): return lax.ppermute(array, ('seq', 'head'), pairs)]
    pallas_call x3, Pallas kernels: 17.4 us -> 15.2 us  [attend_call(): pl.pallas_call(functools.partial(attend, before is None, gives is not Non...]
    unnamed x21 -> x32, local copies, waits for them, and re-layouts: 1.59 us -> 3.35 us
    ppermute x6 -> x3, starting transfers between devices: 2.4 us -> 0.71 us  [seq_flip(): return lax.ppermute(array, 'seq', [(s, s ^ bit) for s in range(seq_size)])]
    ppermute x14, waiting for transfers between devices: 11.5 us -> 10 us  [partner(): return lax.ppermute(array, ('seq', 'head'), pairs)]
    another operation x8 -> x1, local copies, waits for them, and re-layouts: 0.88 us -> 0.01 us  [per_device(): keys = jnp.stack([array[:rows] for array in arrived])]
  transfers between devices with their start and end apart: 20 -> 17, of which waited for: 6 -> 5; matrix products, arithmetic and copies ran while one was open for 4% -> 5% of each run, Pallas kernels for 17% -> 19%
where the time goes in v2:
time: 70.4 us; the launch traced here: 70.3 us
  starting transfers between devices  25.5 us (36%)
  Pallas kernels  23.5 us (33%)
  waiting for transfers between devices  16.9 us (24%)
  local copies, waits for them, and re-layouts  3.55 us (5%)
    ppermute x14, starting transfers between devices, partner(): return lax.ppermute(array, ('seq', 'head'), pairs)  24.8 us
    pallas_call x3, Pallas kernels, attend_call(): pl.pallas_call(functools.partial(attend, before is None, gives is not Non...  15.2 us
    ppermute x14, waiting for transfers between devices, partner(): return lax.ppermute(array, ('seq', 'head'), pairs)  10 us
    ppermute x3, waiting for transfers between devices, seq_flip(): return lax.ppermute(array, 'seq', [(s, s ^ bit) for s in range(seq_size)])  6.85 us
    unnamed x32, local copies, waits for them, and re-layouts  3.35 us
    pallas_call x1, Pallas kernels, per_device(): pl.pallas_call(project, out_shape=[jax.ShapeDtypeStruct((rows + half, LAN...  3.32 us
    pallas_call x1, Pallas kernels, per_device(): pl.pallas_call(finish, out_shape=jax.ShapeDtypeStruct((rows, width), bf16...  2.67 us
    pallas_call x1, Pallas kernels, per_device(): pl.pallas_call(project_gating, out_shape=jax.ShapeDtypeStruct((rows, H *...  2.31 us
  transfers between devices with their start and end apart: 17, of which 5 were waited for; matrix products, arithmetic and copies ran while one was open for 5% of the time, Pallas kernels for 19%

profile of v2, /device:TPU:4, one launch (start us, length us, event | category | flops | bytes accessed | tf_op | source)
XLA Modules:
  0.0 70.3 jit_solution(17674316126549978686)
XLA Ops:
  0.0 3.3 %project.1 = (bf16[384,128]{1,0:T(8,128)(2,1)}, bf16[384,128]{1,0:T(8,128)(2,1)}, bf16[384,128]{1,0:T(8,128)(2,1)}, bf16[384,128]{1,0:T(8,128)(2,1)}, bf16[384,1...) custom-call(s32[1]{0:T(128)} %bitcast.me_ref, ...), custom_call_target="tpu_custom_call" | custom-call | tf_op jit(solution)/shard_map/project/pallas_call | solution.py:238
  3.3 1.6 %collective-permute-start = (bf16[384,128]{1,0:T(8,128)(2,1)}, bf16[384,128]{1,0:T(8,128)(2,1)S(1)}, u32[]{:S(2)}, u32[]{:S(2)}) collective-permute-start(bf16[384,128]{1,0:T(8,128)(2,1)} %get-tuple-element.16), channel_id=1, source_target_pairs={{0,1},{1,0},{2,3},{3,2},{4,5},{5,4},{6,7},{7,6},{8,9},{9,8},{10,11... | collective-permute-start | bytes 294920 | tf_op jit(solution)/shard_map/ppermute | solution.py:233
  4.9 2.6 %collective-permute-start.1 = (bf16[384,128]{1,0:T(8,128)(2,1)}, bf16[384,128]{1,0:T(8,128)(2,1)S(1)}, u32[]{:S(2)}, u32[]{:S(2)}) collective-permute-start(bf16[384,128]{1,0:T(8,128)(2,1)} %get-tuple-element.17), channel_id=1, source_target_pairs={{0,2},{1,3},{2,0},{3,1},{4,6},{5,7},{6,4},{7,5},{8,10},{9,11},{10,... | collective-permute-start | bytes 294920 | tf_op jit(solution)/shard_map/ppermute | solution.py:233
  7.7 1.5 %collective-permute-start.3 = (bf16[384,128]{1,0:T(8,128)(2,1)}, bf16[384,128]{1,0:T(8,128)(2,1)S(1)}, u32[]{:S(2)}, u32[]{:S(2)}) collective-permute-start(bf16[384,128]{1,0:T(8,128)(2,1)} %get-tuple-element.19), channel_id=1, source_target_pairs={{0,8},{1,9},{2,10},{3,11},{4,12},{5,13},{6,14},{7,15},{8,0},{9,1},... | collective-permute-start | bytes 294920 | tf_op jit(solution)/shard_map/ppermute | solution.py:233
  11.0 0.8 %constant_dynamic-update-slice_fusion.15 = bf16[8,256,128]{2,1,0:T(8,128)(2,1)S(1)} fusion(bf16[384,128]{1,0:T(8,128)(2,1)} %get-tuple-element.15), kind=kLoop, calls=%fused_computation.16 | loop fusion | bytes 131072
  12.0 4.4 %collective-permute-start.5 = (bf16[384,128]{1,0:T(8,128)(2,1)}, bf16[384,128]{1,0:T(8,128)(2,1)S(1)}, u32[]{:S(2)}, u32[]{:S(2)}) collective-permute-start(bf16[384,128]{1,0:T(8,128)(2,1)} %get-tuple-element.21), channel_id=1, source_target_pairs={{0,10},{1,11},{2,8},{3,9},{4,14},{5,15},{6,12},{7,13},{8,2},{9,3},... | collective-permute-start | bytes 294920 | tf_op jit(solution)/shard_map/ppermute | solution.py:233
  16.4 2.6 %collective-permute-start.6 = (bf16[384,128]{1,0:T(8,128)(2,1)}, bf16[384,128]{1,0:T(8,128)(2,1)S(1)}, u32[]{:S(2)}, u32[]{:S(2)}) collective-permute-start(bf16[384,128]{1,0:T(8,128)(2,1)} %get-tuple-element.22), channel_id=1, source_target_pairs={{0,11},{1,10},{2,9},{3,8},{4,15},{5,14},{6,13},{7,12},{8,3},{9,2},... | collective-permute-start | bytes 294920 | tf_op jit(solution)/shard_map/ppermute | solution.py:233
  19.1 5.8 %collective-permute-done.5 = bf16[384,128]{1,0:T(8,128)(2,1)S(1)} collective-permute-done((bf16[384,128]{1,0:T(8,128)(2,1)}, bf16[384,128]{1,0:T(8,128)(2,1)S(1)}, u32[]{:S(2)}, u32[]{:S(2)}) %collective-permute-start.5) | collective-permute-done | bytes 98336 | tf_op jit(solution)/shard_map/ppermute | solution.py:233
  25.7 0.8 %collective-permute-done.8.queries_ref = bf16[8,128,128]{2,1,0:T(8,128)(2,1)S(1)} collective-permute-done((bf16[8,128,128]{2,1,0:T(8,128)(2,1)S(1)}, bf16[8,128,128]{2,1,0:T(8,128)(2,1)S(1)}, u32[]{:S(2)}, u32[]{:S(2)}) %collective-permute-start.8) | collective-permute-done | bytes 262176 | tf_op jit(solution)/shard_map/ppermute | solution.py:236
  26.5 0.8 %constant_dynamic-update-slice_fusion.23 = bf16[16,128,128]{2,1,0:T(8,128)(2,1)S(1)} fusion(bf16[16,128,128]{2,1,0:T(8,128)(2,1)S(1)} %constant_dynamic-update-slice_fusion.24, bf16[384,128]{1,0:T(8,128)(2,1)} %get-tuple-element.15), kind=kLoop, calls=%fused_computation.24 | loop fusion | bytes 65536
  27.4 6.1 %attend.3 = f32[4096,128]{1,0:T(8,128)S(1)} custom-call(s32[64]{0:T(128)S(1)} %convert_reduce_fusion.1.start_ref, f32[64]{0:T(128)S(1)} %multiply_divide_fusion.inverse_ref, s32[16]{0:T(128)S(1)} %pad_add_fusion.block_ref, s32[2]{0:T(128)S(1)} %multiply_add_fusion.team_ref, s32[8]{0:T(128)S(1)} %iota_xor_fusion.slot_ref, ...), custom_call_target="tpu_custom_call" | custom-call | flops 8000000000 | bytes 4000000 | tf_op jit(solution)/shard_map/attend/pallas_call | solution.py:156
  33.5 6.0 %collective-permute-done.7.refs_0_ = bf16[8,256,128]{2,1,0:T(8,128)(2,1)S(1)} collective-permute-done((bf16[8,256,128]{2,1,0:T(8,128)(2,1)S(1)}, bf16[8,256,128]{2,1,0:T(8,128)(2,1)S(1)}, u32[]{:S(2)}, u32[]{:S(2)}) %collective-permute-start.7) | collective-permute-done | bytes 524320 | tf_op jit(solution)/shard_map/ppermute | solution.py:236
  39.6 4.4 %attend.5 = bf16[8,128,128]{2,1,0:T(8,128)(2,1)S(1)} custom-call(s32[64]{0:T(128)S(1)} %convert_reduce_fusion.1.start_ref, f32[64]{0:T(128)S(1)} %multiply_divide_fusion.inverse_ref, s32[8]{0:T(128)S(1)} %get-tuple-element.35.block_ref, s32[2]{0:T(128)S(1)} %multiply_add_fusion.2.team_ref, s32[8]{0:T(128)S(1)} %iota_xor_fusion.slot_ref, ...), custom_call_target="tpu_custom_call" | custom-call | flops 4000000000 | bytes 4000000 | tf_op jit(solution)/shard_map/attend/pallas_call | solution.py:156
  44.1 4.8 %attend.4 = f32[8,128,128]{2,1,0:T(8,128)S(1)} custom-call(s32[64]{0:T(128)S(1)} %convert_reduce_fusion.1.start_ref, f32[64]{0:T(128)S(1)} %multiply_divide_fusion.inverse_ref, s32[8]{0:T(128)S(1)} %get-tuple-element.36.block_ref, s32[2]{0:T(128)S(1)} %multiply_add_fusion.2.team_ref, s32[8]{0:T(128)S(1)} %iota_xor_fusion.slot_ref, ...), custom_call_target="tpu_custom_call" | custom-call | flops 4000000000 | bytes 4000000 | tf_op jit(solution)/shard_map/attend/pallas_call | solution.py:156
  49.0 1.6 %collective-permute-start.10 = (bf16[128,128]{1,0:T(8,128)(2,1)S(1)}, bf16[128,128]{1,0:T(8,128)(2,1)S(1)}, u32[]{:S(2)}, u32[]{:S(2)}) collective-permute-start(bf16[128,128]{1,0:T(8,128)(2,1)S(1)} %get-tuple-element.33), channel_id=1, source_target_pairs={{0,1},{1,0},{2,3},{3,2},{4,5},{5,4},{6,7},{7,6},{8,9},{9,8},{10,11... | collective-permute-start | bytes 98312 | tf_op jit(solution)/shard_map/ppermute | solution.py:233
  50.6 2.3 %project_gating.1.gating_ref = bf16[256,512]{1,0:T(8,128)(2,1)} custom-call(bf16[256,512]{1,0:T(8,128)(2,1)} %tokens_ref.5, bf16[512,2048]{1,0:T(8,128)(2,1)} %gating_weights.1), custom_call_target="tpu_custom_call" | custom-call | tf_op jit(solution)/shard_map/project_gating/pallas_call | solution.py:247
  52.9 1.5 %collective-permute-start.11 = (bf16[128,128]{1,0:T(8,128)(2,1)S(1)}, bf16[128,128]{1,0:T(8,128)(2,1)S(1)}, u32[]{:S(2)}, u32[]{:S(2)}) collective-permute-start(bf16[128,128]{1,0:T(8,128)(2,1)S(1)} %get-tuple-element.32), channel_id=1, source_target_pairs={{0,2},{1,3},{2,0},{3,1},{4,6},{5,7},{6,4},{7,5},{8,10},{9,11},{10,... | collective-permute-start | bytes 98312 | tf_op jit(solution)/shard_map/ppermute | solution.py:233
  54.4 1.4 %collective-permute-start.12 = (bf16[128,128]{1,0:T(8,128)(2,1)S(1)}, bf16[128,128]{1,0:T(8,128)(2,1)S(1)}, u32[]{:S(2)}, u32[]{:S(2)}) collective-permute-start(bf16[128,128]{1,0:T(8,128)(2,1)S(1)} %get-tuple-element.31), channel_id=1, source_target_pairs={{0,3},{1,2},{2,1},{3,0},{4,7},{5,6},{6,5},{7,4},{8,11},{9,10},{10,... | collective-permute-start | bytes 98312 | tf_op jit(solution)/shard_map/ppermute | solution.py:233
  56.3 1.6 %collective-permute-start.14 = (bf16[128,128]{1,0:T(8,128)(2,1)S(1)}, bf16[128,128]{1,0:T(8,128)(2,1)S(1)}, u32[]{:S(2)}, u32[]{:S(2)}) collective-permute-start(bf16[128,128]{1,0:T(8,128)(2,1)S(1)} %get-tuple-element.29), channel_id=1, source_target_pairs={{0,9},{1,8},{2,11},{3,10},{4,13},{5,12},{6,15},{7,14},{8,1},{9,0},... | collective-permute-start | bytes 98312 | tf_op jit(solution)/shard_map/ppermute | solution.py:233
  57.8 2.4 %collective-permute-start.15 = (bf16[128,128]{1,0:T(8,128)(2,1)S(1)}, bf16[128,128]{1,0:T(8,128)(2,1)S(1)}, u32[]{:S(2)}, u32[]{:S(2)}) collective-permute-start(bf16[128,128]{1,0:T(8,128)(2,1)S(1)} %get-tuple-element.28), channel_id=1, source_target_pairs={{0,10},{1,11},{2,8},{3,9},{4,14},{5,15},{6,12},{7,13},{8,2},{9,3},... | collective-permute-start | bytes 98312 | tf_op jit(solution)/shard_map/ppermute | solution.py:233
  60.2 2.3 %collective-permute-start.16 = (bf16[128,128]{1,0:T(8,128)(2,1)S(1)}, bf16[128,128]{1,0:T(8,128)(2,1)S(1)}, u32[]{:S(2)}, u32[]{:S(2)}) collective-permute-start(bf16[128,128]{1,0:T(8,128)(2,1)S(1)} %get-tuple-element.27), channel_id=1, source_target_pairs={{0,11},{1,10},{2,9},{3,8},{4,15},{5,14},{6,13},{7,12},{8,3},{9,2},... | collective-permute-start | bytes 98312 | tf_op jit(solution)/shard_map/ppermute | solution.py:233
  62.7 0.9 %collective-permute-done.15 = bf16[128,128]{1,0:T(8,128)(2,1)S(1)} collective-permute-done((bf16[128,128]{1,0:T(8,128)(2,1)S(1)}, bf16[128,128]{1,0:T(8,128)(2,1)S(1)}, u32[]{:S(2)}, u32[]{:S(2)}) %collective-permute-start.15) | collective-permute-done | bytes 32800 | tf_op jit(solution)/shard_map/ppermute | solution.py:233
  63.6 3.4 %collective-permute-done.16 = bf16[128,128]{1,0:T(8,128)(2,1)S(1)} collective-permute-done((bf16[128,128]{1,0:T(8,128)(2,1)S(1)}, bf16[128,128]{1,0:T(8,128)(2,1)S(1)}, u32[]{:S(2)}, u32[]{:S(2)}) %collective-permute-start.16) | collective-permute-done | bytes 32800 | tf_op jit(solution)/shard_map/ppermute | solution.py:233
  67.6 2.7 %finish.1 = bf16[256,512]{1,0:T(8,128)(2,1)} custom-call(s32[1]{0:T(128)} %bitcast.me_ref, bf16[256,512]{1,0:T(8,128)(2,1)} %tokens_ref.5, bf16[8,128,128]{2,1,0:T(8,128)(2,1)} %copy-done, bf16[256,512]{1,0:T(8,128)(2,1)} %project_gating.1.gating_ref, bf16[512,512]{1,0:T(8,128)(2,1)} %weights_ref.1), custom_call_target="tpu_custom_call" | custom-call | tf_op jit(solution)/shard_map/finish/pallas_call | solution.py:297
  (63 shorter events, 4.6 us)
Async XLA Ops:
  0.0 9.8 %copy-start.1 = (s32[64]{0:T(128)S(1)}, s32[64]{0:T(128)}, u32[]{:S(2)}) copy-start(s32[64]{0:T(128)} %param.7) | copy-start | bytes 772
  3.3 8.7 %collective-permute-start = (bf16[384,128]{1,0:T(8,128)(2,1)}, bf16[384,128]{1,0:T(8,128)(2,1)S(1)}, u32[]{:S(2)}, u32[]{:S(2)}) collective-permute-start(bf16[384,128]{1,0:T(8,128)(2,1)} %get-tuple-element.16), channel_id=1, source_target_pairs={{0,1},{1,0},{2,3},{3,2},{4,5},{5,4},{6,7},{7,6},{8,9},{9,8},{10,11... | collective-permute-start | bytes 294920 | tf_op jit(solution)/shard_map/ppermute | solution.py:233
  4.9 11.5 %collective-permute-start.1 = (bf16[384,128]{1,0:T(8,128)(2,1)}, bf16[384,128]{1,0:T(8,128)(2,1)S(1)}, u32[]{:S(2)}, u32[]{:S(2)}) collective-permute-start(bf16[384,128]{1,0:T(8,128)(2,1)} %get-tuple-element.17), channel_id=1, source_target_pairs={{0,2},{1,3},{2,0},{3,1},{4,6},{5,7},{6,4},{7,5},{8,10},{9,11},{10,... | collective-permute-start | bytes 294920 | tf_op jit(solution)/shard_map/ppermute | solution.py:233
  7.5 11.6 %collective-permute-start.2 = (bf16[384,128]{1,0:T(8,128)(2,1)}, bf16[384,128]{1,0:T(8,128)(2,1)S(1)}, u32[]{:S(2)}, u32[]{:S(2)}) collective-permute-start(bf16[384,128]{1,0:T(8,128)(2,1)} %get-tuple-element.18), channel_id=1, source_target_pairs={{0,3},{1,2},{2,1},{3,0},{4,7},{5,6},{6,5},{7,4},{8,11},{9,10},{10,... | collective-permute-start | bytes 294920 | tf_op jit(solution)/shard_map/ppermute | solution.py:233
  7.7 11.4 %collective-permute-start.3 = (bf16[384,128]{1,0:T(8,128)(2,1)}, bf16[384,128]{1,0:T(8,128)(2,1)S(1)}, u32[]{:S(2)}, u32[]{:S(2)}) collective-permute-start(bf16[384,128]{1,0:T(8,128)(2,1)} %get-tuple-element.19), channel_id=1, source_target_pairs={{0,8},{1,9},{2,10},{3,11},{4,12},{5,13},{6,14},{7,15},{8,0},{9,1},... | collective-permute-start | bytes 294920 | tf_op jit(solution)/shard_map/ppermute | solution.py:233
  9.2 9.9 %collective-permute-start.4 = (bf16[384,128]{1,0:T(8,128)(2,1)}, bf16[384,128]{1,0:T(8,128)(2,1)S(1)}, u32[]{:S(2)}, u32[]{:S(2)}) collective-permute-start(bf16[384,128]{1,0:T(8,128)(2,1)} %get-tuple-element.20), channel_id=1, source_target_pairs={{0,9},{1,8},{2,11},{3,10},{4,13},{5,12},{6,15},{7,14},{8,1},{9,0},... | collective-permute-start | bytes 294920 | tf_op jit(solution)/shard_map/ppermute | solution.py:233
  12.0 12.9 %collective-permute-start.5 = (bf16[384,128]{1,0:T(8,128)(2,1)}, bf16[384,128]{1,0:T(8,128)(2,1)S(1)}, u32[]{:S(2)}, u32[]{:S(2)}) collective-permute-start(bf16[384,128]{1,0:T(8,128)(2,1)} %get-tuple-element.21), channel_id=1, source_target_pairs={{0,10},{1,11},{2,8},{3,9},{4,14},{5,15},{6,12},{7,13},{8,2},{9,3},... | collective-permute-start | bytes 294920 | tf_op jit(solution)/shard_map/ppermute | solution.py:233
  16.4 8.5 %collective-permute-start.6 = (bf16[384,128]{1,0:T(8,128)(2,1)}, bf16[384,128]{1,0:T(8,128)(2,1)S(1)}, u32[]{:S(2)}, u32[]{:S(2)}) collective-permute-start(bf16[384,128]{1,0:T(8,128)(2,1)} %get-tuple-element.22), channel_id=1, source_target_pairs={{0,11},{1,10},{2,9},{3,8},{4,15},{5,14},{6,13},{7,12},{8,3},{9,2},... | collective-permute-start | bytes 294920 | tf_op jit(solution)/shard_map/ppermute | solution.py:233
  24.9 1.6 %collective-permute-start.8 = (bf16[8,128,128]{2,1,0:T(8,128)(2,1)S(1)}, bf16[8,128,128]{2,1,0:T(8,128)(2,1)S(1)}, u32[]{:S(2)}, u32[]{:S(2)}) collective-permute-start(bf16[8,128,128]{2,1,0:T(8,128)(2,1)S(1)} %constant_dynamic-update-slice_fusion.queries_ref), channel_id=1, source_target_pairs={{0,4},{4,0},{8,12},{12,8},{16,20},{20,16},{24,28},{28,24},{1,5},{5... | collective-permute-start | bytes 786440 | tf_op jit(solution)/shard_map/ppermute | solution.py:236
  25.1 14.4 %collective-permute-start.7 = (bf16[8,256,128]{2,1,0:T(8,128)(2,1)S(1)}, bf16[8,256,128]{2,1,0:T(8,128)(2,1)S(1)}, u32[]{:S(2)}, u32[]{:S(2)}) collective-permute-start(bf16[8,256,128]{2,1,0:T(8,128)(2,1)S(1)} %constant_dynamic-update-slice_fusion.8.refs_0_), channel_id=1, source_target_pairs={{0,16},{4,20},{8,24},{12,28},{16,0},{20,4},{24,8},{28,12},{1,17},{... | collective-permute-start | bytes 1572872 | tf_op jit(solution)/shard_map/ppermute | solution.py:236
  44.0 4.9 %collective-permute-start.9 = (bf16[8,128,128]{2,1,0:T(8,128)(2,1)S(1)}, bf16[8,128,128]{2,1,0:T(8,128)(2,1)S(1)}, u32[]{:S(2)}, u32[]{:S(2)}) collective-permute-start(bf16[8,128,128]{2,1,0:T(8,128)(2,1)S(1)} %attend.5), channel_id=1, source_target_pairs={{0,4},{4,0},{8,12},{12,8},{16,20},{20,16},{24,28},{28,24},{1,5},{5... | collective-permute-start | bytes 786440 | tf_op jit(solution)/shard_map/ppermute | solution.py:236
  49.0 8.9 %collective-permute-start.10 = (bf16[128,128]{1,0:T(8,128)(2,1)S(1)}, bf16[128,128]{1,0:T(8,128)(2,1)S(1)}, u32[]{:S(2)}, u32[]{:S(2)}) collective-permute-start(bf16[128,128]{1,0:T(8,128)(2,1)S(1)} %get-tuple-element.33), channel_id=1, source_target_pairs={{0,1},{1,0},{2,3},{3,2},{4,5},{5,4},{6,7},{7,6},{8,9},{9,8},{10,11... | collective-permute-start | bytes 98312 | tf_op jit(solution)/shard_map/ppermute | solution.py:233
  52.9 7.4 %collective-permute-start.11 = (bf16[128,128]{1,0:T(8,128)(2,1)S(1)}, bf16[128,128]{1,0:T(8,128)(2,1)S(1)}, u32[]{:S(2)}, u32[]{:S(2)}) collective-permute-start(bf16[128,128]{1,0:T(8,128)(2,1)S(1)} %get-tuple-element.32), channel_id=1, source_target_pairs={{0,2},{1,3},{2,0},{3,1},{4,6},{5,7},{6,4},{7,5},{8,10},{9,11},{10,... | collective-permute-start | bytes 98312 | tf_op jit(solution)/shard_map/ppermute | solution.py:233
  54.4 8.2 %collective-permute-start.12 = (bf16[128,128]{1,0:T(8,128)(2,1)S(1)}, bf16[128,128]{1,0:T(8,128)(2,1)S(1)}, u32[]{:S(2)}, u32[]{:S(2)}) collective-permute-start(bf16[128,128]{1,0:T(8,128)(2,1)S(1)} %get-tuple-element.31), channel_id=1, source_target_pairs={{0,3},{1,2},{2,1},{3,0},{4,7},{5,6},{6,5},{7,4},{8,11},{9,10},{10,... | collective-permute-start | bytes 98312 | tf_op jit(solution)/shard_map/ppermute | solution.py:233
  55.8 6.9 %collective-permute-start.13 = (bf16[128,128]{1,0:T(8,128)(2,1)S(1)}, bf16[128,128]{1,0:T(8,128)(2,1)S(1)}, u32[]{:S(2)}, u32[]{:S(2)}) collective-permute-start(bf16[128,128]{1,0:T(8,128)(2,1)S(1)} %get-tuple-element.30), channel_id=1, source_target_pairs={{0,8},{1,9},{2,10},{3,11},{4,12},{5,13},{6,14},{7,15},{8,0},{9,1},... | collective-permute-start | bytes 98312 | tf_op jit(solution)/shard_map/ppermute | solution.py:233
  56.3 6.4 %collective-permute-start.14 = (bf16[128,128]{1,0:T(8,128)(2,1)S(1)}, bf16[128,128]{1,0:T(8,128)(2,1)S(1)}, u32[]{:S(2)}, u32[]{:S(2)}) collective-permute-start(bf16[128,128]{1,0:T(8,128)(2,1)S(1)} %get-tuple-element.29), channel_id=1, source_target_pairs={{0,9},{1,8},{2,11},{3,10},{4,13},{5,12},{6,15},{7,14},{8,1},{9,0},... | collective-permute-start | bytes 98312 | tf_op jit(solution)/shard_map/ppermute | solution.py:233
  57.8 5.7 %collective-permute-start.15 = (bf16[128,128]{1,0:T(8,128)(2,1)S(1)}, bf16[128,128]{1,0:T(8,128)(2,1)S(1)}, u32[]{:S(2)}, u32[]{:S(2)}) collective-permute-start(bf16[128,128]{1,0:T(8,128)(2,1)S(1)} %get-tuple-element.28), channel_id=1, source_target_pairs={{0,10},{1,11},{2,8},{3,9},{4,14},{5,15},{6,12},{7,13},{8,2},{9,3},... | collective-permute-start | bytes 98312 | tf_op jit(solution)/shard_map/ppermute | solution.py:233
  60.2 6.7 %collective-permute-start.16 = (bf16[128,128]{1,0:T(8,128)(2,1)S(1)}, bf16[128,128]{1,0:T(8,128)(2,1)S(1)}, u32[]{:S(2)}, u32[]{:S(2)}) collective-permute-start(bf16[128,128]{1,0:T(8,128)(2,1)S(1)} %get-tuple-element.27), channel_id=1, source_target_pairs={{0,11},{1,10},{2,9},{3,8},{4,15},{5,14},{6,13},{7,12},{8,3},{9,2},... | collective-permute-start | bytes 98312 | tf_op jit(solution)/shard_map/ppermute | solution.py:233
  66.9 0.7 copy-start

commit v3 on v2

--- a/solution.py
+++ b/solution.py
@@ -39,7 +39,8 @@
 
 
 def project(me_ref, tokens_ref, values_ref, queries_ref, keys_ref, *refs):
-    outs, held = refs[:-1], refs[-1]
+    key_outs, query_outs = refs[:H], refs[H : H + 2]
+    held_keys, held_queries = refs[H + 2 :]
     rows = tokens_ref.shape[0]
     half = rows // 2
     normed = layer_norm(tokens_ref[...].astype(f32)).astype(bf16)
@@ -51,12 +52,14 @@
     for pair in range(H // 2):
         at = slice(pair * LANES, (pair + 1) * LANES)
         key, value, upper, lower = keys[:, at], values[:, at], queries[:half, at], queries[half:, at]
-        held[2 * pair, :rows] = jnp.where(low, key, swap_halves(value)).astype(bf16)
-        held[2 * pair + 1, :rows] = jnp.where(low, swap_halves(key), value).astype(bf16)
-        held[2 * pair, rows:] = jnp.where(half_low, upper, swap_halves(lower)).astype(bf16)
-        held[2 * pair + 1, rows:] = jnp.where(half_low, swap_halves(upper), lower).astype(bf16)
-    for k, out in enumerate(outs):
-        out[...] = held[jnp.bitwise_xor(me_ref[0], k)]
+        held_keys[2 * pair] = jnp.where(low, key, swap_halves(value)).astype(bf16)
+        held_keys[2 * pair + 1] = jnp.where(low, swap_halves(key), value).astype(bf16)
+        held_queries[2 * pair] = jnp.where(half_low, upper, swap_halves(lower)).astype(bf16)
+        held_queries[2 * pair + 1] = jnp.where(half_low, swap_halves(upper), lower).astype(bf16)
+    for k in range(H):
+        place = jnp.bitwise_xor(me_ref[0], k)
+        key_outs[k][...] = held_keys[place]
+        query_outs[k // TEAM][k % TEAM] = held_queries[place]
 
 
 def project_gating(tokens_ref, gating_weights, out_ref):
@@ -170,7 +173,7 @@
         out_shape=jax.ShapeDtypeStruct((steps * TEAM * rows, LANES), f32)
         if gives is None
         else jax.ShapeDtypeStruct(queries.shape, gives),
-        compiler_params=pltpu.CompilerParams(vmem_limit_bytes=40 << 20),
+        compiler_params=pltpu.CompilerParams(vmem_limit_bytes=24 << 20),
         cost_estimate=pl.CostEstimate(
             flops=steps * 2_000_000_000, bytes_accessed=4_000_000, transcendentals=4_000_000
         ),
@@ -235,13 +238,15 @@
     def seq_flip(array, bit):
         return lax.ppermute(array, "seq", [(s, s ^ bit) for s in range(seq_size)])
 
-    sent = pl.pallas_call(
+    *sent, queries_a, queries_b = pl.pallas_call(
         project,
-        out_shape=[jax.ShapeDtypeStruct((rows + half, LANES), bf16)] * H,
+        out_shape=[jax.ShapeDtypeStruct((rows, LANES), bf16)] * H
+        + [jax.ShapeDtypeStruct((TEAM, half, LANES), bf16)] * 2,
         grid=(1,),
         in_specs=[SMEM, VMEM] + [columns_of(width, i) for i in (1, 2, 3)],
-        out_specs=[VMEM] * H,
-        scratch_shapes=[pltpu.VMEM((H, rows + half, LANES), bf16)],
+        out_specs=[VMEM] * (H + 2),
+        scratch_shapes=[pltpu.VMEM((H, rows, LANES), bf16), pltpu.VMEM((H, half, LANES), bf16)],
+        compiler_params=pltpu.CompilerParams(vmem_limit_bytes=12 << 20),
         name="project",
     )(me_array, tokens, w_proj, w_proj, w_proj)
     gating = pl.pallas_call(
@@ -250,6 +255,7 @@
         grid=(1,),
         in_specs=[VMEM, columns_of(width, 0)],
         out_specs=VMEM,
+        compiler_params=pltpu.CompilerParams(vmem_limit_bytes=12 << 20),
         name="project_gating",
     )(tokens, w_proj)
 
@@ -261,9 +267,18 @@
         in_seq = (in_group * fold + places // head_size) * share + in_core
         return in_seq * head_size + places % head_size
 
+    def exchange(near, far):
+        got = [(near[0], far[0])]
+        for k in range(1, TEAM):
+            both = partner(jnp.stack([near[k], far[k]]), k)
+            got.append((both[0], both[1]))
+        return jnp.stack([pair[0] for pair in got] + [pair[1] for pair in got])
+
+    queries_b = partner(queries_b, TEAM)
     arrived = [partner(sent[k], k) for k in range(H)]
-    queries = jnp.stack([array[rows:] for array in arrived])
-    keys = jnp.stack([array[:rows] for array in arrived])
+    queries_a, queries_b, _ = lax.optimization_barrier((queries_a, queries_b, arrived[-1]))
+    queries = exchange(queries_a, queries_b)
+    keys = jnp.stack(arrived)
     first_places = jnp.arange(0, H, TEAM, dtype=jnp.int32)
     mine = blocks_of(asked, group, core)
     if groups == 2 and share == 2:
@@ -274,31 +289,39 @@
         def tables(query_blocks, in_group):
             return start, 1.0 / length, query_blocks, blocks_of(first_places, in_group, core), asked
 
-        totals = attend_call(
-            tables(jnp.concatenate([others, mine]), group),
-            jnp.concatenate([other_queries, queries]),
-            keys,
+        near_ours = attend_call(tables(mine, group), queries, keys)
+        near_theirs = attend_call(tables(others, group), other_queries, keys)
+        size = near_ours.shape[0] // 2
+        far_keys, near_theirs, near_ours, gating = lax.optimization_barrier(
+            (far_keys, near_theirs, near_ours, gating)
         )
-        size = totals.shape[0] // 2
-        far_keys, totals = lax.optimization_barrier((far_keys, totals))
         theirs = attend_call(
-            tables(others, 1 - group), other_queries, far_keys, totals[:size], bf16
+            tables(others, 1 - group), other_queries, far_keys, near_theirs, bf16
         )
         theirs = seq_flip(theirs, 1)
-        ours = attend_call(tables(mine, 1 - group), queries, far_keys, totals[size:], f32)
-        attention = (ours + theirs.astype(f32)).astype(bf16)
+        team_b = attend_call(
+            tables(mine[TEAM:], 1 - group), queries[TEAM:], far_keys, near_ours[size:], f32
+        )
+        attention_b = (team_b + theirs[TEAM:].astype(f32)).astype(bf16)
+        attention_b, totals_a = lax.optimization_barrier((attention_b, near_ours[:size]))
+        team_a = attend_call(
+            tables(mine[:TEAM], 1 - group), queries[:TEAM], far_keys, totals_a, f32
+        )
+        attention_a = (team_a + theirs[:TEAM].astype(f32)).astype(bf16)
     else:
         everything = lax.all_gather(keys, "seq", axis=0, tiled=True)
         index = jnp.arange(blocks, dtype=jnp.int32)
         slot = index // head_size * H + jnp.bitwise_xor(index % head_size, me)
         tables = (start, 1.0 / length, mine, index[::TEAM], slot)
         attention = attend_call(tables, queries, everything, gives=bf16)
-    returned = jnp.stack([partner(attention[k], k) for k in range(H)])
+        attention_a, attention_b = attention[:TEAM], attention[TEAM:]
+    returned = exchange(attention_a, partner(attention_b, TEAM))
     return pl.pallas_call(
         finish,
         out_shape=jax.ShapeDtypeStruct((rows, width), bf16),
         in_specs=[SMEM, VMEM, VMEM, VMEM, VMEM],
         out_specs=VMEM,
+        compiler_params=pltpu.CompilerParams(vmem_limit_bytes=12 << 20),
         name="finish",
     )(me_array, tokens, returned, gating, w_out)
 

time: 70.4 us -> 68.1 us (0.967); the launches traced: 70.3 us -> 67 us
  waiting for transfers between devices: 16.9 us -> 10.5 us
  local copies, waits for them, and re-layouts: 3.55 us -> 6.37 us
    ppermute x3, waiting for transfers between devices: 6.85 us -> 0.01 us  [seq_flip(): return lax.ppermute(array, 'seq', [(s, s ^ bit) for s in range(seq_size)])]
    pallas_call x3 -> x5, Pallas kernels: 15.2 us -> 20.6 us  [attend_call(): pl.pallas_call(functools.partial(attend, before is None, gives is not Non...]
    pallas_call x1, Pallas kernels: 3.32 us -> 1.05 us  [per_device(): pl.pallas_call(project, out_shape=[jax.ShapeDtypeStruct((rows, LANES), bf...]
    unnamed x32 -> x28, local copies, waits for them, and re-layouts: 3.35 us -> 5.26 us
    pallas_call x1, Pallas kernels: 2.31 us -> 0.5 us  [per_device(): pl.pallas_call(project_gating, out_shape=jax.ShapeDtypeStruct((rows, H *...]
    pallas_call x1, Pallas kernels: 2.67 us -> 1.42 us  [per_device(): pl.pallas_call(finish, out_shape=jax.ShapeDtypeStruct((rows, width), bf16...]
    another operation x3, local copies, waits for them, and re-layouts: 0.03 us -> 0.87 us  [the longest x1 0.85 us: per_device(): keys = jnp.stack(arrived)]
    ppermute x14 -> x15, waiting for transfers between devices: 10 us -> 10.5 us  [partner(): return lax.ppermute(array, ('seq', 'head'), pairs)]
  transfers between devices with their start and end apart: 17 -> 18, of which waited for: 5 -> 7; matrix products, arithmetic and copies ran while one was open for 5% -> 6% of each run, Pallas kernels for 19% -> 25%
where the time goes in v3:
time: 68.1 us; the launch traced here: 67 us
  starting transfers between devices  25.6 us (38%)
  Pallas kernels  23.6 us (35%)
  waiting for transfers between devices  10.5 us (15%)
  local copies, waits for them, and re-layouts  6.37 us (9%)
    ppermute x15, starting transfers between devices, partner(): return lax.ppermute(array, ('seq', 'head'), pairs)  24.9 us
    pallas_call x5, Pallas kernels, attend_call(): pl.pallas_call(functools.partial(attend, before is None, gives is not Non...  20.6 us
    ppermute x15, waiting for transfers between devices, partner(): return lax.ppermute(array, ('seq', 'head'), pairs)  10.5 us
    unnamed x28, local copies, waits for them, and re-layouts  5.26 us
    pallas_call x1, Pallas kernels, per_device(): pl.pallas_call(finish, out_shape=jax.ShapeDtypeStruct((rows, width), bf16...  1.42 us
  transfers between devices with their start and end apart: 18, of which 7 were waited for; matrix products, arithmetic and copies ran while one was open for 6% of the time, Pallas kernels for 25%

profile of v3, /device:TPU:4, one launch (start us, length us, event | category | flops | bytes accessed | tf_op | source)
XLA Modules:
  0.0 67.0 jit_solution(5686299062654376031)
XLA Ops:
  0.0 1.6 %copy-done = bf16[512,2048]{1,0:T(8,128)(2,1)S(1)} copy-done((bf16[512,2048]{1,0:T(8,128)(2,1)S(1)}, bf16[512,2048]{1,0:T(8,128)(2,1)}, u32[]{:S(2)}) %copy-start) | copy-done | bytes 2097176
  1.6 0.9 %copy-done.2 = bf16[256,512]{1,0:T(8,128)(2,1)S(1)} copy-done((bf16[256,512]{1,0:T(8,128)(2,1)S(1)}, bf16[256,512]{1,0:T(8,128)(2,1)}, u32[]{:S(2)}) %copy-start.2) | copy-done | bytes 262168
  2.5 1.0 %project.1 = (bf16[256,128]{1,0:T(8,128)(2,1)S(1)}, bf16[256,128]{1,0:T(8,128)(2,1)S(1)}, bf16[256,128]{1,0:T(8,128)(2,1)S(1)}, bf16[256,128]{1,0:T(8,128)(2,1)S...) custom-call(s32[1]{0:T(128)} %bitcast.me_ref, ...), custom_call_target="tpu_custom_call" | custom-call | tf_op jit(solution)/shard_map/project/pallas_call | solution.py:241
  3.6 1.6 %collective-permute-start = (bf16[4,128,128]{2,1,0:T(8,128)(2,1)S(1)}, bf16[4,128,128]{2,1,0:T(8,128)(2,1)S(1)}, u32[]{:S(2)}, u32[]{:S(2)}) collective-permute-start(bf16[4,128,128]{2,1,0:T(8,128)(2,1)S(1)} %get-tuple-element.24), channel_id=1, source_target_pairs={{0,8},{1,9},{2,10},{3,11},{4,12},{5,13},{6,14},{7,15},{8,0},{9,1},... | collective-permute-start | bytes 393224 | tf_op jit(solution)/shard_map/ppermute | solution.py:236
  5.2 3.6 %collective-permute-start.1 = (bf16[256,128]{1,0:T(8,128)(2,1)S(1)}, bf16[256,128]{1,0:T(8,128)(2,1)}, u32[]{:S(2)}, u32[]{:S(2)}) collective-permute-start(bf16[256,128]{1,0:T(8,128)(2,1)S(1)} %get-tuple-element.25), channel_id=1, source_target_pairs={{0,11},{1,10},{2,9},{3,8},{4,15},{5,14},{6,13},{7,12},{8,3},{9,2},... | collective-permute-start | bytes 196616 | tf_op jit(solution)/shard_map/ppermute | solution.py:236
  9.5 3.6 %collective-permute-start.7 = (bf16[256,128]{1,0:T(8,128)(2,1)S(1)}, bf16[256,128]{1,0:T(8,128)(2,1)}, u32[]{:S(2)}, u32[]{:S(2)}) collective-permute-start(bf16[256,128]{1,0:T(8,128)(2,1)S(1)} %get-tuple-element.31), channel_id=1, source_target_pairs={{0,3},{1,2},{2,1},{3,0},{4,7},{5,6},{6,5},{7,4},{8,11},{9,10},{10,... | collective-permute-start | bytes 196616 | tf_op jit(solution)/shard_map/ppermute | solution.py:236
  14.2 1.6 %collective-permute-start.8 = (bf16[256,128]{1,0:T(8,128)(2,1)S(1)}, bf16[256,128]{1,0:T(8,128)(2,1)S(1)}, u32[]{:S(2)}, u32[]{:S(2)}) collective-permute-start(bf16[256,128]{1,0:T(8,128)(2,1)S(1)} %get-tuple-element.32), channel_id=1, source_target_pairs={{0,8},{1,9},{2,10},{3,11},{4,12},{5,13},{6,14},{7,15},{8,0},{9,1},... | collective-permute-start | bytes 196616 | tf_op jit(solution)/shard_map/ppermute | solution.py:236
  17.9 3.0 %collective-permute-start.10 = (bf16[256,128]{1,0:T(8,128)(2,1)S(1)}, bf16[256,128]{1,0:T(8,128)(2,1)S(1)}, u32[]{:S(2)}, u32[]{:S(2)}) collective-permute-start(bf16[256,128]{1,0:T(8,128)(2,1)S(1)} %get-tuple-element.34), channel_id=1, source_target_pairs={{0,10},{1,11},{2,8},{3,9},{4,14},{5,15},{6,12},{7,13},{8,2},{9,3},... | collective-permute-start | bytes 196616 | tf_op jit(solution)/shard_map/ppermute | solution.py:236
  21.9 2.1 %collective-permute-done.10 = bf16[256,128]{1,0:T(8,128)(2,1)S(1)} collective-permute-done((bf16[256,128]{1,0:T(8,128)(2,1)S(1)}, bf16[256,128]{1,0:T(8,128)(2,1)S(1)}, u32[]{:S(2)}, u32[]{:S(2)}) %collective-permute-start.10) | collective-permute-done | bytes 65568 | tf_op jit(solution)/shard_map/ppermute | solution.py:236
  24.1 0.9 %bitcast_dynamic-update-slice_fusion.refs_0_ = bf16[8,256,128]{2,1,0:T(8,128)(2,1)S(1)} fusion(bf16[8,256,128]{2,1,0:T(8,128)(2,1)S(1)} %bitcast_dynamic-update-slice_fusion.1, bf16[256,128]{1,0:T(8,128)(2,1)} %collective-permute-done.1), kind=kLoop, calls=%fused_computation.10 | loop fusion | bytes 131072 | tf_op jit(solution)/shard_map/stack | solution.py:281
  25.5 2.5 %collective-permute-start.2 = (bf16[2,128,128]{2,1,0:T(8,128)(2,1)S(1)}, bf16[2,128,128]{2,1,0:T(8,128)(2,1)S(1)}, u32[]{:S(2)}, u32[]{:S(2)}) collective-permute-start(bf16[2,128,128]{2,1,0:T(8,128)(2,1)S(1)} %pad_maximum_fusion.2), channel_id=1, source_target_pairs={{0,1},{1,0},{2,3},{3,2},{4,5},{5,4},{6,7},{7,6},{8,9},{9,8},{10,11... | collective-permute-start | bytes 196616 | tf_op jit(solution)/shard_map/ppermute | solution.py:236
  28.7 1.8 %collective-permute-start.4 = (bf16[2,128,128]{2,1,0:T(8,128)(2,1)S(1)}, bf16[2,128,128]{2,1,0:T(8,128)(2,1)S(1)}, u32[]{:S(2)}, u32[]{:S(2)}) collective-permute-start(bf16[2,128,128]{2,1,0:T(8,128)(2,1)S(1)} %pad_maximum_fusion.4), channel_id=1, source_target_pairs={{0,3},{1,2},{2,1},{3,0},{4,7},{5,6},{6,5},{7,4},{8,11},{9,10},{10,... | collective-permute-start | bytes 196616 | tf_op jit(solution)/shard_map/ppermute | solution.py:236
  30.6 3.1 %collective-permute-done.3 = bf16[2,128,128]{2,1,0:T(8,128)(2,1)S(1)} collective-permute-done((bf16[2,128,128]{2,1,0:T(8,128)(2,1)S(1)}, bf16[2,128,128]{2,1,0:T(8,128)(2,1)S(1)}, u32[]{:S(2)}, u32[]{:S(2)}) %collective-permute-start.3) | collective-permute-done | bytes 65568 | tf_op jit(solution)/shard_map/ppermute | solution.py:236
  33.7 1.2 %collective-permute-done.4 = bf16[2,128,128]{2,1,0:T(8,128)(2,1)S(1)} collective-permute-done((bf16[2,128,128]{2,1,0:T(8,128)(2,1)S(1)}, bf16[2,128,128]{2,1,0:T(8,128)(2,1)S(1)}, u32[]{:S(2)}, u32[]{:S(2)}) %collective-permute-start.4) | collective-permute-done | bytes 65568 | tf_op jit(solution)/shard_map/ppermute | solution.py:236
  35.1 5.3 %attend.6 = f32[2048,128]{1,0:T(8,128)S(1)} custom-call(s32[64]{0:T(128)S(1)} %convert_reduce_fusion.1.start_ref, f32[64]{0:T(128)S(1)} %multiply_divide_fusion.inverse_ref, s32[8]{0:T(128)S(1)} %get-tuple-element.72.block_ref, s32[2]{0:T(128)S(1)} %multiply_add_fusion.team_ref, s32[8]{0:T(128)S(1)} %iota_xor_fusion.slot_ref, ...), custom_call_target="tpu_custom_call" | custom-call | flops 4000000000 | bytes 4000000 | tf_op jit(solution)/shard_map/attend/pallas_call | solution.py:159
  40.5 4.4 %attend.5.refs_1_ = f32[2048,128]{1,0:T(8,128)S(1)} custom-call(s32[64]{0:T(128)S(1)} %convert_reduce_fusion.1.start_ref, f32[64]{0:T(128)S(1)} %multiply_divide_fusion.inverse_ref, s32[8]{0:T(128)S(1)} %get-tuple-element.71.block_ref, s32[2]{0:T(128)S(1)} %multiply_add_fusion.team_ref, s32[8]{0:T(128)S(1)} %iota_xor_fusion.slot_ref, ...), custom_call_target="tpu_custom_call" | custom-call | flops 4000000000 | bytes 4000000 | tf_op jit(solution)/shard_map/attend/pallas_call | solution.py:159
  45.0 4.6 %attend.8 = bf16[8,128,128]{2,1,0:T(8,128)(2,1)S(1)} custom-call(s32[64]{0:T(128)S(1)} %convert_reduce_fusion.1.start_ref, f32[64]{0:T(128)S(1)} %multiply_divide_fusion.inverse_ref, s32[8]{0:T(128)S(1)} %get-tuple-element.71.block_ref, s32[2]{0:T(128)S(1)} %multiply_add_fusion.2.team_ref, s32[8]{0:T(128)S(1)} %iota_xor_fusion.slot_ref, ...), custom_call_target="tpu_custom_call" | custom-call | flops 4000000000 | bytes 4000000 | tf_op jit(solution)/shard_map/attend/pallas_call | solution.py:159
  49.7 3.0 %attend.7 = f32[4,128,128]{2,1,0:T(8,128)S(1)} custom-call(s32[64]{0:T(128)S(1)} %convert_reduce_fusion.1.start_ref, f32[64]{0:T(128)S(1)} %multiply_divide_fusion.inverse_ref, s32[4]{0:T(128)S(1)} %get-tuple-element.69.block_ref, s32[2]{0:T(128)S(1)} %multiply_add_fusion.2.team_ref, s32[8]{0:T(128)S(1)} %iota_xor_fusion.slot_ref, ...), custom_call_target="tpu_custom_call" | custom-call | flops 2000000000 | bytes 4000000 | tf_op jit(solution)/shard_map/attend/pallas_call | solution.py:159
  53.6 3.2 %attend.9 = f32[4,128,128]{2,1,0:T(8,128)S(1)} custom-call(s32[64]{0:T(128)S(1)} %convert_reduce_fusion.1.start_ref, f32[64]{0:T(128)S(1)} %multiply_divide_fusion.inverse_ref, s32[4]{0:T(128)S(1)} %get-tuple-element.70.block_ref, s32[2]{0:T(128)S(1)} %multiply_add_fusion.2.team_ref, s32[8]{0:T(128)S(1)} %iota_xor_fusion.slot_ref, ...), custom_call_target="tpu_custom_call" | custom-call | flops 2000000000 | bytes 4000000 | tf_op jit(solution)/shard_map/attend/pallas_call | solution.py:159
  56.9 0.9 %collective-permute-done.14 = bf16[4,128,128]{2,1,0:T(8,128)(2,1)S(1)} collective-permute-done((bf16[4,128,128]{2,1,0:T(8,128)(2,1)S(1)}, bf16[4,128,128]{2,1,0:T(8,128)(2,1)S(1)}, u32[]{:S(2)}, u32[]{:S(2)}) %collective-permute-start.14) | collective-permute-done | bytes 131104 | tf_op jit(solution)/shard_map/ppermute | solution.py:236
  57.9 1.8 %collective-permute-start.17 = (bf16[2,128,128]{2,1,0:T(8,128)(2,1)S(1)}, bf16[2,128,128]{2,1,0:T(8,128)(2,1)S(1)}, u32[]{:S(2)}, u32[]{:S(2)}) collective-permute-start(bf16[2,128,128]{2,1,0:T(8,128)(2,1)S(1)} %pad_maximum_fusion.7), channel_id=1, source_target_pairs={{0,3},{1,2},{2,1},{3,0},{4,7},{5,6},{6,5},{7,4},{8,11},{9,10},{10,... | collective-permute-start | bytes 196616 | tf_op jit(solution)/shard_map/ppermute | solution.py:236
  59.8 2.7 %collective-permute-start.16 = (bf16[2,128,128]{2,1,0:T(8,128)(2,1)S(1)}, bf16[2,128,128]{2,1,0:T(8,128)(2,1)S(1)}, u32[]{:S(2)}, u32[]{:S(2)}) collective-permute-start(bf16[2,128,128]{2,1,0:T(8,128)(2,1)S(1)} %pad_maximum_fusion.6), channel_id=1, source_target_pairs={{0,2},{1,3},{2,0},{3,1},{4,6},{5,7},{6,4},{7,5},{8,10},{9,11},{10,... | collective-permute-start | bytes 196616 | tf_op jit(solution)/shard_map/ppermute | solution.py:236
  62.4 3.0 %collective-permute-done.15 = bf16[2,128,128]{2,1,0:T(8,128)(2,1)S(1)} collective-permute-done((bf16[2,128,128]{2,1,0:T(8,128)(2,1)S(1)}, bf16[2,128,128]{2,1,0:T(8,128)(2,1)S(1)}, u32[]{:S(2)}, u32[]{:S(2)}) %collective-permute-start.15) | collective-permute-done | bytes 65568 | tf_op jit(solution)/shard_map/ppermute | solution.py:236
  65.6 1.4 %finish.1 = bf16[256,512]{1,0:T(8,128)(2,1)} custom-call(s32[1]{0:T(128)} %bitcast.me_ref, bf16[256,512]{1,0:T(8,128)(2,1)S(1)} %copy-done.3, bf16[8,128,128]{2,1,0:T(8,128)(2,1)S(1)} %constant_dynamic-update-slice_fusion.8.attention_ref, bf16[256,512]{1,0:T(8,128)(2,1)S(1)} %project_gating.1.gating_ref, bf16[512,512]{1,0:T(8,128)(2,1)S(1)} %copy-done.4), custom_call_target="tpu_custom_call" | custom-call | tf_op jit(solution)/shard_map/finish/pallas_call | solution.py:319
  (76 shorter events, 7.7 us)
Async XLA Ops:
  0.0 1.6 %copy-start = (bf16[512,2048]{1,0:T(8,128)(2,1)S(1)}, bf16[512,2048]{1,0:T(8,128)(2,1)}, u32[]{:S(2)}) copy-start(bf16[512,2048]{1,0:T(8,128)(2,1)} %gating_weights.1) | copy-start | bytes 6291460
  1.6 0.9 %copy-start.2 = (bf16[256,512]{1,0:T(8,128)(2,1)S(1)}, bf16[256,512]{1,0:T(8,128)(2,1)}, u32[]{:S(2)}) copy-start(bf16[256,512]{1,0:T(8,128)(2,1)} %tokens_ref.5) | copy-start | bytes 786436
  2.5 10.6 %copy-start.5 = (s32[64]{0:T(128)S(1)}, s32[64]{0:T(128)}, u32[]{:S(2)}) copy-start(s32[64]{0:T(128)} %param.7) | copy-start | bytes 772
  2.5 10.9 %copy-start.1 = (bf16[512,2048]{1,0:T(8,128)(2,1)S(1)}, bf16[512,2048]{1,0:T(8,128)(2,1)}, u32[]{:S(2)}) copy-start(bf16[512,2048]{1,0:T(8,128)(2,1)} %gating_weights.1) | copy-start | bytes 6291460
  2.5 11.0 %copy-start.3 = (bf16[256,512]{1,0:T(8,128)(2,1)S(1)}, bf16[256,512]{1,0:T(8,128)(2,1)}, u32[]{:S(2)}) copy-start(bf16[256,512]{1,0:T(8,128)(2,1)} %tokens_ref.5) | copy-start | bytes 786436
  3.6 21.9 %collective-permute-start = (bf16[4,128,128]{2,1,0:T(8,128)(2,1)S(1)}, bf16[4,128,128]{2,1,0:T(8,128)(2,1)S(1)}, u32[]{:S(2)}, u32[]{:S(2)}) collective-permute-start(bf16[4,128,128]{2,1,0:T(8,128)(2,1)S(1)} %get-tuple-element.24), channel_id=1, source_target_pairs={{0,8},{1,9},{2,10},{3,11},{4,12},{5,13},{6,14},{7,15},{8,0},{9,1},... | collective-permute-start | bytes 393224 | tf_op jit(solution)/shard_map/ppermute | solution.py:236
  5.2 18.9 %collective-permute-start.1 = (bf16[256,128]{1,0:T(8,128)(2,1)S(1)}, bf16[256,128]{1,0:T(8,128)(2,1)}, u32[]{:S(2)}, u32[]{:S(2)}) collective-permute-start(bf16[256,128]{1,0:T(8,128)(2,1)S(1)} %get-tuple-element.25), channel_id=1, source_target_pairs={{0,11},{1,10},{2,9},{3,8},{4,15},{5,14},{6,13},{7,12},{8,3},{9,2},... | collective-permute-start | bytes 196616 | tf_op jit(solution)/shard_map/ppermute | solution.py:236
  8.7 5.5 %collective-permute-start.5 = (bf16[256,128]{1,0:T(8,128)(2,1)S(1)}, bf16[256,128]{1,0:T(8,128)(2,1)}, u32[]{:S(2)}, u32[]{:S(2)}) collective-permute-start(bf16[256,128]{1,0:T(8,128)(2,1)S(1)} %get-tuple-element.29), channel_id=1, source_target_pairs={{0,1},{1,0},{2,3},{3,2},{4,5},{5,4},{6,7},{7,6},{8,9},{9,8},{10,11... | collective-permute-start | bytes 196616 | tf_op jit(solution)/shard_map/ppermute | solution.py:236
  8.7 7.9 %collective-permute-start.6 = (bf16[256,128]{1,0:T(8,128)(2,1)S(1)}, bf16[256,128]{1,0:T(8,128)(2,1)}, u32[]{:S(2)}, u32[]{:S(2)}) collective-permute-start(bf16[256,128]{1,0:T(8,128)(2,1)S(1)} %get-tuple-element.30), channel_id=1, source_target_pairs={{0,2},{1,3},{2,0},{3,1},{4,6},{5,7},{6,4},{7,5},{8,10},{9,11},{10,... | collective-permute-start | bytes 196616 | tf_op jit(solution)/shard_map/ppermute | solution.py:236
  9.5 8.4 %collective-permute-start.7 = (bf16[256,128]{1,0:T(8,128)(2,1)S(1)}, bf16[256,128]{1,0:T(8,128)(2,1)}, u32[]{:S(2)}, u32[]{:S(2)}) collective-permute-start(bf16[256,128]{1,0:T(8,128)(2,1)S(1)} %get-tuple-element.31), channel_id=1, source_target_pairs={{0,3},{1,2},{2,1},{3,0},{4,7},{5,6},{6,5},{7,4},{8,11},{9,10},{10,... | collective-permute-start | bytes 196616 | tf_op jit(solution)/shard_map/ppermute | solution.py:236
  14.2 7.6 %collective-permute-start.8 = (bf16[256,128]{1,0:T(8,128)(2,1)S(1)}, bf16[256,128]{1,0:T(8,128)(2,1)S(1)}, u32[]{:S(2)}, u32[]{:S(2)}) collective-permute-start(bf16[256,128]{1,0:T(8,128)(2,1)S(1)} %get-tuple-element.32), channel_id=1, source_target_pairs={{0,8},{1,9},{2,10},{3,11},{4,12},{5,13},{6,14},{7,15},{8,0},{9,1},... | collective-permute-start | bytes 196616 | tf_op jit(solution)/shard_map/ppermute | solution.py:236
  16.6 5.3 %collective-permute-start.9 = (bf16[256,128]{1,0:T(8,128)(2,1)S(1)}, bf16[256,128]{1,0:T(8,128)(2,1)S(1)}, u32[]{:S(2)}, u32[]{:S(2)}) collective-permute-start(bf16[256,128]{1,0:T(8,128)(2,1)S(1)} %get-tuple-element.33), channel_id=1, source_target_pairs={{0,9},{1,8},{2,11},{3,10},{4,13},{5,12},{6,15},{7,14},{8,1},{9,0},... | collective-permute-start | bytes 196616 | tf_op jit(solution)/shard_map/ppermute | solution.py:236
  17.9 6.1 %collective-permute-start.10 = (bf16[256,128]{1,0:T(8,128)(2,1)S(1)}, bf16[256,128]{1,0:T(8,128)(2,1)S(1)}, u32[]{:S(2)}, u32[]{:S(2)}) collective-permute-start(bf16[256,128]{1,0:T(8,128)(2,1)S(1)} %get-tuple-element.34), channel_id=1, source_target_pairs={{0,10},{1,11},{2,8},{3,9},{4,14},{5,15},{6,12},{7,13},{8,2},{9,3},... | collective-permute-start | bytes 196616 | tf_op jit(solution)/shard_map/ppermute | solution.py:236
  24.9 20.0 %collective-permute-start.11 = (bf16[8,256,128]{2,1,0:T(8,128)(2,1)S(1)}, bf16[8,256,128]{2,1,0:T(8,128)(2,1)S(1)}, u32[]{:S(2)}, u32[]{:S(2)}) collective-permute-start(bf16[8,256,128]{2,1,0:T(8,128)(2,1)S(1)} %bitcast_dynamic-update-slice_fusion.refs_0_), channel_id=1, source_target_pairs={{0,16},{4,20},{8,24},{12,28},{16,0},{20,4},{24,8},{28,12},{1,17},{... | collective-permute-start | bytes 1572872 | tf_op jit(solution)/shard_map/ppermute | solution.py:239
  25.5 5.1 %collective-permute-start.2 = (bf16[2,128,128]{2,1,0:T(8,128)(2,1)S(1)}, bf16[2,128,128]{2,1,0:T(8,128)(2,1)S(1)}, u32[]{:S(2)}, u32[]{:S(2)}) collective-permute-start(bf16[2,128,128]{2,1,0:T(8,128)(2,1)S(1)} %pad_maximum_fusion.2), channel_id=1, source_target_pairs={{0,1},{1,0},{2,3},{3,2},{4,5},{5,4},{6,7},{7,6},{8,9},{9,8},{10,11... | collective-permute-start | bytes 196616 | tf_op jit(solution)/shard_map/ppermute | solution.py:236
  28.0 5.7 %collective-permute-start.3 = (bf16[2,128,128]{2,1,0:T(8,128)(2,1)S(1)}, bf16[2,128,128]{2,1,0:T(8,128)(2,1)S(1)}, u32[]{:S(2)}, u32[]{:S(2)}) collective-permute-start(bf16[2,128,128]{2,1,0:T(8,128)(2,1)S(1)} %pad_maximum_fusion.3), channel_id=1, source_target_pairs={{0,2},{1,3},{2,0},{3,1},{4,6},{5,7},{6,4},{7,5},{8,10},{9,11},{10,... | collective-permute-start | bytes 196616 | tf_op jit(solution)/shard_map/ppermute | solution.py:236
  28.7 6.2 %collective-permute-start.4 = (bf16[2,128,128]{2,1,0:T(8,128)(2,1)S(1)}, bf16[2,128,128]{2,1,0:T(8,128)(2,1)S(1)}, u32[]{:S(2)}, u32[]{:S(2)}) collective-permute-start(bf16[2,128,128]{2,1,0:T(8,128)(2,1)S(1)} %pad_maximum_fusion.4), channel_id=1, source_target_pairs={{0,3},{1,2},{2,1},{3,0},{4,7},{5,6},{6,5},{7,4},{8,11},{9,10},{10,... | collective-permute-start | bytes 196616 | tf_op jit(solution)/shard_map/ppermute | solution.py:236
  35.0 5.5 %collective-permute-start.12 = (bf16[8,128,128]{2,1,0:T(8,128)(2,1)S(1)}, bf16[8,128,128]{2,1,0:T(8,128)(2,1)S(1)}, u32[]{:S(2)}, u32[]{:S(2)}) collective-permute-start(bf16[8,128,128]{2,1,0:T(8,128)(2,1)S(1)} %constant_dynamic-update-slice_fusion.queries_ref), channel_id=1, source_target_pairs={{0,4},{4,0},{8,12},{12,8},{16,20},{20,16},{24,28},{28,24},{1,5},{5... | collective-permute-start | bytes 786440 | tf_op jit(solution)/shard_map/ppermute | solution.py:239
  49.5 3.2 %collective-permute-start.13 = (bf16[8,128,128]{2,1,0:T(8,128)(2,1)S(1)}, bf16[8,128,128]{2,1,0:T(8,128)(2,1)S(1)}, u32[]{:S(2)}, u32[]{:S(2)}) collective-permute-start(bf16[8,128,128]{2,1,0:T(8,128)(2,1)S(1)} %attend.8), channel_id=1, source_target_pairs={{0,4},{4,0},{8,12},{12,8},{16,20},{20,16},{24,28},{28,24},{1,5},{5... | collective-permute-start | bytes 786440 | tf_op jit(solution)/shard_map/ppermute | solution.py:239
  52.8 5.0 %collective-permute-start.14 = (bf16[4,128,128]{2,1,0:T(8,128)(2,1)S(1)}, bf16[4,128,128]{2,1,0:T(8,128)(2,1)S(1)}, u32[]{:S(2)}, u32[]{:S(2)}) collective-permute-start(bf16[4,128,128]{2,1,0:T(8,128)(2,1)S(1)} %add_convert_fusion.1), channel_id=1, source_target_pairs={{0,8},{1,9},{2,10},{3,11},{4,12},{5,13},{6,14},{7,15},{8,0},{9,1},... | collective-permute-start | bytes 393224 | tf_op jit(solution)/shard_map/ppermute | solution.py:236
  56.9 8.7 %copy-start.4 = (bf16[512,512]{1,0:T(8,128)(2,1)S(1)}, bf16[512,512]{1,0:T(8,128)(2,1)}, u32[]{:S(2)}) copy-start(bf16[512,512]{1,0:T(8,128)(2,1)} %weights_ref.1) | copy-start | bytes 1572868
  57.9 7.6 %collective-permute-start.17 = (bf16[2,128,128]{2,1,0:T(8,128)(2,1)S(1)}, bf16[2,128,128]{2,1,0:T(8,128)(2,1)S(1)}, u32[]{:S(2)}, u32[]{:S(2)}) collective-permute-start(bf16[2,128,128]{2,1,0:T(8,128)(2,1)S(1)} %pad_maximum_fusion.7), channel_id=1, source_target_pairs={{0,3},{1,2},{2,1},{3,0},{4,7},{5,6},{6,5},{7,4},{8,11},{9,10},{10,... | collective-permute-start | bytes 196616 | tf_op jit(solution)/shard_map/ppermute | solution.py:236
  59.7 5.7 %collective-permute-start.15 = (bf16[2,128,128]{2,1,0:T(8,128)(2,1)S(1)}, bf16[2,128,128]{2,1,0:T(8,128)(2,1)S(1)}, u32[]{:S(2)}, u32[]{:S(2)}) collective-permute-start(bf16[2,128,128]{2,1,0:T(8,128)(2,1)S(1)} %pad_maximum_fusion.5), channel_id=1, source_target_pairs={{0,1},{1,0},{2,3},{3,2},{4,5},{5,4},{6,7},{7,6},{8,9},{9,8},{10,11... | collective-permute-start | bytes 196616 | tf_op jit(solution)/shard_map/ppermute | solution.py:236
  59.8 5.7 %collective-permute-start.16 = (bf16[2,128,128]{2,1,0:T(8,128)(2,1)S(1)}, bf16[2,128,128]{2,1,0:T(8,128)(2,1)S(1)}, u32[]{:S(2)}, u32[]{:S(2)}) collective-permute-start(bf16[2,128,128]{2,1,0:T(8,128)(2,1)S(1)} %pad_maximum_fusion.6), channel_id=1, source_target_pairs={{0,2},{1,3},{2,0},{3,1},{4,6},{5,7},{6,4},{7,5},{8,10},{9,11},{10,... | collective-permute-start | bytes 196616 | tf_op jit(solution)/shard_map/ppermute | solution.py:236

commit v4 on v2

--- a/solution.py
+++ b/solution.py
@@ -38,16 +38,28 @@
     return lax.broadcasted_iota(jnp.int32, (rows, LANES), 1) < DH
 
 
-def project(me_ref, tokens_ref, values_ref, queries_ref, keys_ref, *refs):
-    outs, held = refs[:-1], refs[-1]
-    rows = tokens_ref.shape[0]
+def project(me_ref, tokens_ref, weights_ref, *refs):
+    outs, (tokens, weights, held, sems) = refs[:-4], refs[-4:]
+    rows = tokens.shape[0]
     half = rows // 2
-    normed = layer_norm(tokens_ref[...].astype(f32)).astype(bf16)
+    copies = [pltpu.make_async_copy(tokens_ref, tokens, sems.at[0])]
+    for i, block in enumerate((3, 1, 2)):
+        at = pl.ds(block * H * DH, H * DH)
+        copies.append(
+            pltpu.make_async_copy(weights_ref.at[:, at], weights.at[i], sems.at[i + 1])
+        )
+    for copy in copies:
+        copy.start()
+    copies[0].wait()
+    normed = layer_norm(tokens[...].astype(f32)).astype(bf16)
     low, half_low = low_lanes(rows), low_lanes(half)
     scale = 0.5 * DH ** (-0.5)
-    keys = silu(jnp.dot(normed, keys_ref[...], preferred_element_type=f32))
-    values = silu(jnp.dot(normed, values_ref[...], preferred_element_type=f32))
-    queries = silu(jnp.dot(normed, queries_ref[...], preferred_element_type=f32)) * scale
+    copies[1].wait()
+    keys = silu(jnp.dot(normed, weights[0], preferred_element_type=f32))
+    copies[2].wait()
+    values = silu(jnp.dot(normed, weights[1], preferred_element_type=f32))
+    copies[3].wait()
+    queries = silu(jnp.dot(normed, weights[2], preferred_element_type=f32)) * scale
     for pair in range(H // 2):
         at = slice(pair * LANES, (pair + 1) * LANES)
         key, value, upper, lower = keys[:, at], values[:, at], queries[:half, at], queries[half:, at]
@@ -59,28 +71,28 @@
         out[...] = held[jnp.bitwise_xor(me_ref[0], k)]
 
 
-def project_gating(tokens_ref, gating_weights, out_ref):
-    normed = layer_norm(tokens_ref[...].astype(f32)).astype(bf16)
-    gating = silu(jnp.dot(normed, gating_weights[...], preferred_element_type=f32))
+def project_gating(tokens_ref, weights_ref, out_ref, tokens, weights, sems):
+    copies = [
+        pltpu.make_async_copy(tokens_ref, tokens, sems.at[0]),
+        pltpu.make_async_copy(weights_ref.at[:, pl.ds(0, H * DH)], weights, sems.at[1]),
+    ]
+    for copy in copies:
+        copy.start()
+    for copy in copies:
+        copy.wait()
+    normed = layer_norm(tokens[...].astype(f32)).astype(bf16)
+    gating = silu(jnp.dot(normed, weights[...], preferred_element_type=f32))
     out_ref[...] = gating.astype(bf16)
 
 
 def attend(
-    opens, closes, start_ref, inverse_ref, block_ref, team_ref, slot_ref, queries_ref, *refs
+    start_ref, inverse_ref, block_ref, team_ref, slot_ref, queries_ref, held, *refs
 ):
     step = pl.program_id(0)
-    held, total, queries, sem = refs[-4:]
-    out_ref, keys_ref = refs[-5], refs[0]
+    *before, out_ref, total, queries = refs
     rows = held.shape[1]
     half = rows // 2
     tiles = rows // TILE
-
-    @pl.when(step == 0)
-    def _():
-        copy = pltpu.make_async_copy(keys_ref, held, sem)
-        copy.start()
-        copy.wait()
-
     low = low_lanes(half)
     blocks = [block_ref[step * TEAM + i] for i in range(TEAM)]
     for i in range(TEAM):
@@ -90,13 +102,15 @@
             low, swap_halves(packed), 0.0
         ).astype(bf16)
     starts = [start_ref[block * tiles + j] for block in blocks for j in range(tiles)]
-    least, low_start, high_start = blocks[0], starts[0], starts[0]
+    least, low_start, high_start, high_first = blocks[0], starts[0], starts[0], starts[0]
     for block in blocks[1:]:
         least = jnp.minimum(least, block)
     for start in starts[1:]:
         low_start = jnp.minimum(low_start, start)
         high_start = jnp.maximum(high_start, start)
-    total[...] = jnp.zeros_like(total) if opens else refs[1][...]
+    for start in starts[tiles::tiles]:
+        high_first = jnp.maximum(high_first, start)
+    total[...] = jnp.zeros_like(total)
 
     def add(team, key_block, masked, chosen):
         key_rows = jnp.concatenate([held[slot_ref[team * TEAM + i]] for i in range(TEAM)], axis=0)
@@ -129,53 +143,54 @@
 
     def one_team(team, carry):
         key_block = team_ref[team]
-        before = (key_block < least) & ((key_block + TEAM) * tiles > low_start)
+        earlier = (key_block < least) & ((key_block + TEAM) * tiles > low_start)
         whole = key_block * tiles >= high_start
-        pl.when(before & whole)(lambda: add(team, key_block, False, False))
-        pl.when(before & ~whole)(lambda: add(team, key_block, True, True))
-        pl.when(key_block == least)(lambda: add(team, key_block, True, False))
+        every = (key_block + TEAM) * tiles > high_first
+        pl.when(earlier & whole)(lambda: add(team, key_block, False, False))
+        pl.when(earlier & ~every)(lambda: add(team, key_block, True, True))
+        pl.when((earlier & ~whole & every) | (key_block == least))(
+            lambda: add(team, key_block, True, False)
+        )
         return carry
 
     lax.fori_loop(0, held.shape[0] // TEAM, one_team, 0)
-    if not closes:
-        out_ref[...] = total[...]
-        return
     for i in range(TEAM):
         at = i * rows
         upper = total[at : at + half] * inverse_ref[blocks[i] * tiles]
         lower = total[at + half : at + rows] * inverse_ref[blocks[i] * tiles + tiles - 1]
-        out_ref[i] = jnp.where(low, swap_halves(upper), lower).astype(out_ref.dtype)
-
-
-def attend_call(tables, queries, keys, before=None, gives=None):
+        packed = jnp.where(low, swap_halves(upper), lower)
+        for more in before:
+            packed = packed + more[i].astype(f32)
+        out_ref[i] = packed.astype(out_ref.dtype)
+
+
+def attend_call(tables, queries, keys, gives, *before):
     half, rows = queries.shape[1], 2 * queries.shape[1]
     steps = queries.shape[0] // TEAM
-    totals = pl.BlockSpec((TEAM * rows, LANES), lambda i, *_: (i, 0))
     packed = pl.BlockSpec((TEAM, half, LANES), lambda i, *_: (i, 0, 0))
-    extra = [] if before is None else [before]
     return pl.pallas_call(
-        functools.partial(attend, before is None, gives is not None),
+        attend,
         grid_spec=pltpu.PrefetchScalarGridSpec(
             num_scalar_prefetch=5,
             grid=(steps,),
-            in_specs=[packed, ANY] + [totals] * len(extra),
-            out_specs=totals if gives is None else packed,
+            in_specs=[
+                packed,
+                pl.BlockSpec(keys.shape, lambda i, *_: (0, 0, 0), pipeline_mode=pl.Buffered(1)),
+            ]
+            + [packed] * len(before),
+            out_specs=packed,
             scratch_shapes=[
-                pltpu.VMEM(keys.shape, bf16),
                 pltpu.VMEM((TEAM * rows, LANES), f32),
                 pltpu.VMEM((TEAM * rows, LANES), bf16),
-                pltpu.SemaphoreType.DMA,
             ],
         ),
-        out_shape=jax.ShapeDtypeStruct((steps * TEAM * rows, LANES), f32)
-        if gives is None
-        else jax.ShapeDtypeStruct(queries.shape, gives),
-        compiler_params=pltpu.CompilerParams(vmem_limit_bytes=40 << 20),
+        out_shape=jax.ShapeDtypeStruct(queries.shape, gives),
+        compiler_params=pltpu.CompilerParams(vmem_limit_bytes=24 << 20),
         cost_estimate=pl.CostEstimate(
             flops=steps * 2_000_000_000, bytes_accessed=4_000_000, transcendentals=4_000_000
         ),
         name="attend",
-    )(*tables, queries, keys, *extra)
+    )(*tables, queries, keys, *before)
 
 
 def finish(me_ref, tokens_ref, attention_ref, gating_ref, weights_ref, out_ref):
@@ -200,11 +215,7 @@
 
 VMEM = pl.BlockSpec(memory_space=pltpu.VMEM)
 SMEM = pl.BlockSpec(memory_space=pltpu.SMEM)
-ANY = pl.BlockSpec(memory_space=pl.ANY)
-
-
-def columns_of(width, block):
-    return pl.BlockSpec((width, H * DH), lambda i: (0, block))
+HBM = pl.BlockSpec(memory_space=pltpu.HBM)
 
 
 def per_device(seq_size, head_size, tokens, w_proj, w_out, tile_user):
@@ -238,20 +249,31 @@
     sent = pl.pallas_call(
         project,
         out_shape=[jax.ShapeDtypeStruct((rows + half, LANES), bf16)] * H,
-        grid=(1,),
-        in_specs=[SMEM, VMEM] + [columns_of(width, i) for i in (1, 2, 3)],
+        in_specs=[SMEM, HBM, HBM],
         out_specs=[VMEM] * H,
-        scratch_shapes=[pltpu.VMEM((H, rows + half, LANES), bf16)],
+        scratch_shapes=[
+            pltpu.VMEM((rows, width), bf16),
+            pltpu.VMEM((3, width, H * DH), bf16),
+            pltpu.VMEM((H, rows + half, LANES), bf16),
+            pltpu.SemaphoreType.DMA((4,)),
+        ],
+        compiler_params=pltpu.CompilerParams(vmem_limit_bytes=58 << 20),
         name="project",
-    )(me_array, tokens, w_proj, w_proj, w_proj)
-    gating = pl.pallas_call(
-        project_gating,
-        out_shape=jax.ShapeDtypeStruct((rows, H * DH), bf16),
-        grid=(1,),
-        in_specs=[VMEM, columns_of(width, 0)],
-        out_specs=VMEM,
-        name="project_gating",
-    )(tokens, w_proj)
+    )(me_array, tokens, w_proj)
+    def gating_of(tokens):
+        return pl.pallas_call(
+            project_gating,
+            out_shape=jax.ShapeDtypeStruct((rows, H * DH), bf16),
+            in_specs=[HBM, HBM],
+            out_specs=VMEM,
+            scratch_shapes=[
+                pltpu.VMEM((rows, width), bf16),
+                pltpu.VMEM((width, H * DH), bf16),
+                pltpu.SemaphoreType.DMA((2,)),
+            ],
+            compiler_params=pltpu.CompilerParams(vmem_limit_bytes=12 << 20),
+            name="project_gating",
+        )(tokens, w_proj)
 
     start = jnp.sum((tile_user[None, :] < tile_user[:, None]).astype(jnp.int32), axis=1)
     length = jnp.sum((tile_user[None, :] == tile_user[:, None]).astype(f32), axis=1) * TILE
@@ -260,6 +282,13 @@
     def blocks_of(places, in_group, in_core):
         in_seq = (in_group * fold + places // head_size) * share + in_core
         return in_seq * head_size + places % head_size
+
+    def exchange(near, far):
+        got = [(near[0], far[0])]
+        for k in range(1, TEAM):
+            both = partner(jnp.stack([near[k], far[k]]), k)
+            got.append((both[0], both[1]))
+        return jnp.stack([pair[0] for pair in got] + [pair[1] for pair in got])
 
     arrived = [partner(sent[k], k) for k in range(H)]
     queries = jnp.stack([array[rows:] for array in arrived])
@@ -274,31 +303,39 @@
         def tables(query_blocks, in_group):
             return start, 1.0 / length, query_blocks, blocks_of(first_places, in_group, core), asked
 
-        totals = attend_call(
-            tables(jnp.concatenate([others, mine]), group),
-            jnp.concatenate([other_queries, queries]),
-            keys,
-        )
-        size = totals.shape[0] // 2
-        far_keys, totals = lax.optimization_barrier((far_keys, totals))
+        near_ours = attend_call(tables(mine, group), queries, keys, f32)
+        near_theirs = attend_call(tables(others, group), other_queries, keys, f32)
+        gating = gating_of(lax.optimization_barrier((tokens, near_theirs))[0])
+        far_keys, near_theirs, near_ours, gating = lax.optimization_barrier(
+            (far_keys, near_theirs, near_ours, gating)
+        )
         theirs = attend_call(
-            tables(others, 1 - group), other_queries, far_keys, totals[:size], bf16
+            tables(others, 1 - group), other_queries, far_keys, bf16, near_theirs
         )
         theirs = seq_flip(theirs, 1)
-        ours = attend_call(tables(mine, 1 - group), queries, far_keys, totals[size:], f32)
-        attention = (ours + theirs.astype(f32)).astype(bf16)
+        team_b = attend_call(
+            tables(mine[TEAM:], 1 - group), queries[TEAM:], far_keys, f32, near_ours[TEAM:]
+        )
+        attention_b = (team_b + theirs[TEAM:].astype(f32)).astype(bf16)
+        attention_b, near_a = lax.optimization_barrier((attention_b, near_ours[:TEAM]))
+        attention_a = attend_call(
+            tables(mine[:TEAM], 1 - group), queries[:TEAM], far_keys, bf16, near_a, theirs[:TEAM]
+        )
     else:
         everything = lax.all_gather(keys, "seq", axis=0, tiled=True)
         index = jnp.arange(blocks, dtype=jnp.int32)
         slot = index // head_size * H + jnp.bitwise_xor(index % head_size, me)
         tables = (start, 1.0 / length, mine, index[::TEAM], slot)
-        attention = attend_call(tables, queries, everything, gives=bf16)
-    returned = jnp.stack([partner(attention[k], k) for k in range(H)])
+        attention = attend_call(tables, queries, everything, bf16)
+        attention_a, attention_b = attention[:TEAM], attention[TEAM:]
+        gating = gating_of(tokens)
+    returned = exchange(attention_a, partner(attention_b, TEAM))
     return pl.pallas_call(
         finish,
         out_shape=jax.ShapeDtypeStruct((rows, width), bf16),
         in_specs=[SMEM, VMEM, VMEM, VMEM, VMEM],
         out_specs=VMEM,
+        compiler_params=pltpu.CompilerParams(vmem_limit_bytes=12 << 20),
         name="finish",
     )(me_array, tokens, returned, gating, w_out)
 

time: 70.4 us -> 62.6 us (0.89)
  starting transfers between devices: 25.5 us -> 18.6 us
  waiting for transfers between devices: 16.9 us -> 15.6 us
  Pallas kernels: 23.5 us -> 24.4 us
  local copies, waits for them, and re-layouts: 3.55 us -> 2.8 us
    ppermute x14 -> x11, starting transfers between devices: 24.8 us -> 18 us  [partner(): return lax.ppermute(array, ('seq', 'head'), pairs)]
    ppermute x3, waiting for transfers between devices: 6.85 us -> 2.82 us  [seq_flip(): return lax.ppermute(array, 'seq', [(s, s ^ bit) for s in range(seq_size)])]
    ppermute x14 -> x11, waiting for transfers between devices: 10 us -> 12.8 us  [partner(): return lax.ppermute(array, ('seq', 'head'), pairs)]
    pallas_call x4 -> x6, Pallas kernels: 17.5 us -> 19.8 us  [the longest x5 19.2 us: attend_call(): pl.pallas_call(attend, grid_spec=pltpu.PrefetchScalarGridSpec(num_scalar_...]
    unnamed x32 -> x28, local copies, waits for them, and re-layouts: 3.35 us -> 1.82 us
    pallas_call x1, Pallas kernels: 2.67 us -> 1.41 us  [per_device(): pl.pallas_call(finish, out_shape=jax.ShapeDtypeStruct((rows, width), bf16...]
    another operation x1 -> x9, local copies, waits for them, and re-layouts: 0.01 us -> 0.81 us  [per_device(): queries = jnp.stack([array[rows:] for array in arrived])]
  transfers between devices with their start and end apart: 17 -> 14, of which waited for: 5 -> 7; matrix products, arithmetic and copies ran while one was open for 5% -> 5% of each run, Pallas kernels for 19% -> 25%
where the time goes in v4:
time: 62.6 us; the launch traced here: 62.3 us
  Pallas kernels  24.4 us (39%)
  starting transfers between devices  18.6 us (30%)
  waiting for transfers between devices  15.6 us (25%)
  local copies, waits for them, and re-layouts  2.8 us (4%)
    pallas_call x5, Pallas kernels, attend_call(): pl.pallas_call(attend, grid_spec=pltpu.PrefetchScalarGridSpec(num_scalar_...  19.2 us
    ppermute x11, starting transfers between devices, partner(): return lax.ppermute(array, ('seq', 'head'), pairs)  18 us
    ppermute x11, waiting for transfers between devices, partner(): return lax.ppermute(array, ('seq', 'head'), pairs)  12.8 us
    pallas_call x1, Pallas kernels, per_device(): pl.pallas_call(project, out_shape=[jax.ShapeDtypeStruct((rows + half, LAN...  3.25 us
    ppermute x3, waiting for transfers between devices, seq_flip(): return lax.ppermute(array, 'seq', [(s, s ^ bit) for s in range(seq_size)])  2.82 us
    unnamed x28, local copies, waits for them, and re-layouts  1.82 us
    pallas_call x1, Pallas kernels, per_device(): pl.pallas_call(finish, out_shape=jax.ShapeDtypeStruct((rows, width), bf16...  1.41 us
  transfers between devices with their start and end apart: 14, of which 7 were waited for; matrix products, arithmetic and copies ran while one was open for 5% of the time, Pallas kernels for 25%

profile of v4, /device:TPU:4, one launch (start us, length us, event | category | flops | bytes accessed | tf_op | source)
XLA Modules:
  0.0 62.3 jit_solution(2513321100371815028)
XLA Ops:
  0.0 3.3 %project.1 = (bf16[384,128]{1,0:T(8,128)(2,1)}, bf16[384,128]{1,0:T(8,128)(2,1)}, bf16[384,128]{1,0:T(8,128)(2,1)}, bf16[384,128]{1,0:T(8,128)(2,1)}, bf16[384,1...) custom-call(s32[1]{0:T(128)} %bitcast.me_ref, ...), custom_call_target="tpu_custom_call" | custom-call | tf_op jit(solution)/shard_map/project/pallas_call | solution.py:249
  3.3 1.6 %collective-permute-start = (bf16[384,128]{1,0:T(8,128)(2,1)}, bf16[384,128]{1,0:T(8,128)(2,1)S(1)}, u32[]{:S(2)}, u32[]{:S(2)}) collective-permute-start(bf16[384,128]{1,0:T(8,128)(2,1)} %get-tuple-element.21), channel_id=1, source_target_pairs={{0,1},{1,0},{2,3},{3,2},{4,5},{5,4},{6,7},{7,6},{8,9},{9,8},{10,11... | collective-permute-start | bytes 294920 | tf_op jit(solution)/shard_map/ppermute | solution.py:244
  4.9 2.6 %collective-permute-start.1 = (bf16[384,128]{1,0:T(8,128)(2,1)}, bf16[384,128]{1,0:T(8,128)(2,1)S(1)}, u32[]{:S(2)}, u32[]{:S(2)}) collective-permute-start(bf16[384,128]{1,0:T(8,128)(2,1)} %get-tuple-element.22), channel_id=1, source_target_pairs={{0,2},{1,3},{2,0},{3,1},{4,6},{5,7},{6,4},{7,5},{8,10},{9,11},{10,... | collective-permute-start | bytes 294920 | tf_op jit(solution)/shard_map/ppermute | solution.py:244
  7.7 1.5 %collective-permute-start.3 = (bf16[384,128]{1,0:T(8,128)(2,1)}, bf16[384,128]{1,0:T(8,128)(2,1)S(1)}, u32[]{:S(2)}, u32[]{:S(2)}) collective-permute-start(bf16[384,128]{1,0:T(8,128)(2,1)} %get-tuple-element.24), channel_id=1, source_target_pairs={{0,8},{1,9},{2,10},{3,11},{4,12},{5,13},{6,14},{7,15},{8,0},{9,1},... | collective-permute-start | bytes 294920 | tf_op jit(solution)/shard_map/ppermute | solution.py:244
  10.2 0.8 %slice_bitcast_fusion.14 = bf16[1,128,128]{2,1,0:T(8,128)(2,1)S(1)} fusion(bf16[384,128]{1,0:T(8,128)(2,1)} %get-tuple-element.20), kind=kLoop, calls=%fused_computation.44 | loop fusion | bytes 65536 | tf_op jit(solution)/shard_map/stack | solution.py:294
  11.0 0.8 %constant_dynamic-update-slice_fusion.7 = bf16[8,128,128]{2,1,0:T(8,128)(2,1)S(1)} fusion(bf16[384,128]{1,0:T(8,128)(2,1)} %get-tuple-element.20), kind=kLoop, calls=%fused_computation.28 | loop fusion | bytes 65536
  11.8 0.8 %bitcast_dynamic-update-slice_fusion = bf16[8,256,128]{2,1,0:T(8,128)(2,1)S(1)} fusion(bf16[384,128]{1,0:T(8,128)(2,1)} %get-tuple-element.20), kind=kLoop, calls=%fused_computation.20 | loop fusion | bytes 131072
  12.7 4.5 %collective-permute-start.5 = (bf16[384,128]{1,0:T(8,128)(2,1)}, bf16[384,128]{1,0:T(8,128)(2,1)S(1)}, u32[]{:S(2)}, u32[]{:S(2)}) collective-permute-start(bf16[384,128]{1,0:T(8,128)(2,1)} %get-tuple-element.26), channel_id=1, source_target_pairs={{0,10},{1,11},{2,8},{3,9},{4,14},{5,15},{6,12},{7,13},{8,2},{9,3},... | collective-permute-start | bytes 294920 | tf_op jit(solution)/shard_map/ppermute | solution.py:244
  17.2 1.7 %collective-permute-start.6 = (bf16[384,128]{1,0:T(8,128)(2,1)}, bf16[384,128]{1,0:T(8,128)(2,1)S(1)}, u32[]{:S(2)}, u32[]{:S(2)}) collective-permute-start(bf16[384,128]{1,0:T(8,128)(2,1)} %get-tuple-element.27), channel_id=1, source_target_pairs={{0,11},{1,10},{2,9},{3,8},{4,15},{5,14},{6,13},{7,12},{8,3},{9,2},... | collective-permute-start | bytes 294920 | tf_op jit(solution)/shard_map/ppermute | solution.py:244
  19.0 4.5 %collective-permute-done.5 = bf16[384,128]{1,0:T(8,128)(2,1)S(1)} collective-permute-done((bf16[384,128]{1,0:T(8,128)(2,1)}, bf16[384,128]{1,0:T(8,128)(2,1)S(1)}, u32[]{:S(2)}, u32[]{:S(2)}) %collective-permute-start.5) | collective-permute-done | bytes 98336 | tf_op jit(solution)/shard_map/ppermute | solution.py:244
  23.5 1.4 %collective-permute-done.6 = bf16[384,128]{1,0:T(8,128)(2,1)S(1)} collective-permute-done((bf16[384,128]{1,0:T(8,128)(2,1)}, bf16[384,128]{1,0:T(8,128)(2,1)S(1)}, u32[]{:S(2)}, u32[]{:S(2)}) %collective-permute-start.6) | collective-permute-done | bytes 98336 | tf_op jit(solution)/shard_map/ppermute | solution.py:244
  25.7 5.5 %attend.6 = f32[8,128,128]{2,1,0:T(8,128)S(1)} custom-call(s32[64]{0:T(128)S(1)} %convert_reduce_fusion.1.start_ref, f32[64]{0:T(128)S(1)} %multiply_divide_fusion.inverse_ref, s32[8]{0:T(128)S(1)} %get-tuple-element.47.block_ref, s32[2]{0:T(128)S(1)} %multiply_add_fusion.team_ref, s32[8]{0:T(128)S(1)} %iota_xor_fusion.slot_ref, ...), custom_call_target="tpu_custom_call" | custom-call | flops 4000000000 | bytes 4000000 | tf_op jit(solution)/shard_map/attend/pallas_call | solution.py:171
  31.4 4.6 %attend.5.refs_0_ = f32[8,128,128]{2,1,0:T(8,128)S(1)} custom-call(s32[64]{0:T(128)S(1)} %convert_reduce_fusion.1.start_ref, f32[64]{0:T(128)S(1)} %multiply_divide_fusion.inverse_ref, s32[8]{0:T(128)S(1)} %get-tuple-element.46.block_ref, s32[2]{0:T(128)S(1)} %multiply_add_fusion.team_ref, s32[8]{0:T(128)S(1)} %iota_xor_fusion.slot_ref, ...), custom_call_target="tpu_custom_call" | custom-call | flops 4000000000 | bytes 4000000 | tf_op jit(solution)/shard_map/attend/pallas_call | solution.py:171
  36.7 2.8 %collective-permute-done.7.held = bf16[8,256,128]{2,1,0:T(8,128)(2,1)S(1)} collective-permute-done((bf16[8,256,128]{2,1,0:T(8,128)(2,1)S(1)}, bf16[8,256,128]{2,1,0:T(8,128)(2,1)S(1)}, u32[]{:S(2)}, u32[]{:S(2)}) %collective-permute-start.7) | collective-permute-done | bytes 524320 | tf_op jit(solution)/shard_map/ppermute | solution.py:247
  39.5 4.0 %attend.8 = bf16[8,128,128]{2,1,0:T(8,128)(2,1)S(1)} custom-call(s32[64]{0:T(128)S(1)} %convert_reduce_fusion.1.start_ref, f32[64]{0:T(128)S(1)} %multiply_divide_fusion.inverse_ref, s32[8]{0:T(128)S(1)} %get-tuple-element.46.block_ref, s32[2]{0:T(128)S(1)} %multiply_add_fusion.2.team_ref, s32[8]{0:T(128)S(1)} %iota_xor_fusion.slot_ref, ...), custom_call_target="tpu_custom_call" | custom-call | flops 4000000000 | bytes 4000000 | tf_op jit(solution)/shard_map/attend/pallas_call | solution.py:171
  43.6 2.4 %attend.7 = f32[4,128,128]{2,1,0:T(8,128)S(1)} custom-call(s32[64]{0:T(128)S(1)} %convert_reduce_fusion.1.start_ref, f32[64]{0:T(128)S(1)} %multiply_divide_fusion.inverse_ref, s32[4]{0:T(128)S(1)} %get-tuple-element.44.block_ref, s32[2]{0:T(128)S(1)} %multiply_add_fusion.2.team_ref, s32[8]{0:T(128)S(1)} %iota_xor_fusion.slot_ref, ...), custom_call_target="tpu_custom_call" | custom-call | flops 2000000000 | bytes 4000000 | tf_op jit(solution)/shard_map/attend/pallas_call | solution.py:171
  46.7 2.6 %attend.9 = bf16[4,128,128]{2,1,0:T(8,128)(2,1)S(1)} custom-call(s32[64]{0:T(128)S(1)} %convert_reduce_fusion.1.start_ref, f32[64]{0:T(128)S(1)} %multiply_divide_fusion.inverse_ref, s32[4]{0:T(128)S(1)} %get-tuple-element.45.block_ref, s32[2]{0:T(128)S(1)} %multiply_add_fusion.2.team_ref, s32[8]{0:T(128)S(1)} %iota_xor_fusion.slot_ref, ...), custom_call_target="tpu_custom_call" | custom-call | flops 2000000000 | bytes 4000000 | tf_op jit(solution)/shard_map/attend/pallas_call | solution.py:171
  49.3 2.2 %collective-permute-done.10 = bf16[4,128,128]{2,1,0:T(8,128)(2,1)S(1)} collective-permute-done((bf16[4,128,128]{2,1,0:T(8,128)(2,1)S(1)}, bf16[4,128,128]{2,1,0:T(8,128)(2,1)S(1)}, u32[]{:S(2)}, u32[]{:S(2)}) %collective-permute-start.10) | collective-permute-done | bytes 131104 | tf_op jit(solution)/shard_map/ppermute | solution.py:244
  51.6 1.6 %collective-permute-start.11 = (bf16[2,128,128]{2,1,0:T(8,128)(2,1)S(1)}, bf16[2,128,128]{2,1,0:T(8,128)(2,1)S(1)}, u32[]{:S(2)}, u32[]{:S(2)}) collective-permute-start(bf16[2,128,128]{2,1,0:T(8,128)(2,1)S(1)} %pad_maximum_fusion.2), channel_id=1, source_target_pairs={{0,1},{1,0},{2,3},{3,2},{4,5},{5,4},{6,7},{7,6},{8,9},{9,8},{10,11... | collective-permute-start | bytes 196616 | tf_op jit(solution)/shard_map/ppermute | solution.py:244
  53.2 1.4 %collective-permute-start.12 = (bf16[2,128,128]{2,1,0:T(8,128)(2,1)S(1)}, bf16[2,128,128]{2,1,0:T(8,128)(2,1)S(1)}, u32[]{:S(2)}, u32[]{:S(2)}) collective-permute-start(bf16[2,128,128]{2,1,0:T(8,128)(2,1)S(1)} %pad_maximum_fusion.3), channel_id=1, source_target_pairs={{0,2},{1,3},{2,0},{3,1},{4,6},{5,7},{6,4},{7,5},{8,10},{9,11},{10,... | collective-permute-start | bytes 196616 | tf_op jit(solution)/shard_map/ppermute | solution.py:244
  54.6 1.6 %collective-permute-start.13 = (bf16[2,128,128]{2,1,0:T(8,128)(2,1)S(1)}, bf16[2,128,128]{2,1,0:T(8,128)(2,1)S(1)}, u32[]{:S(2)}, u32[]{:S(2)}) collective-permute-start(bf16[2,128,128]{2,1,0:T(8,128)(2,1)S(1)} %pad_maximum_fusion.4), channel_id=1, source_target_pairs={{0,3},{1,2},{2,1},{3,0},{4,7},{5,6},{6,5},{7,4},{8,11},{9,10},{10,... | collective-permute-start | bytes 196616 | tf_op jit(solution)/shard_map/ppermute | solution.py:244
  56.5 3.4 %collective-permute-done.12 = bf16[2,128,128]{2,1,0:T(8,128)(2,1)S(1)} collective-permute-done((bf16[2,128,128]{2,1,0:T(8,128)(2,1)S(1)}, bf16[2,128,128]{2,1,0:T(8,128)(2,1)S(1)}, u32[]{:S(2)}, u32[]{:S(2)}) %collective-permute-start.12) | collective-permute-done | bytes 65568 | tf_op jit(solution)/shard_map/ppermute | solution.py:244
  59.9 0.9 %collective-permute-done.13 = bf16[2,128,128]{2,1,0:T(8,128)(2,1)S(1)} collective-permute-done((bf16[2,128,128]{2,1,0:T(8,128)(2,1)S(1)}, bf16[2,128,128]{2,1,0:T(8,128)(2,1)S(1)}, u32[]{:S(2)}, u32[]{:S(2)}) %collective-permute-start.13) | collective-permute-done | bytes 65568 | tf_op jit(solution)/shard_map/ppermute | solution.py:244
  60.9 1.4 %finish.1 = bf16[256,512]{1,0:T(8,128)(2,1)} custom-call(s32[1]{0:T(128)} %bitcast.me_ref, bf16[256,512]{1,0:T(8,128)(2,1)S(1)} %copy-done.1, bf16[8,128,128]{2,1,0:T(8,128)(2,1)S(1)} %constant_dynamic-update-slice_fusion.8.attention_ref, bf16[256,512]{1,0:T(8,128)(2,1)S(1)} %project_gating.1.gating_ref, bf16[512,512]{1,0:T(8,128)(2,1)S(1)} %copy-done.2), custom_call_target="tpu_custom_call" | custom-call | tf_op jit(solution)/shard_map/finish/pallas_call | solution.py:333
  (69 shorter events, 4.0 us)
Async XLA Ops:
  0.0 9.9 %copy-start.3 = (s32[64]{0:T(128)S(1)}, s32[64]{0:T(128)}, u32[]{:S(2)}) copy-start(s32[64]{0:T(128)} %param.7) | copy-start | bytes 772
  3.3 9.5 %collective-permute-start = (bf16[384,128]{1,0:T(8,128)(2,1)}, bf16[384,128]{1,0:T(8,128)(2,1)S(1)}, u32[]{:S(2)}, u32[]{:S(2)}) collective-permute-start(bf16[384,128]{1,0:T(8,128)(2,1)} %get-tuple-element.21), channel_id=1, source_target_pairs={{0,1},{1,0},{2,3},{3,2},{4,5},{5,4},{6,7},{7,6},{8,9},{9,8},{10,11... | collective-permute-start | bytes 294920 | tf_op jit(solution)/shard_map/ppermute | solution.py:244
  4.9 12.3 %collective-permute-start.1 = (bf16[384,128]{1,0:T(8,128)(2,1)}, bf16[384,128]{1,0:T(8,128)(2,1)S(1)}, u32[]{:S(2)}, u32[]{:S(2)}) collective-permute-start(bf16[384,128]{1,0:T(8,128)(2,1)} %get-tuple-element.22), channel_id=1, source_target_pairs={{0,2},{1,3},{2,0},{3,1},{4,6},{5,7},{6,4},{7,5},{8,10},{9,11},{10,... | collective-permute-start | bytes 294920 | tf_op jit(solution)/shard_map/ppermute | solution.py:244
  7.5 11.5 %collective-permute-start.2 = (bf16[384,128]{1,0:T(8,128)(2,1)}, bf16[384,128]{1,0:T(8,128)(2,1)S(1)}, u32[]{:S(2)}, u32[]{:S(2)}) collective-permute-start(bf16[384,128]{1,0:T(8,128)(2,1)} %get-tuple-element.23), channel_id=1, source_target_pairs={{0,3},{1,2},{2,1},{3,0},{4,7},{5,6},{6,5},{7,4},{8,11},{9,10},{10,... | collective-permute-start | bytes 294920 | tf_op jit(solution)/shard_map/ppermute | solution.py:244
  7.7 11.3 %collective-permute-start.3 = (bf16[384,128]{1,0:T(8,128)(2,1)}, bf16[384,128]{1,0:T(8,128)(2,1)S(1)}, u32[]{:S(2)}, u32[]{:S(2)}) collective-permute-start(bf16[384,128]{1,0:T(8,128)(2,1)} %get-tuple-element.24), channel_id=1, source_target_pairs={{0,8},{1,9},{2,10},{3,11},{4,12},{5,13},{6,14},{7,15},{8,0},{9,1},... | collective-permute-start | bytes 294920 | tf_op jit(solution)/shard_map/ppermute | solution.py:244
  9.2 9.8 %collective-permute-start.4 = (bf16[384,128]{1,0:T(8,128)(2,1)}, bf16[384,128]{1,0:T(8,128)(2,1)S(1)}, u32[]{:S(2)}, u32[]{:S(2)}) collective-permute-start(bf16[384,128]{1,0:T(8,128)(2,1)} %get-tuple-element.25), channel_id=1, source_target_pairs={{0,9},{1,8},{2,11},{3,10},{4,13},{5,12},{6,15},{7,14},{8,1},{9,0},... | collective-permute-start | bytes 294920 | tf_op jit(solution)/shard_map/ppermute | solution.py:244
  12.7 10.8 %collective-permute-start.5 = (bf16[384,128]{1,0:T(8,128)(2,1)}, bf16[384,128]{1,0:T(8,128)(2,1)S(1)}, u32[]{:S(2)}, u32[]{:S(2)}) collective-permute-start(bf16[384,128]{1,0:T(8,128)(2,1)} %get-tuple-element.26), channel_id=1, source_target_pairs={{0,10},{1,11},{2,8},{3,9},{4,14},{5,15},{6,12},{7,13},{8,2},{9,3},... | collective-permute-start | bytes 294920 | tf_op jit(solution)/shard_map/ppermute | solution.py:244
  17.2 7.7 %collective-permute-start.6 = (bf16[384,128]{1,0:T(8,128)(2,1)}, bf16[384,128]{1,0:T(8,128)(2,1)S(1)}, u32[]{:S(2)}, u32[]{:S(2)}) collective-permute-start(bf16[384,128]{1,0:T(8,128)(2,1)} %get-tuple-element.27), channel_id=1, source_target_pairs={{0,11},{1,10},{2,9},{3,8},{4,15},{5,14},{6,13},{7,12},{8,3},{9,2},... | collective-permute-start | bytes 294920 | tf_op jit(solution)/shard_map/ppermute | solution.py:244
  24.9 6.4 %collective-permute-start.8 = (bf16[8,128,128]{2,1,0:T(8,128)(2,1)S(1)}, bf16[8,128,128]{2,1,0:T(8,128)(2,1)S(1)}, u32[]{:S(2)}, u32[]{:S(2)}) collective-permute-start(bf16[8,128,128]{2,1,0:T(8,128)(2,1)S(1)} %constant_dynamic-update-slice_fusion.queries_ref), channel_id=1, source_target_pairs={{0,4},{4,0},{8,12},{12,8},{16,20},{20,16},{24,28},{28,24},{1,5},{5... | collective-permute-start | bytes 786440 | tf_op jit(solution)/shard_map/ppermute | solution.py:247
  25.1 14.4 %collective-permute-start.7 = (bf16[8,256,128]{2,1,0:T(8,128)(2,1)S(1)}, bf16[8,256,128]{2,1,0:T(8,128)(2,1)S(1)}, u32[]{:S(2)}, u32[]{:S(2)}) collective-permute-start(bf16[8,256,128]{2,1,0:T(8,128)(2,1)S(1)} %fusion.held), channel_id=1, source_target_pairs={{0,16},{4,20},{8,24},{12,28},{16,0},{20,4},{24,8},{28,12},{1,17},{... | collective-permute-start | bytes 1572872 | tf_op jit(solution)/shard_map/ppermute | solution.py:247
  31.3 4.7 %copy-start = (bf16[512,2048]{1,0:T(8,128)(2,1)S(1)}, bf16[512,2048]{1,0:T(8,128)(2,1)}, u32[]{:S(2)}) copy-start(bf16[512,2048]{1,0:T(8,128)(2,1)} %weights_ref.4) | copy-start | bytes 6291460
  31.4 4.7 %copy-start.1 = (bf16[256,512]{1,0:T(8,128)(2,1)S(1)}, bf16[256,512]{1,0:T(8,128)(2,1)}, u32[]{:S(2)}) copy-start(bf16[256,512]{1,0:T(8,128)(2,1)} %tokens_ref.4) | copy-start | bytes 786436
  43.5 2.5 %collective-permute-start.9 = (bf16[8,128,128]{2,1,0:T(8,128)(2,1)S(1)}, bf16[8,128,128]{2,1,0:T(8,128)(2,1)S(1)}, u32[]{:S(2)}, u32[]{:S(2)}) collective-permute-start(bf16[8,128,128]{2,1,0:T(8,128)(2,1)S(1)} %attend.8), channel_id=1, source_target_pairs={{0,4},{4,0},{8,12},{12,8},{16,20},{20,16},{24,28},{28,24},{1,5},{5... | collective-permute-start | bytes 786440 | tf_op jit(solution)/shard_map/ppermute | solution.py:247
  46.1 5.5 %collective-permute-start.10 = (bf16[4,128,128]{2,1,0:T(8,128)(2,1)S(1)}, bf16[4,128,128]{2,1,0:T(8,128)(2,1)S(1)}, u32[]{:S(2)}, u32[]{:S(2)}) collective-permute-start(bf16[4,128,128]{2,1,0:T(8,128)(2,1)S(1)} %add_convert_fusion), channel_id=1, source_target_pairs={{0,8},{1,9},{2,10},{3,11},{4,12},{5,13},{6,14},{7,15},{8,0},{9,1},... | collective-permute-start | bytes 393224 | tf_op jit(solution)/shard_map/ppermute | solution.py:244
  46.7 14.2 %copy-start.2 = (bf16[512,512]{1,0:T(8,128)(2,1)S(1)}, bf16[512,512]{1,0:T(8,128)(2,1)}, u32[]{:S(2)}) copy-start(bf16[512,512]{1,0:T(8,128)(2,1)} %weights_ref.5) | copy-start | bytes 1572868
  51.6 4.9 %collective-permute-start.11 = (bf16[2,128,128]{2,1,0:T(8,128)(2,1)S(1)}, bf16[2,128,128]{2,1,0:T(8,128)(2,1)S(1)}, u32[]{:S(2)}, u32[]{:S(2)}) collective-permute-start(bf16[2,128,128]{2,1,0:T(8,128)(2,1)S(1)} %pad_maximum_fusion.2), channel_id=1, source_target_pairs={{0,1},{1,0},{2,3},{3,2},{4,5},{5,4},{6,7},{7,6},{8,9},{9,8},{10,11... | collective-permute-start | bytes 196616 | tf_op jit(solution)/shard_map/ppermute | solution.py:244
  53.2 6.7 %collective-permute-start.12 = (bf16[2,128,128]{2,1,0:T(8,128)(2,1)S(1)}, bf16[2,128,128]{2,1,0:T(8,128)(2,1)S(1)}, u32[]{:S(2)}, u32[]{:S(2)}) collective-permute-start(bf16[2,128,128]{2,1,0:T(8,128)(2,1)S(1)} %pad_maximum_fusion.3), channel_id=1, source_target_pairs={{0,2},{1,3},{2,0},{3,1},{4,6},{5,7},{6,4},{7,5},{8,10},{9,11},{10,... | collective-permute-start | bytes 196616 | tf_op jit(solution)/shard_map/ppermute | solution.py:244
  54.6 6.2 %collective-permute-start.13 = (bf16[2,128,128]{2,1,0:T(8,128)(2,1)S(1)}, bf16[2,128,128]{2,1,0:T(8,128)(2,1)S(1)}, u32[]{:S(2)}, u32[]{:S(2)}) collective-permute-start(bf16[2,128,128]{2,1,0:T(8,128)(2,1)S(1)} %pad_maximum_fusion.4), channel_id=1, source_target_pairs={{0,3},{1,2},{2,1},{3,0},{4,7},{5,6},{6,5},{7,4},{8,11},{9,10},{10,... | collective-permute-start | bytes 196616 | tf_op jit(solution)/shard_map/ppermute | solution.py:244

commit v5 on v4

--- a/solution.py
+++ b/solution.py
@@ -290,18 +290,28 @@
             got.append((both[0], both[1]))
         return jnp.stack([pair[0] for pair in got] + [pair[1] for pair in got])
 
-    arrived = [partner(sent[k], k) for k in range(H)]
-    queries = jnp.stack([array[rows:] for array in arrived])
-    keys = jnp.stack([array[:rows] for array in arrived])
+    order = [0, 1, 5, 4, 2, 3, 6, 7]
+    place_of = jnp.array([order.index(k) for k in range(H)], jnp.int32)
+    arrived = {0: sent[0]}
+    for k in order[1:-2]:
+        arrived[k] = partner(sent[k], k)
+    first_lot = jnp.stack([arrived[k][:rows] for k in order[:TEAM]])
+    *held_back, first_lot = lax.optimization_barrier((sent[order[-2]], sent[order[-1]], first_lot))
+    for k, array in zip(order[-2:], held_back):
+        arrived[k] = partner(array, k)
+    queries = jnp.stack([arrived[k][rows:] for k in range(H)])
+    lots = [first_lot, jnp.stack([arrived[k][:rows] for k in order[TEAM:]])]
+    keys = jnp.concatenate(lots)
     first_places = jnp.arange(0, H, TEAM, dtype=jnp.int32)
     mine = blocks_of(asked, group, core)
     if groups == 2 and share == 2:
-        far_keys = seq_flip(keys, fold * share)
+        far_keys = jnp.concatenate([seq_flip(lot, fold * share) for lot in lots])
         other_queries = seq_flip(queries, 1)
         others = blocks_of(asked, group, 1 - core)
 
         def tables(query_blocks, in_group):
-            return start, 1.0 / length, query_blocks, blocks_of(first_places, in_group, core), asked
+            teams = blocks_of(first_places, in_group, core)
+            return start, 1.0 / length, query_blocks, teams, place_of[asked]
 
         near_ours = attend_call(tables(mine, group), queries, keys, f32)
         near_theirs = attend_call(tables(others, group), other_queries, keys, f32)
@@ -324,7 +334,7 @@
     else:
         everything = lax.all_gather(keys, "seq", axis=0, tiled=True)
         index = jnp.arange(blocks, dtype=jnp.int32)
-        slot = index // head_size * H + jnp.bitwise_xor(index % head_size, me)
+        slot = index // head_size * H + place_of[jnp.bitwise_xor(index % head_size, me)]
         tables = (start, 1.0 / length, mine, index[::TEAM], slot)
         attention = attend_call(tables, queries, everything, bf16)
         attention_a, attention_b = attention[:TEAM], attention[TEAM:]

time: 62.6 us -> 60 us (0.958)
  waiting for transfers between devices: 15.6 us -> 12.7 us
  starting transfers between devices: 18.6 us -> 21.1 us
  Pallas kernels: 24.4 us -> 22 us
  local copies, waits for them, and re-layouts: 2.8 us -> 3.45 us
    pallas_call x5, Pallas kernels: 19.2 us -> 16.7 us  [attend_call(): pl.pallas_call(attend, grid_spec=pltpu.PrefetchScalarGridSpec(num_scalar_...]
    ppermute x3 -> x4, waiting for transfers between devices: 2.82 us -> 0.73 us  [seq_flip(): return lax.ppermute(array, 'seq', [(s, s ^ bit) for s in range(seq_size)])]
    ppermute x11, starting transfers between devices: 18 us -> 19.9 us  [partner(): return lax.ppermute(array, ('seq', 'head'), pairs)]
    another operation x10 -> x17, local copies, waits for them, and re-layouts: 0.82 us -> 1.69 us  [the longest x4 0.86 us: per_device(): first_lot = jnp.stack([arrived[k][:rows] for k in order[:TEAM]])]
    unnamed x28 -> x27, local copies, waits for them, and re-layouts: 1.82 us -> 0.96 us
    ppermute x11, waiting for transfers between devices: 12.8 us -> 12 us  [partner(): return lax.ppermute(array, ('seq', 'head'), pairs)]
    gather x0 -> x1, local copies, waits for them, and re-layouts: none -> 0.64 us  [tables(): return (start, 1.0 / length, query_blocks, teams, place_of[asked])]
  transfers between devices with their start and end apart: 14 -> 15, of which waited for: 7 -> 9; matrix products, arithmetic and copies ran while one was open for 5% -> 7% of each run, Pallas kernels for 25% -> 21%
where the time goes in v5:
time: 60 us; the launch traced here: 60.3 us
  Pallas kernels  22 us (37%)
  starting transfers between devices  21.1 us (35%)
  waiting for transfers between devices  12.7 us (21%)
  local copies, waits for them, and re-layouts  3.45 us (6%)
  other arithmetic  0.64 us (1%)
    ppermute x11, starting transfers between devices, partner(): return lax.ppermute(array, ('seq', 'head'), pairs)  19.9 us
    pallas_call x5, Pallas kernels, attend_call(): pl.pallas_call(attend, grid_spec=pltpu.PrefetchScalarGridSpec(num_scalar_...  16.7 us
    ppermute x11, waiting for transfers between devices, partner(): return lax.ppermute(array, ('seq', 'head'), pairs)  12 us
    pallas_call x1, Pallas kernels, per_device(): pl.pallas_call(project, out_shape=[jax.ShapeDtypeStruct((rows + half, LAN...  3.27 us
    pallas_call x1, Pallas kernels, per_device(): pl.pallas_call(finish, out_shape=jax.ShapeDtypeStruct((rows, width), bf16...  1.41 us
  transfers between devices with their start and end apart: 15, of which 9 were waited for; matrix products, arithmetic and copies ran while one was open for 7% of the time, Pallas kernels for 21%

profile of v5, /device:TPU:4, one launch (start us, length us, event | category | flops | bytes accessed | tf_op | source)
XLA Modules:
  0.0 60.3 jit_solution(1883752693283312618)
XLA Ops:
  0.0 3.3 %project.1 = (bf16[384,128]{1,0:T(8,128)(2,1)}, bf16[384,128]{1,0:T(8,128)(2,1)}, bf16[384,128]{1,0:T(8,128)(2,1)}, bf16[384,128]{1,0:T(8,128)(2,1)}, bf16[384,1...) custom-call(s32[1]{0:T(128)} %bitcast.me_ref, ...), custom_call_target="tpu_custom_call" | custom-call | tf_op jit(solution)/shard_map/project/pallas_call | solution.py:249
  3.3 1.6 %collective-permute-start = (bf16[384,128]{1,0:T(8,128)(2,1)}, bf16[384,128]{1,0:T(8,128)(2,1)S(1)}, u32[]{:S(2)}, u32[]{:S(2)}) collective-permute-start(bf16[384,128]{1,0:T(8,128)(2,1)} %get-tuple-element.24), channel_id=1, source_target_pairs={{0,1},{1,0},{2,3},{3,2},{4,5},{5,4},{6,7},{7,6},{8,9},{9,8},{10,11... | collective-permute-start | bytes 294920 | tf_op jit(solution)/shard_map/ppermute | solution.py:244
  4.9 2.6 %collective-permute-start.1 = (bf16[384,128]{1,0:T(8,128)(2,1)}, bf16[384,128]{1,0:T(8,128)(2,1)S(1)}, u32[]{:S(2)}, u32[]{:S(2)}) collective-permute-start(bf16[384,128]{1,0:T(8,128)(2,1)} %get-tuple-element.25), channel_id=1, source_target_pairs={{0,2},{1,3},{2,0},{3,1},{4,6},{5,7},{6,4},{7,5},{8,10},{9,11},{10,... | collective-permute-start | bytes 294920 | tf_op jit(solution)/shard_map/ppermute | solution.py:244
  7.7 1.6 %collective-permute-start.3 = (bf16[384,128]{1,0:T(8,128)(2,1)}, bf16[384,128]{1,0:T(8,128)(2,1)S(1)}, u32[]{:S(2)}, u32[]{:S(2)}) collective-permute-start(bf16[384,128]{1,0:T(8,128)(2,1)} %get-tuple-element.29), channel_id=1, source_target_pairs={{0,9},{1,8},{2,11},{3,10},{4,13},{5,12},{6,15},{7,14},{8,1},{9,0},... | collective-permute-start | bytes 294920 | tf_op jit(solution)/shard_map/ppermute | solution.py:244
  10.3 0.8 %slice_bitcast_fusion.15 = bf16[1,128,128]{2,1,0:T(8,128)(2,1)S(1)} fusion(bf16[384,128]{1,0:T(8,128)(2,1)} %get-tuple-element.23), kind=kLoop, calls=%fused_computation.46 | loop fusion | bytes 65536 | tf_op jit(solution)/shard_map/stack | solution.py:302
  11.0 0.8 %slice_bitcast_fusion.7 = bf16[1,256,128]{2,1,0:T(8,128)(2,1)S(1)} fusion(bf16[384,128]{1,0:T(8,128)(2,1)} %get-tuple-element.23), kind=kLoop, calls=%fused_computation.17 | loop fusion | bytes 131072 | tf_op jit(solution)/shard_map/stack | solution.py:298
  11.9 0.8 %constant_dynamic-update-slice_fusion.7 = bf16[8,128,128]{2,1,0:T(8,128)(2,1)S(1)} fusion(bf16[384,128]{1,0:T(8,128)(2,1)} %get-tuple-element.23), kind=kLoop, calls=%fused_computation.25 | loop fusion | bytes 65536
  13.4 2.1 %collective-permute-done.3 = bf16[384,128]{1,0:T(8,128)(2,1)S(1)} collective-permute-done((bf16[384,128]{1,0:T(8,128)(2,1)}, bf16[384,128]{1,0:T(8,128)(2,1)S(1)}, u32[]{:S(2)}, u32[]{:S(2)}) %collective-permute-start.3) | collective-permute-done | bytes 98336 | tf_op jit(solution)/shard_map/ppermute | solution.py:244
  15.6 3.4 %collective-permute-start.6 = (bf16[384,128]{1,0:T(8,128)(2,1)}, bf16[384,128]{1,0:T(8,128)(2,1)S(1)}, u32[]{:S(2)}, u32[]{:S(2)}) collective-permute-start(bf16[384,128]{1,0:T(8,128)(2,1)} %get-tuple-element.32), channel_id=1, source_target_pairs={{0,10},{1,11},{2,8},{3,9},{4,14},{5,15},{6,12},{7,13},{8,2},{9,3},... | collective-permute-start | bytes 294920 | tf_op jit(solution)/shard_map/ppermute | solution.py:244
  19.0 1.6 %collective-permute-start.7 = (bf16[384,128]{1,0:T(8,128)(2,1)}, bf16[384,128]{1,0:T(8,128)(2,1)S(1)}, u32[]{:S(2)}, u32[]{:S(2)}) collective-permute-start(bf16[384,128]{1,0:T(8,128)(2,1)} %get-tuple-element.33), channel_id=1, source_target_pairs={{0,11},{1,10},{2,9},{3,8},{4,15},{5,14},{6,13},{7,12},{8,3},{9,2},... | collective-permute-start | bytes 294920 | tf_op jit(solution)/shard_map/ppermute | solution.py:244
  21.4 3.7 %collective-permute-done.6 = bf16[384,128]{1,0:T(8,128)(2,1)S(1)} collective-permute-done((bf16[384,128]{1,0:T(8,128)(2,1)}, bf16[384,128]{1,0:T(8,128)(2,1)S(1)}, u32[]{:S(2)}, u32[]{:S(2)}) %collective-permute-start.6) | collective-permute-done | bytes 98336 | tf_op jit(solution)/shard_map/ppermute | solution.py:244
  25.0 1.6 %collective-permute-done.7 = bf16[384,128]{1,0:T(8,128)(2,1)S(1)} collective-permute-done((bf16[384,128]{1,0:T(8,128)(2,1)}, bf16[384,128]{1,0:T(8,128)(2,1)S(1)}, u32[]{:S(2)}, u32[]{:S(2)}) %collective-permute-start.7) | collective-permute-done | bytes 98336 | tf_op jit(solution)/shard_map/ppermute | solution.py:244
  27.4 4.5 %attend.6 = f32[8,128,128]{2,1,0:T(8,128)S(1)} custom-call(s32[64]{0:T(128)S(1)} %convert_reduce_fusion.1.start_ref, f32[64]{0:T(128)S(1)} %multiply_divide_fusion.inverse_ref, s32[8]{0:T(128)S(1)} %get-tuple-element.53.block_ref, s32[2]{0:T(128)S(1)} %multiply_add_fusion.team_ref, s32[8]{0:T(128)S(1)} %gather_fusion, ...), custom_call_target="tpu_custom_call" | custom-call | flops 4000000000 | bytes 4000000 | tf_op jit(solution)/shard_map/attend/pallas_call | solution.py:171
  31.9 2.8 %attend.5.refs_0_ = f32[8,128,128]{2,1,0:T(8,128)S(1)} custom-call(s32[64]{0:T(128)S(1)} %convert_reduce_fusion.1.start_ref, f32[64]{0:T(128)S(1)} %multiply_divide_fusion.inverse_ref, s32[8]{0:T(128)S(1)} %get-tuple-element.52.block_ref, s32[2]{0:T(128)S(1)} %multiply_add_fusion.team_ref, s32[8]{0:T(128)S(1)} %gather_fusion, ...), custom_call_target="tpu_custom_call" | custom-call | flops 4000000000 | bytes 4000000 | tf_op jit(solution)/shard_map/attend/pallas_call | solution.py:171
  35.5 4.6 %attend.8 = bf16[8,128,128]{2,1,0:T(8,128)(2,1)S(1)} custom-call(s32[64]{0:T(128)S(1)} %convert_reduce_fusion.1.start_ref, f32[64]{0:T(128)S(1)} %multiply_divide_fusion.inverse_ref, s32[8]{0:T(128)S(1)} %get-tuple-element.52.block_ref, s32[2]{0:T(128)S(1)} %multiply_add_fusion.2.team_ref, s32[8]{0:T(128)S(1)} %gather_fusion, ...), custom_call_target="tpu_custom_call" | custom-call | flops 4000000000 | bytes 4000000 | tf_op jit(solution)/shard_map/attend/pallas_call | solution.py:171
  40.3 0.9 %attend.7 = f32[4,128,128]{2,1,0:T(8,128)S(1)} custom-call(s32[64]{0:T(128)S(1)} %convert_reduce_fusion.1.start_ref, f32[64]{0:T(128)S(1)} %multiply_divide_fusion.inverse_ref, s32[4]{0:T(128)S(1)} %get-tuple-element.50.block_ref, s32[2]{0:T(128)S(1)} %multiply_add_fusion.2.team_ref, s32[8]{0:T(128)S(1)} %gather_fusion, ...), custom_call_target="tpu_custom_call" | custom-call | flops 2000000000 | bytes 4000000 | tf_op jit(solution)/shard_map/attend/pallas_call | solution.py:171
  41.8 3.7 %collective-permute-start.11 = (bf16[4,128,128]{2,1,0:T(8,128)(2,1)S(1)}, bf16[4,128,128]{2,1,0:T(8,128)(2,1)S(1)}, u32[]{:S(2)}, u32[]{:S(2)}) collective-permute-start(bf16[4,128,128]{2,1,0:T(8,128)(2,1)S(1)} %add_convert_fusion), channel_id=1, source_target_pairs={{0,8},{1,9},{2,10},{3,11},{4,12},{5,13},{6,14},{7,15},{8,0},{9,1},... | collective-permute-start | bytes 393224 | tf_op jit(solution)/shard_map/ppermute | solution.py:244
  45.6 3.9 %attend.9 = bf16[4,128,128]{2,1,0:T(8,128)(2,1)S(1)} custom-call(s32[64]{0:T(128)S(1)} %convert_reduce_fusion.1.start_ref, f32[64]{0:T(128)S(1)} %multiply_divide_fusion.inverse_ref, s32[4]{0:T(128)S(1)} %get-tuple-element.51.block_ref, s32[2]{0:T(128)S(1)} %multiply_add_fusion.2.team_ref, s32[8]{0:T(128)S(1)} %gather_fusion, ...), custom_call_target="tpu_custom_call" | custom-call | flops 2000000000 | bytes 4000000 | tf_op jit(solution)/shard_map/attend/pallas_call | solution.py:171
  49.8 0.7 %collective-permute-start.12 = (bf16[2,128,128]{2,1,0:T(8,128)(2,1)S(1)}, bf16[2,128,128]{2,1,0:T(8,128)(2,1)S(1)}, u32[]{:S(2)}, u32[]{:S(2)}) collective-permute-start(bf16[2,128,128]{2,1,0:T(8,128)(2,1)S(1)} %pad_maximum_fusion.5), channel_id=1, source_target_pairs={{0,1},{1,0},{2,3},{3,2},{4,5},{5,4},{6,7},{7,6},{8,9},{9,8},{10,11... | collective-permute-start | bytes 196616 | tf_op jit(solution)/shard_map/ppermute | solution.py:244
  50.5 1.9 %collective-permute-start.13 = (bf16[2,128,128]{2,1,0:T(8,128)(2,1)S(1)}, bf16[2,128,128]{2,1,0:T(8,128)(2,1)S(1)}, u32[]{:S(2)}, u32[]{:S(2)}) collective-permute-start(bf16[2,128,128]{2,1,0:T(8,128)(2,1)S(1)} %pad_maximum_fusion.6), channel_id=1, source_target_pairs={{0,2},{1,3},{2,0},{3,1},{4,6},{5,7},{6,4},{7,5},{8,10},{9,11},{10,... | collective-permute-start | bytes 196616 | tf_op jit(solution)/shard_map/ppermute | solution.py:244
  52.4 2.0 %collective-permute-start.14 = (bf16[2,128,128]{2,1,0:T(8,128)(2,1)S(1)}, bf16[2,128,128]{2,1,0:T(8,128)(2,1)S(1)}, u32[]{:S(2)}, u32[]{:S(2)}) collective-permute-start(bf16[2,128,128]{2,1,0:T(8,128)(2,1)S(1)} %pad_maximum_fusion.7), channel_id=1, source_target_pairs={{0,3},{1,2},{2,1},{3,0},{4,7},{5,6},{6,5},{7,4},{8,11},{9,10},{10,... | collective-permute-start | bytes 196616 | tf_op jit(solution)/shard_map/ppermute | solution.py:244
  54.6 1.5 %collective-permute-done.13 = bf16[2,128,128]{2,1,0:T(8,128)(2,1)S(1)} collective-permute-done((bf16[2,128,128]{2,1,0:T(8,128)(2,1)S(1)}, bf16[2,128,128]{2,1,0:T(8,128)(2,1)S(1)}, u32[]{:S(2)}, u32[]{:S(2)}) %collective-permute-start.13) | collective-permute-done | bytes 65568 | tf_op jit(solution)/shard_map/ppermute | solution.py:244
  56.1 2.7 %collective-permute-done.14 = bf16[2,128,128]{2,1,0:T(8,128)(2,1)S(1)} collective-permute-done((bf16[2,128,128]{2,1,0:T(8,128)(2,1)S(1)}, bf16[2,128,128]{2,1,0:T(8,128)(2,1)S(1)}, u32[]{:S(2)}, u32[]{:S(2)}) %collective-permute-start.14) | collective-permute-done | bytes 65568 | tf_op jit(solution)/shard_map/ppermute | solution.py:244
  58.9 1.4 %finish.1 = bf16[256,512]{1,0:T(8,128)(2,1)} custom-call(s32[1]{0:T(128)} %bitcast.me_ref, bf16[256,512]{1,0:T(8,128)(2,1)S(1)} %copy-done.1, bf16[8,128,128]{2,1,0:T(8,128)(2,1)S(1)} %constant_dynamic-update-slice_fusion.13.attention_ref, bf16[256,512]{1,0:T(8,128)(2,1)S(1)} %project_gating.1.gating_ref, bf16[512,512]{1,0:T(8,128)(2,1)S(1)} %copy-done.2), custom_call_target="tpu_custom_call" | custom-call | tf_op jit(solution)/shard_map/finish/pallas_call | solution.py:343
  (83 shorter events, 5.4 us)
Async XLA Ops:
  0.0 12.8 %copy-start.3 = (s32[8]{0:T(128)S(1)}, s32[8]{0:T(128)}, u32[]{:S(2)}) copy-start(s32[8]{0:T(128)} %constant.127.clone) | copy-start | bytes 100
  0.0 9.9 %copy-start.4 = (s32[64]{0:T(128)S(1)}, s32[64]{0:T(128)}, u32[]{:S(2)}) copy-start(s32[64]{0:T(128)} %param.8) | copy-start | bytes 772
  3.3 10.1 %collective-permute-start = (bf16[384,128]{1,0:T(8,128)(2,1)}, bf16[384,128]{1,0:T(8,128)(2,1)S(1)}, u32[]{:S(2)}, u32[]{:S(2)}) collective-permute-start(bf16[384,128]{1,0:T(8,128)(2,1)} %get-tuple-element.24), channel_id=1, source_target_pairs={{0,1},{1,0},{2,3},{3,2},{4,5},{5,4},{6,7},{7,6},{8,9},{9,8},{10,11... | collective-permute-start | bytes 294920 | tf_op jit(solution)/shard_map/ppermute | solution.py:244
  4.9 16.2 %collective-permute-start.1 = (bf16[384,128]{1,0:T(8,128)(2,1)}, bf16[384,128]{1,0:T(8,128)(2,1)S(1)}, u32[]{:S(2)}, u32[]{:S(2)}) collective-permute-start(bf16[384,128]{1,0:T(8,128)(2,1)} %get-tuple-element.25), channel_id=1, source_target_pairs={{0,2},{1,3},{2,0},{3,1},{4,6},{5,7},{6,4},{7,5},{8,10},{9,11},{10,... | collective-permute-start | bytes 294920 | tf_op jit(solution)/shard_map/ppermute | solution.py:244
  7.5 13.7 %collective-permute-start.2 = (bf16[384,128]{1,0:T(8,128)(2,1)}, bf16[384,128]{1,0:T(8,128)(2,1)S(1)}, u32[]{:S(2)}, u32[]{:S(2)}) collective-permute-start(bf16[384,128]{1,0:T(8,128)(2,1)} %get-tuple-element.26), channel_id=1, source_target_pairs={{0,3},{1,2},{2,1},{3,0},{4,7},{5,6},{6,5},{7,4},{8,11},{9,10},{10,... | collective-permute-start | bytes 294920 | tf_op jit(solution)/shard_map/ppermute | solution.py:244
  7.7 7.8 %collective-permute-start.3 = (bf16[384,128]{1,0:T(8,128)(2,1)}, bf16[384,128]{1,0:T(8,128)(2,1)S(1)}, u32[]{:S(2)}, u32[]{:S(2)}) collective-permute-start(bf16[384,128]{1,0:T(8,128)(2,1)} %get-tuple-element.29), channel_id=1, source_target_pairs={{0,9},{1,8},{2,11},{3,10},{4,13},{5,12},{6,15},{7,14},{8,1},{9,0},... | collective-permute-start | bytes 294920 | tf_op jit(solution)/shard_map/ppermute | solution.py:244
  9.3 6.2 %collective-permute-start.4 = (bf16[384,128]{1,0:T(8,128)(2,1)}, bf16[384,128]{1,0:T(8,128)(2,1)S(1)}, u32[]{:S(2)}, u32[]{:S(2)}) collective-permute-start(bf16[384,128]{1,0:T(8,128)(2,1)} %get-tuple-element.30), channel_id=1, source_target_pairs={{0,8},{1,9},{2,10},{3,11},{4,12},{5,13},{6,14},{7,15},{8,0},{9,1},... | collective-permute-start | bytes 294920 | tf_op jit(solution)/shard_map/ppermute | solution.py:244
  15.6 9.5 %collective-permute-start.6 = (bf16[384,128]{1,0:T(8,128)(2,1)}, bf16[384,128]{1,0:T(8,128)(2,1)S(1)}, u32[]{:S(2)}, u32[]{:S(2)}) collective-permute-start(bf16[384,128]{1,0:T(8,128)(2,1)} %get-tuple-element.32), channel_id=1, source_target_pairs={{0,10},{1,11},{2,8},{3,9},{4,14},{5,15},{6,12},{7,13},{8,2},{9,3},... | collective-permute-start | bytes 294920 | tf_op jit(solution)/shard_map/ppermute | solution.py:244
  19.0 7.6 %collective-permute-start.7 = (bf16[384,128]{1,0:T(8,128)(2,1)}, bf16[384,128]{1,0:T(8,128)(2,1)S(1)}, u32[]{:S(2)}, u32[]{:S(2)}) collective-permute-start(bf16[384,128]{1,0:T(8,128)(2,1)} %get-tuple-element.33), channel_id=1, source_target_pairs={{0,11},{1,10},{2,9},{3,8},{4,15},{5,14},{6,13},{7,12},{8,3},{9,2},... | collective-permute-start | bytes 294920 | tf_op jit(solution)/shard_map/ppermute | solution.py:244
  20.6 14.8 %collective-permute-start.5 = (bf16[4,256,128]{2,1,0:T(8,128)(2,1)S(1)}, bf16[4,256,128]{2,1,0:T(8,128)(2,1)S(1)}, u32[]{:S(2)}, u32[]{:S(2)}) collective-permute-start(bf16[4,256,128]{2,1,0:T(8,128)(2,1)S(1)} %pad_maximum_fusion.1), channel_id=1, source_target_pairs={{0,16},{4,20},{8,24},{12,28},{16,0},{20,4},{24,8},{28,12},{1,17},{... | collective-permute-start | bytes 786440 | tf_op jit(solution)/shard_map/ppermute | solution.py:247
  26.6 5.2 %collective-permute-start.9 = (bf16[8,128,128]{2,1,0:T(8,128)(2,1)S(1)}, bf16[8,128,128]{2,1,0:T(8,128)(2,1)S(1)}, u32[]{:S(2)}, u32[]{:S(2)}) collective-permute-start(bf16[8,128,128]{2,1,0:T(8,128)(2,1)S(1)} %constant_dynamic-update-slice_fusion.queries_ref), channel_id=1, source_target_pairs={{0,4},{4,0},{8,12},{12,8},{16,20},{20,16},{24,28},{28,24},{1,5},{5... | collective-permute-start | bytes 786440 | tf_op jit(solution)/shard_map/ppermute | solution.py:247
  26.7 8.8 %collective-permute-start.8 = (bf16[4,256,128]{2,1,0:T(8,128)(2,1)S(1)}, bf16[4,256,128]{2,1,0:T(8,128)(2,1)S(1)}, u32[]{:S(2)}, u32[]{:S(2)}) collective-permute-start(bf16[4,256,128]{2,1,0:T(8,128)(2,1)S(1)} %pad_maximum_fusion.2), channel_id=1, source_target_pairs={{0,16},{4,20},{8,24},{12,28},{16,0},{20,4},{24,8},{28,12},{1,17},{... | collective-permute-start | bytes 786440 | tf_op jit(solution)/shard_map/ppermute | solution.py:247
  31.9 2.8 %copy-start = (bf16[512,2048]{1,0:T(8,128)(2,1)S(1)}, bf16[512,2048]{1,0:T(8,128)(2,1)}, u32[]{:S(2)}) copy-start(bf16[512,2048]{1,0:T(8,128)(2,1)} %weights_ref.4) | copy-start | bytes 6291460
  31.9 2.8 %copy-start.1 = (bf16[256,512]{1,0:T(8,128)(2,1)S(1)}, bf16[256,512]{1,0:T(8,128)(2,1)}, u32[]{:S(2)}) copy-start(bf16[256,512]{1,0:T(8,128)(2,1)} %tokens_ref.4) | copy-start | bytes 786436
  40.2 1.6 %collective-permute-start.10 = (bf16[8,128,128]{2,1,0:T(8,128)(2,1)S(1)}, bf16[8,128,128]{2,1,0:T(8,128)(2,1)S(1)}, u32[]{:S(2)}, u32[]{:S(2)}) collective-permute-start(bf16[8,128,128]{2,1,0:T(8,128)(2,1)S(1)} %attend.8), channel_id=1, source_target_pairs={{0,4},{4,0},{8,12},{12,8},{16,20},{20,16},{24,28},{28,24},{1,5},{5... | collective-permute-start | bytes 786440 | tf_op jit(solution)/shard_map/ppermute | solution.py:247
  41.8 7.9 %collective-permute-start.11 = (bf16[4,128,128]{2,1,0:T(8,128)(2,1)S(1)}, bf16[4,128,128]{2,1,0:T(8,128)(2,1)S(1)}, u32[]{:S(2)}, u32[]{:S(2)}) collective-permute-start(bf16[4,128,128]{2,1,0:T(8,128)(2,1)S(1)} %add_convert_fusion), channel_id=1, source_target_pairs={{0,8},{1,9},{2,10},{3,11},{4,12},{5,13},{6,14},{7,15},{8,0},{9,1},... | collective-permute-start | bytes 393224 | tf_op jit(solution)/shard_map/ppermute | solution.py:244
  45.5 13.4 %copy-start.2 = (bf16[512,512]{1,0:T(8,128)(2,1)S(1)}, bf16[512,512]{1,0:T(8,128)(2,1)}, u32[]{:S(2)}) copy-start(bf16[512,512]{1,0:T(8,128)(2,1)} %weights_ref.5) | copy-start | bytes 1572868
  49.8 4.8 %collective-permute-start.12 = (bf16[2,128,128]{2,1,0:T(8,128)(2,1)S(1)}, bf16[2,128,128]{2,1,0:T(8,128)(2,1)S(1)}, u32[]{:S(2)}, u32[]{:S(2)}) collective-permute-start(bf16[2,128,128]{2,1,0:T(8,128)(2,1)S(1)} %pad_maximum_fusion.5), channel_id=1, source_target_pairs={{0,1},{1,0},{2,3},{3,2},{4,5},{5,4},{6,7},{7,6},{8,9},{9,8},{10,11... | collective-permute-start | bytes 196616 | tf_op jit(solution)/shard_map/ppermute | solution.py:244
  50.5 5.6 %collective-permute-start.13 = (bf16[2,128,128]{2,1,0:T(8,128)(2,1)S(1)}, bf16[2,128,128]{2,1,0:T(8,128)(2,1)S(1)}, u32[]{:S(2)}, u32[]{:S(2)}) collective-permute-start(bf16[2,128,128]{2,1,0:T(8,128)(2,1)S(1)} %pad_maximum_fusion.6), channel_id=1, source_target_pairs={{0,2},{1,3},{2,0},{3,1},{4,6},{5,7},{6,4},{7,5},{8,10},{9,11},{10,... | collective-permute-start | bytes 196616 | tf_op jit(solution)/shard_map/ppermute | solution.py:244
  52.4 6.5 %collective-permute-start.14 = (bf16[2,128,128]{2,1,0:T(8,128)(2,1)S(1)}, bf16[2,128,128]{2,1,0:T(8,128)(2,1)S(1)}, u32[]{:S(2)}, u32[]{:S(2)}) collective-permute-start(bf16[2,128,128]{2,1,0:T(8,128)(2,1)S(1)} %pad_maximum_fusion.7), channel_id=1, source_target_pairs={{0,3},{1,2},{2,1},{3,0},{4,7},{5,6},{6,5},{7,4},{8,11},{9,10},{10,... | collective-permute-start | bytes 196616 | tf_op jit(solution)/shard_map/ppermute | solution.py:244

commit v6 on v5

--- a/solution.py
+++ b/solution.py
@@ -42,23 +42,34 @@
     outs, (tokens, weights, held, sems) = refs[:-4], refs[-4:]
     rows = tokens.shape[0]
     half = rows // 2
-    copies = [pltpu.make_async_copy(tokens_ref, tokens, sems.at[0])]
+    copies = [[pltpu.make_async_copy(tokens_ref, tokens, sems.at[0])]]
+    deep = weights.shape[1] // 2
     for i, block in enumerate((3, 1, 2)):
-        at = pl.ds(block * H * DH, H * DH)
-        copies.append(
-            pltpu.make_async_copy(weights_ref.at[:, at], weights.at[i], sems.at[i + 1])
-        )
-    for copy in copies:
-        copy.start()
-    copies[0].wait()
+        pieces = []
+        for j in range(2):
+            inner = pl.ds(j * deep, deep)
+            source = weights_ref.at[inner, pl.ds(block * H * DH, H * DH)]
+            pieces.append(
+                pltpu.make_async_copy(source, weights.at[i, inner], sems.at[1 + 2 * i + j])
+            )
+        copies.append(pieces)
+    for pieces in copies:
+        for copy in pieces:
+            copy.start()
+
+    def wait(number):
+        for copy in copies[number]:
+            copy.wait()
+
+    wait(0)
     normed = layer_norm(tokens[...].astype(f32)).astype(bf16)
     low, half_low = low_lanes(rows), low_lanes(half)
     scale = 0.5 * DH ** (-0.5)
-    copies[1].wait()
+    wait(1)
     keys = silu(jnp.dot(normed, weights[0], preferred_element_type=f32))
-    copies[2].wait()
+    wait(2)
     values = silu(jnp.dot(normed, weights[1], preferred_element_type=f32))
-    copies[3].wait()
+    wait(3)
     queries = silu(jnp.dot(normed, weights[2], preferred_element_type=f32)) * scale
     for pair in range(H // 2):
         at = slice(pair * LANES, (pair + 1) * LANES)
@@ -141,6 +152,26 @@
             else:
                 add_to(i)
 
+    def add_diagonal(team):
+        key_rows = jnp.concatenate([held[slot_ref[team * TEAM + i]] for i in range(TEAM)], axis=0)
+        turn = blocks[0] - least
+        for i in range(TEAM):
+            seen = (i + 1) * rows
+            at = pl.ds(pl.multiple_of(jnp.bitwise_xor(turn, i) * rows, rows), rows)
+            score = lax.dot_general(
+                queries[at], key_rows[:seen], (((1,), (1,)), ((), ())), preferred_element_type=f32
+            )
+            weights = score + score * jnp.tanh(score)
+            column = lax.broadcasted_iota(jnp.int32, (TILE, seen), 1)
+            ahead = column - lax.broadcasted_iota(jnp.int32, (TILE, seen), 0)
+            pieces = []
+            for j in range(tiles):
+                from_start = start_ref[(least + i) * tiles + j] * TILE - least * rows
+                allowed = (column >= from_start) & (ahead <= i * rows + j * TILE)
+                pieces.append(jnp.where(allowed, weights[j * TILE : (j + 1) * TILE], 0.0))
+            weights = jnp.concatenate(pieces, axis=0).astype(bf16)
+            total[at] += jnp.dot(weights, key_rows[:seen], preferred_element_type=f32)
+
     def one_team(team, carry):
         key_block = team_ref[team]
         earlier = (key_block < least) & ((key_block + TEAM) * tiles > low_start)
@@ -148,9 +179,8 @@
         every = (key_block + TEAM) * tiles > high_first
         pl.when(earlier & whole)(lambda: add(team, key_block, False, False))
         pl.when(earlier & ~every)(lambda: add(team, key_block, True, True))
-        pl.when((earlier & ~whole & every) | (key_block == least))(
-            lambda: add(team, key_block, True, False)
-        )
+        pl.when(earlier & ~whole & every)(lambda: add(team, key_block, True, False))
+        pl.when(key_block == least)(lambda: add_diagonal(team))
         return carry
 
     lax.fori_loop(0, held.shape[0] // TEAM, one_team, 0)
@@ -255,9 +285,9 @@
             pltpu.VMEM((rows, width), bf16),
             pltpu.VMEM((3, width, H * DH), bf16),
             pltpu.VMEM((H, rows + half, LANES), bf16),
-            pltpu.SemaphoreType.DMA((4,)),
+            pltpu.SemaphoreType.DMA((7,)),
         ],
-        compiler_params=pltpu.CompilerParams(vmem_limit_bytes=58 << 20),
+        compiler_params=pltpu.CompilerParams(vmem_limit_bytes=52 << 20),
         name="project",
     )(me_array, tokens, w_proj)
     def gating_of(tokens):
@@ -295,10 +325,13 @@
     arrived = {0: sent[0]}
     for k in order[1:-2]:
         arrived[k] = partner(sent[k], k)
-    first_lot = jnp.stack([arrived[k][:rows] for k in order[:TEAM]])
-    *held_back, first_lot = lax.optimization_barrier((sent[order[-2]], sent[order[-1]], first_lot))
+    nearest = order[1:3]
+    *held_back, arrived[nearest[0]], arrived[nearest[1]] = lax.optimization_barrier(
+        (sent[order[-2]], sent[order[-1]], arrived[nearest[0]], arrived[nearest[1]])
+    )
     for k, array in zip(order[-2:], held_back):
         arrived[k] = partner(array, k)
+    first_lot = jnp.stack([arrived[k][:rows] for k in order[:TEAM]])
     queries = jnp.stack([arrived[k][rows:] for k in range(H)])
     lots = [first_lot, jnp.stack([arrived[k][:rows] for k in order[TEAM:]])]
     keys = jnp.concatenate(lots)

time: 60 us -> 60.9 us (1.015); the launches traced: 60.3 us -> 60.1 us
  waiting for transfers between devices: 12.7 us -> 15.1 us
  Pallas kernels: 22 us -> 20.5 us
  local copies, waits for them, and re-layouts: 3.45 us -> 2.1 us
    ppermute x11, waiting for transfers between devices: 12 us -> 14.1 us  [partner(): return lax.ppermute(array, ('seq', 'head'), pairs)]
    pallas_call x1, Pallas kernels: 3.27 us -> 2.32 us  [per_device(): pl.pallas_call(project, out_shape=[jax.ShapeDtypeStruct((rows + half, LAN...]
    another operation x4 -> x3, local copies, waits for them, and re-layouts: 0.86 us -> 0.02 us  [per_device(): first_lot = jnp.stack([arrived[k][:rows] for k in order[:TEAM]])]
    another operation x9, local copies, waits for them, and re-layouts: 0.8 us -> 0.04 us  [per_device(): queries = jnp.stack([arrived[k][rows:] for k in range(H)])]
  transfers between devices with their start and end apart: 15 -> 15, of which waited for: 9 -> 8; matrix products, arithmetic and copies ran while one was open for 7% -> 3% of each run, Pallas kernels for 21% -> 21%
where the time goes in v6:
time: 60.9 us; the launch traced here: 60.1 us
  starting transfers between devices  21.3 us (35%)
  Pallas kernels  20.5 us (34%)
  waiting for transfers between devices  15.1 us (25%)
  local copies, waits for them, and re-layouts  2.1 us (3%)
  other arithmetic  0.64 us (1%)
    ppermute x11, starting transfers between devices, partner(): return lax.ppermute(array, ('seq', 'head'), pairs)  20.2 us
    pallas_call x5, Pallas kernels, attend_call(): pl.pallas_call(attend, grid_spec=pltpu.PrefetchScalarGridSpec(num_scalar_...  16.2 us
    ppermute x11, waiting for transfers between devices, partner(): return lax.ppermute(array, ('seq', 'head'), pairs)  14.1 us
    pallas_call x1, Pallas kernels, per_device(): pl.pallas_call(project, out_shape=[jax.ShapeDtypeStruct((rows + half, LAN...  2.32 us
    pallas_call x1, Pallas kernels, per_device(): pl.pallas_call(finish, out_shape=jax.ShapeDtypeStruct((rows, width), bf16...  1.42 us
  transfers between devices with their start and end apart: 15, of which 8 were waited for; matrix products, arithmetic and copies ran while one was open for 3% of the time, Pallas kernels for 21%

profile of v6, /device:TPU:4, one launch (start us, length us, event | category | flops | bytes accessed | tf_op | source)
XLA Modules:
  0.0 60.1 jit_solution(416270252336523182)
XLA Ops:
  0.0 1.0 %copy-done.1 = bf16[256,512]{1,0:T(8,128)(2,1)S(1)} copy-done((bf16[256,512]{1,0:T(8,128)(2,1)S(1)}, bf16[256,512]{1,0:T(8,128)(2,1)}, u32[]{:S(2)}) %copy-start.1) | copy-done | bytes 262168
  1.0 2.3 %project.1 = (bf16[384,128]{1,0:T(8,128)(2,1)S(1)}, bf16[384,128]{1,0:T(8,128)(2,1)S(1)}, bf16[384,128]{1,0:T(8,128)(2,1)S(1)}, bf16[384,128]{1,0:T(8,128)(2,1)S...) custom-call(s32[1]{0:T(128)} %bitcast.me_ref, ...), custom_call_target="tpu_custom_call" | custom-call | tf_op jit(solution)/shard_map/project/pallas_call | solution.py:279
  3.3 1.6 %collective-permute-start = (bf16[384,128]{1,0:T(8,128)(2,1)S(1)}, bf16[384,128]{1,0:T(8,128)(2,1)S(1)}, u32[]{:S(2)}, u32[]{:S(2)}) collective-permute-start(bf16[384,128]{1,0:T(8,128)(2,1)S(1)} %get-tuple-element.27), channel_id=1, source_target_pairs={{0,1},{1,0},{2,3},{3,2},{4,5},{5,4},{6,7},{7,6},{8,9},{9,8},{10,11... | collective-permute-start | bytes 294920 | tf_op jit(solution)/shard_map/ppermute | solution.py:274
  5.0 1.4 %collective-permute-start.1 = (bf16[384,128]{1,0:T(8,128)(2,1)S(1)}, bf16[384,128]{1,0:T(8,128)(2,1)S(1)}, u32[]{:S(2)}, u32[]{:S(2)}) collective-permute-start(bf16[384,128]{1,0:T(8,128)(2,1)S(1)} %get-tuple-element.28), channel_id=1, source_target_pairs={{0,9},{1,8},{2,11},{3,10},{4,13},{5,12},{6,15},{7,14},{8,1},{9,0},... | collective-permute-start | bytes 294920 | tf_op jit(solution)/shard_map/ppermute | solution.py:274
  6.3 2.6 %collective-permute-start.2 = (bf16[384,128]{1,0:T(8,128)(2,1)S(1)}, bf16[384,128]{1,0:T(8,128)(2,1)S(1)}, u32[]{:S(2)}, u32[]{:S(2)}) collective-permute-start(bf16[384,128]{1,0:T(8,128)(2,1)S(1)} %get-tuple-element.30), channel_id=1, source_target_pairs={{0,2},{1,3},{2,0},{3,1},{4,6},{5,7},{6,4},{7,5},{8,10},{9,11},{10,... | collective-permute-start | bytes 294920 | tf_op jit(solution)/shard_map/ppermute | solution.py:274
  8.9 1.3 %collective-permute-start.3 = (bf16[384,128]{1,0:T(8,128)(2,1)S(1)}, bf16[384,128]{1,0:T(8,128)(2,1)S(1)}, u32[]{:S(2)}, u32[]{:S(2)}) collective-permute-start(bf16[384,128]{1,0:T(8,128)(2,1)S(1)} %get-tuple-element.31), channel_id=1, source_target_pairs={{0,3},{1,2},{2,1},{3,0},{4,7},{5,6},{6,5},{7,4},{8,11},{9,10},{10,... | collective-permute-start | bytes 294920 | tf_op jit(solution)/shard_map/ppermute | solution.py:274
  11.4 0.6 %gather_fusion = s32[8]{0:T(128)S(1)} fusion(s32[8]{0:T(128)S(1)} %copy-done.4, s32[1024]{0:T(1024)S(1)} %pad_clamp_fusion), kind=kCustom, calls=%fused_computation | custom fusion | bytes 96 | tf_op jit(solution)/shard_map/gather | solution.py:347
  12.1 1.2 %collective-permute-done.1 = bf16[384,128]{1,0:T(8,128)(2,1)S(1)} collective-permute-done((bf16[384,128]{1,0:T(8,128)(2,1)S(1)}, bf16[384,128]{1,0:T(8,128)(2,1)S(1)}, u32[]{:S(2)}, u32[]{:S(2)}) %collective-permute-start.1) | collective-permute-done | bytes 98336 | tf_op jit(solution)/shard_map/ppermute | solution.py:274
  13.2 1.9 %collective-permute-start.6 = (bf16[384,128]{1,0:T(8,128)(2,1)S(1)}, bf16[384,128]{1,0:T(8,128)(2,1)S(1)}, u32[]{:S(2)}, u32[]{:S(2)}) collective-permute-start(bf16[384,128]{1,0:T(8,128)(2,1)S(1)} %get-tuple-element.34), channel_id=1, source_target_pairs={{0,10},{1,11},{2,8},{3,9},{4,14},{5,15},{6,12},{7,13},{8,2},{9,3},... | collective-permute-start | bytes 294920 | tf_op jit(solution)/shard_map/ppermute | solution.py:274
  15.2 1.8 %collective-permute-start.7 = (bf16[384,128]{1,0:T(8,128)(2,1)S(1)}, bf16[384,128]{1,0:T(8,128)(2,1)S(1)}, u32[]{:S(2)}, u32[]{:S(2)}) collective-permute-start(bf16[384,128]{1,0:T(8,128)(2,1)S(1)} %get-tuple-element.35), channel_id=1, source_target_pairs={{0,11},{1,10},{2,9},{3,8},{4,15},{5,14},{6,13},{7,12},{8,3},{9,2},... | collective-permute-start | bytes 294920 | tf_op jit(solution)/shard_map/ppermute | solution.py:274
  17.0 0.8 %collective-permute-done.2 = bf16[384,128]{1,0:T(8,128)(2,1)S(1)} collective-permute-done((bf16[384,128]{1,0:T(8,128)(2,1)S(1)}, bf16[384,128]{1,0:T(8,128)(2,1)S(1)}, u32[]{:S(2)}, u32[]{:S(2)}) %collective-permute-start.2) | collective-permute-done | bytes 98336 | tf_op jit(solution)/shard_map/ppermute | solution.py:274
  18.7 6.6 %collective-permute-done.6 = bf16[384,128]{1,0:T(8,128)(2,1)S(1)} collective-permute-done((bf16[384,128]{1,0:T(8,128)(2,1)S(1)}, bf16[384,128]{1,0:T(8,128)(2,1)S(1)}, u32[]{:S(2)}, u32[]{:S(2)}) %collective-permute-start.6) | collective-permute-done | bytes 98336 | tf_op jit(solution)/shard_map/ppermute | solution.py:274
  25.8 3.4 %attend.6 = f32[8,128,128]{2,1,0:T(8,128)S(1)} custom-call(s32[64]{0:T(128)S(1)} %convert_reduce_fusion.1.start_ref, f32[64]{0:T(128)S(1)} %multiply_divide_fusion.inverse_ref, s32[8]{0:T(128)S(1)} %get-tuple-element.55.block_ref, s32[2]{0:T(128)S(1)} %multiply_add_fusion.team_ref, s32[8]{0:T(128)S(1)} %gather_fusion, ...), custom_call_target="tpu_custom_call" | custom-call | flops 4000000000 | bytes 4000000 | tf_op jit(solution)/shard_map/attend/pallas_call | solution.py:201
  29.3 3.6 %attend.5.refs_0_ = f32[8,128,128]{2,1,0:T(8,128)S(1)} custom-call(s32[64]{0:T(128)S(1)} %convert_reduce_fusion.1.start_ref, f32[64]{0:T(128)S(1)} %multiply_divide_fusion.inverse_ref, s32[8]{0:T(128)S(1)} %get-tuple-element.54.block_ref, s32[2]{0:T(128)S(1)} %multiply_add_fusion.team_ref, s32[8]{0:T(128)S(1)} %gather_fusion, ...), custom_call_target="tpu_custom_call" | custom-call | flops 4000000000 | bytes 4000000 | tf_op jit(solution)/shard_map/attend/pallas_call | solution.py:201
  34.2 4.4 %attend.8 = bf16[8,128,128]{2,1,0:T(8,128)(2,1)S(1)} custom-call(s32[64]{0:T(128)S(1)} %convert_reduce_fusion.1.start_ref, f32[64]{0:T(128)S(1)} %multiply_divide_fusion.inverse_ref, s32[8]{0:T(128)S(1)} %get-tuple-element.54.block_ref, s32[2]{0:T(128)S(1)} %multiply_add_fusion.2.team_ref, s32[8]{0:T(128)S(1)} %gather_fusion, ...), custom_call_target="tpu_custom_call" | custom-call | flops 4000000000 | bytes 4000000 | tf_op jit(solution)/shard_map/attend/pallas_call | solution.py:201
  38.8 1.1 %attend.7 = f32[4,128,128]{2,1,0:T(8,128)S(1)} custom-call(s32[64]{0:T(128)S(1)} %convert_reduce_fusion.1.start_ref, f32[64]{0:T(128)S(1)} %multiply_divide_fusion.inverse_ref, s32[4]{0:T(128)S(1)} %get-tuple-element.52.block_ref, s32[2]{0:T(128)S(1)} %multiply_add_fusion.2.team_ref, s32[8]{0:T(128)S(1)} %gather_fusion, ...), custom_call_target="tpu_custom_call" | custom-call | flops 2000000000 | bytes 4000000 | tf_op jit(solution)/shard_map/attend/pallas_call | solution.py:201
  40.3 3.9 %collective-permute-start.11 = (bf16[4,128,128]{2,1,0:T(8,128)(2,1)S(1)}, bf16[4,128,128]{2,1,0:T(8,128)(2,1)S(1)}, u32[]{:S(2)}, u32[]{:S(2)}) collective-permute-start(bf16[4,128,128]{2,1,0:T(8,128)(2,1)S(1)} %add_convert_fusion), channel_id=1, source_target_pairs={{0,8},{1,9},{2,10},{3,11},{4,12},{5,13},{6,14},{7,15},{8,0},{9,1},... | collective-permute-start | bytes 393224 | tf_op jit(solution)/shard_map/ppermute | solution.py:274
  44.2 3.7 %attend.9 = bf16[4,128,128]{2,1,0:T(8,128)(2,1)S(1)} custom-call(s32[64]{0:T(128)S(1)} %convert_reduce_fusion.1.start_ref, f32[64]{0:T(128)S(1)} %multiply_divide_fusion.inverse_ref, s32[4]{0:T(128)S(1)} %get-tuple-element.53.block_ref, s32[2]{0:T(128)S(1)} %multiply_add_fusion.2.team_ref, s32[8]{0:T(128)S(1)} %gather_fusion, ...), custom_call_target="tpu_custom_call" | custom-call | flops 2000000000 | bytes 4000000 | tf_op jit(solution)/shard_map/attend/pallas_call | solution.py:201
  48.4 2.0 %collective-permute-start.12 = (bf16[2,128,128]{2,1,0:T(8,128)(2,1)S(1)}, bf16[2,128,128]{2,1,0:T(8,128)(2,1)S(1)}, u32[]{:S(2)}, u32[]{:S(2)}) collective-permute-start(bf16[2,128,128]{2,1,0:T(8,128)(2,1)S(1)} %pad_maximum_fusion.5), channel_id=1, source_target_pairs={{0,1},{1,0},{2,3},{3,2},{4,5},{5,4},{6,7},{7,6},{8,9},{9,8},{10,11... | collective-permute-start | bytes 196616 | tf_op jit(solution)/shard_map/ppermute | solution.py:274
  50.4 1.9 %collective-permute-start.13 = (bf16[2,128,128]{2,1,0:T(8,128)(2,1)S(1)}, bf16[2,128,128]{2,1,0:T(8,128)(2,1)S(1)}, u32[]{:S(2)}, u32[]{:S(2)}) collective-permute-start(bf16[2,128,128]{2,1,0:T(8,128)(2,1)S(1)} %pad_maximum_fusion.6), channel_id=1, source_target_pairs={{0,2},{1,3},{2,0},{3,1},{4,6},{5,7},{6,4},{7,5},{8,10},{9,11},{10,... | collective-permute-start | bytes 196616 | tf_op jit(solution)/shard_map/ppermute | solution.py:274
  52.3 1.2 %collective-permute-start.14 = (bf16[2,128,128]{2,1,0:T(8,128)(2,1)S(1)}, bf16[2,128,128]{2,1,0:T(8,128)(2,1)S(1)}, u32[]{:S(2)}, u32[]{:S(2)}) collective-permute-start(bf16[2,128,128]{2,1,0:T(8,128)(2,1)S(1)} %pad_maximum_fusion.7), channel_id=1, source_target_pairs={{0,3},{1,2},{2,1},{3,0},{4,7},{5,6},{6,5},{7,4},{8,11},{9,10},{10,... | collective-permute-start | bytes 196616 | tf_op jit(solution)/shard_map/ppermute | solution.py:274
  53.5 2.4 %collective-permute-done.13 = bf16[2,128,128]{2,1,0:T(8,128)(2,1)S(1)} collective-permute-done((bf16[2,128,128]{2,1,0:T(8,128)(2,1)S(1)}, bf16[2,128,128]{2,1,0:T(8,128)(2,1)S(1)}, u32[]{:S(2)}, u32[]{:S(2)}) %collective-permute-start.13) | collective-permute-done | bytes 65568 | tf_op jit(solution)/shard_map/ppermute | solution.py:274
  55.9 2.7 %collective-permute-done.14 = bf16[2,128,128]{2,1,0:T(8,128)(2,1)S(1)} collective-permute-done((bf16[2,128,128]{2,1,0:T(8,128)(2,1)S(1)}, bf16[2,128,128]{2,1,0:T(8,128)(2,1)S(1)}, u32[]{:S(2)}, u32[]{:S(2)}) %collective-permute-start.14) | collective-permute-done | bytes 65568 | tf_op jit(solution)/shard_map/ppermute | solution.py:274
  58.7 1.4 %finish.1 = bf16[256,512]{1,0:T(8,128)(2,1)} custom-call(s32[1]{0:T(128)} %bitcast.me_ref, bf16[256,512]{1,0:T(8,128)(2,1)S(1)} %copy-done.2, bf16[8,128,128]{2,1,0:T(8,128)(2,1)S(1)} %constant_dynamic-update-slice_fusion.16.attention_ref, bf16[256,512]{1,0:T(8,128)(2,1)S(1)} %project_gating.1.gating_ref, bf16[512,512]{1,0:T(8,128)(2,1)S(1)} %copy-done.3), custom_call_target="tpu_custom_call" | custom-call | tf_op jit(solution)/shard_map/finish/pallas_call | solution.py:376
  (87 shorter events, 4.8 us)
Async XLA Ops:
  0.0 11.4 %copy-start.4 = (s32[8]{0:T(128)S(1)}, s32[8]{0:T(128)}, u32[]{:S(2)}) copy-start(s32[8]{0:T(128)} %constant.127.clone) | copy-start | bytes 100
  0.0 10.8 %copy-start.5 = (s32[64]{0:T(128)S(1)}, s32[64]{0:T(128)}, u32[]{:S(2)}) copy-start(s32[64]{0:T(128)} %param.8) | copy-start | bytes 772
  0.0 1.0 %copy-start.1 = (bf16[256,512]{1,0:T(8,128)(2,1)S(1)}, bf16[256,512]{1,0:T(8,128)(2,1)}, u32[]{:S(2)}) copy-start(bf16[256,512]{1,0:T(8,128)(2,1)} %tokens_ref.4) | copy-start | bytes 786436
  3.3 8.7 %collective-permute-start = (bf16[384,128]{1,0:T(8,128)(2,1)S(1)}, bf16[384,128]{1,0:T(8,128)(2,1)S(1)}, u32[]{:S(2)}, u32[]{:S(2)}) collective-permute-start(bf16[384,128]{1,0:T(8,128)(2,1)S(1)} %get-tuple-element.27), channel_id=1, source_target_pairs={{0,1},{1,0},{2,3},{3,2},{4,5},{5,4},{6,7},{7,6},{8,9},{9,8},{10,11... | collective-permute-start | bytes 294920 | tf_op jit(solution)/shard_map/ppermute | solution.py:274
  5.0 8.3 %collective-permute-start.1 = (bf16[384,128]{1,0:T(8,128)(2,1)S(1)}, bf16[384,128]{1,0:T(8,128)(2,1)S(1)}, u32[]{:S(2)}, u32[]{:S(2)}) collective-permute-start(bf16[384,128]{1,0:T(8,128)(2,1)S(1)} %get-tuple-element.28), channel_id=1, source_target_pairs={{0,9},{1,8},{2,11},{3,10},{4,13},{5,12},{6,15},{7,14},{8,1},{9,0},... | collective-permute-start | bytes 294920 | tf_op jit(solution)/shard_map/ppermute | solution.py:274
  6.3 11.5 %collective-permute-start.2 = (bf16[384,128]{1,0:T(8,128)(2,1)S(1)}, bf16[384,128]{1,0:T(8,128)(2,1)S(1)}, u32[]{:S(2)}, u32[]{:S(2)}) collective-permute-start(bf16[384,128]{1,0:T(8,128)(2,1)S(1)} %get-tuple-element.30), channel_id=1, source_target_pairs={{0,2},{1,3},{2,0},{3,1},{4,6},{5,7},{6,4},{7,5},{8,10},{9,11},{10,... | collective-permute-start | bytes 294920 | tf_op jit(solution)/shard_map/ppermute | solution.py:274
  8.9 8.9 %collective-permute-start.3 = (bf16[384,128]{1,0:T(8,128)(2,1)S(1)}, bf16[384,128]{1,0:T(8,128)(2,1)S(1)}, u32[]{:S(2)}, u32[]{:S(2)}) collective-permute-start(bf16[384,128]{1,0:T(8,128)(2,1)S(1)} %get-tuple-element.31), channel_id=1, source_target_pairs={{0,3},{1,2},{2,1},{3,0},{4,7},{5,6},{6,5},{7,4},{8,11},{9,10},{10,... | collective-permute-start | bytes 294920 | tf_op jit(solution)/shard_map/ppermute | solution.py:274
  10.3 7.6 %collective-permute-start.4 = (bf16[384,128]{1,0:T(8,128)(2,1)S(1)}, bf16[384,128]{1,0:T(8,128)(2,1)S(1)}, u32[]{:S(2)}, u32[]{:S(2)}) collective-permute-start(bf16[384,128]{1,0:T(8,128)(2,1)S(1)} %get-tuple-element.33), channel_id=1, source_target_pairs={{0,8},{1,9},{2,10},{3,11},{4,12},{5,13},{6,14},{7,15},{8,0},{9,1},... | collective-permute-start | bytes 294920 | tf_op jit(solution)/shard_map/ppermute | solution.py:274
  13.2 12.0 %collective-permute-start.6 = (bf16[384,128]{1,0:T(8,128)(2,1)S(1)}, bf16[384,128]{1,0:T(8,128)(2,1)S(1)}, u32[]{:S(2)}, u32[]{:S(2)}) collective-permute-start(bf16[384,128]{1,0:T(8,128)(2,1)S(1)} %get-tuple-element.34), channel_id=1, source_target_pairs={{0,10},{1,11},{2,8},{3,9},{4,14},{5,15},{6,12},{7,13},{8,2},{9,3},... | collective-permute-start | bytes 294920 | tf_op jit(solution)/shard_map/ppermute | solution.py:274
  15.2 10.1 %collective-permute-start.7 = (bf16[384,128]{1,0:T(8,128)(2,1)S(1)}, bf16[384,128]{1,0:T(8,128)(2,1)S(1)}, u32[]{:S(2)}, u32[]{:S(2)}) collective-permute-start(bf16[384,128]{1,0:T(8,128)(2,1)S(1)} %get-tuple-element.35), channel_id=1, source_target_pairs={{0,11},{1,10},{2,9},{3,8},{4,15},{5,14},{6,13},{7,12},{8,3},{9,2},... | collective-permute-start | bytes 294920 | tf_op jit(solution)/shard_map/ppermute | solution.py:274
  17.9 15.6 %collective-permute-start.5 = (bf16[4,256,128]{2,1,0:T(8,128)(2,1)S(1)}, bf16[4,256,128]{2,1,0:T(8,128)(2,1)S(1)}, u32[]{:S(2)}, u32[]{:S(2)}) collective-permute-start(bf16[4,256,128]{2,1,0:T(8,128)(2,1)S(1)} %pad_maximum_fusion.1), channel_id=1, source_target_pairs={{0,16},{4,20},{8,24},{12,28},{16,0},{20,4},{24,8},{28,12},{1,17},{... | collective-permute-start | bytes 786440 | tf_op jit(solution)/shard_map/ppermute | solution.py:277
  25.2 4.0 %collective-permute-start.9 = (bf16[8,128,128]{2,1,0:T(8,128)(2,1)S(1)}, bf16[8,128,128]{2,1,0:T(8,128)(2,1)S(1)}, u32[]{:S(2)}, u32[]{:S(2)}) collective-permute-start(bf16[8,128,128]{2,1,0:T(8,128)(2,1)S(1)} %constant_dynamic-update-slice_fusion.queries_ref), channel_id=1, source_target_pairs={{0,4},{4,0},{8,12},{12,8},{16,20},{20,16},{24,28},{28,24},{1,5},{5... | collective-permute-start | bytes 786440 | tf_op jit(solution)/shard_map/ppermute | solution.py:277
  25.4 8.8 %collective-permute-start.8 = (bf16[4,256,128]{2,1,0:T(8,128)(2,1)S(1)}, bf16[4,256,128]{2,1,0:T(8,128)(2,1)S(1)}, u32[]{:S(2)}, u32[]{:S(2)}) collective-permute-start(bf16[4,256,128]{2,1,0:T(8,128)(2,1)S(1)} %pad_maximum_fusion.2), channel_id=1, source_target_pairs={{0,16},{4,20},{8,24},{12,28},{16,0},{20,4},{24,8},{28,12},{1,17},{... | collective-permute-start | bytes 786440 | tf_op jit(solution)/shard_map/ppermute | solution.py:277
  29.3 3.6 %copy-start = (bf16[512,2048]{1,0:T(8,128)(2,1)S(1)}, bf16[512,2048]{1,0:T(8,128)(2,1)}, u32[]{:S(2)}) copy-start(bf16[512,2048]{1,0:T(8,128)(2,1)} %weights_ref.4) | copy-start | bytes 6291460
  29.3 3.6 %copy-start.2 = (bf16[256,512]{1,0:T(8,128)(2,1)S(1)}, bf16[256,512]{1,0:T(8,128)(2,1)}, u32[]{:S(2)}) copy-start(bf16[256,512]{1,0:T(8,128)(2,1)} %tokens_ref.4) | copy-start | bytes 786436
  38.6 1.6 %collective-permute-start.10 = (bf16[8,128,128]{2,1,0:T(8,128)(2,1)S(1)}, bf16[8,128,128]{2,1,0:T(8,128)(2,1)S(1)}, u32[]{:S(2)}, u32[]{:S(2)}) collective-permute-start(bf16[8,128,128]{2,1,0:T(8,128)(2,1)S(1)} %attend.8), channel_id=1, source_target_pairs={{0,4},{4,0},{8,12},{12,8},{16,20},{20,16},{24,28},{28,24},{1,5},{5... | collective-permute-start | bytes 786440 | tf_op jit(solution)/shard_map/ppermute | solution.py:277
  40.3 8.1 %collective-permute-start.11 = (bf16[4,128,128]{2,1,0:T(8,128)(2,1)S(1)}, bf16[4,128,128]{2,1,0:T(8,128)(2,1)S(1)}, u32[]{:S(2)}, u32[]{:S(2)}) collective-permute-start(bf16[4,128,128]{2,1,0:T(8,128)(2,1)S(1)} %add_convert_fusion), channel_id=1, source_target_pairs={{0,8},{1,9},{2,10},{3,11},{4,12},{5,13},{6,14},{7,15},{8,0},{9,1},... | collective-permute-start | bytes 393224 | tf_op jit(solution)/shard_map/ppermute | solution.py:274
  44.2 14.5 %copy-start.3 = (bf16[512,512]{1,0:T(8,128)(2,1)S(1)}, bf16[512,512]{1,0:T(8,128)(2,1)}, u32[]{:S(2)}) copy-start(bf16[512,512]{1,0:T(8,128)(2,1)} %weights_ref.5) | copy-start | bytes 1572868
  48.4 5.1 %collective-permute-start.12 = (bf16[2,128,128]{2,1,0:T(8,128)(2,1)S(1)}, bf16[2,128,128]{2,1,0:T(8,128)(2,1)S(1)}, u32[]{:S(2)}, u32[]{:S(2)}) collective-permute-start(bf16[2,128,128]{2,1,0:T(8,128)(2,1)S(1)} %pad_maximum_fusion.5), channel_id=1, source_target_pairs={{0,1},{1,0},{2,3},{3,2},{4,5},{5,4},{6,7},{7,6},{8,9},{9,8},{10,11... | collective-permute-start | bytes 196616 | tf_op jit(solution)/shard_map/ppermute | solution.py:274
  50.4 5.5 %collective-permute-start.13 = (bf16[2,128,128]{2,1,0:T(8,128)(2,1)S(1)}, bf16[2,128,128]{2,1,0:T(8,128)(2,1)S(1)}, u32[]{:S(2)}, u32[]{:S(2)}) collective-permute-start(bf16[2,128,128]{2,1,0:T(8,128)(2,1)S(1)} %pad_maximum_fusion.6), channel_id=1, source_target_pairs={{0,2},{1,3},{2,0},{3,1},{4,6},{5,7},{6,4},{7,5},{8,10},{9,11},{10,... | collective-permute-start | bytes 196616 | tf_op jit(solution)/shard_map/ppermute | solution.py:274
  52.3 6.4 %collective-permute-start.14 = (bf16[2,128,128]{2,1,0:T(8,128)(2,1)S(1)}, bf16[2,128,128]{2,1,0:T(8,128)(2,1)S(1)}, u32[]{:S(2)}, u32[]{:S(2)}) collective-permute-start(bf16[2,128,128]{2,1,0:T(8,128)(2,1)S(1)} %pad_maximum_fusion.7), channel_id=1, source_target_pairs={{0,3},{1,2},{2,1},{3,0},{4,7},{5,6},{6,5},{7,4},{8,11},{9,10},{10,... | collective-permute-start | bytes 196616 | tf_op jit(solution)/shard_map/ppermute | solution.py:274

commit v7 on v6

--- a/solution.py
+++ b/solution.py
@@ -69,13 +69,16 @@
     keys = silu(jnp.dot(normed, weights[0], preferred_element_type=f32))
     wait(2)
     values = silu(jnp.dot(normed, weights[1], preferred_element_type=f32))
+    for pair in range(H // 2):
+        at = slice(pair * LANES, (pair + 1) * LANES)
+        key, value = keys[:, at], values[:, at]
+        held[2 * pair, :rows] = jnp.where(low, key, swap_halves(value)).astype(bf16)
+        held[2 * pair + 1, :rows] = jnp.where(low, swap_halves(key), value).astype(bf16)
     wait(3)
     queries = silu(jnp.dot(normed, weights[2], preferred_element_type=f32)) * scale
     for pair in range(H // 2):
         at = slice(pair * LANES, (pair + 1) * LANES)
-        key, value, upper, lower = keys[:, at], values[:, at], queries[:half, at], queries[half:, at]
-        held[2 * pair, :rows] = jnp.where(low, key, swap_halves(value)).astype(bf16)
-        held[2 * pair + 1, :rows] = jnp.where(low, swap_halves(key), value).astype(bf16)
+        upper, lower = queries[:half, at], queries[half:, at]
         held[2 * pair, rows:] = jnp.where(half_low, upper, swap_halves(lower)).astype(bf16)
         held[2 * pair + 1, rows:] = jnp.where(half_low, swap_halves(upper), lower).astype(bf16)
     for k, out in enumerate(outs):
@@ -287,7 +290,7 @@
             pltpu.VMEM((H, rows + half, LANES), bf16),
             pltpu.SemaphoreType.DMA((7,)),
         ],
-        compiler_params=pltpu.CompilerParams(vmem_limit_bytes=52 << 20),
+        compiler_params=pltpu.CompilerParams(vmem_limit_bytes=53 << 20),
         name="project",
     )(me_array, tokens, w_proj)
     def gating_of(tokens):
@@ -325,13 +328,10 @@
     arrived = {0: sent[0]}
     for k in order[1:-2]:
         arrived[k] = partner(sent[k], k)
-    nearest = order[1:3]
-    *held_back, arrived[nearest[0]], arrived[nearest[1]] = lax.optimization_barrier(
-        (sent[order[-2]], sent[order[-1]], arrived[nearest[0]], arrived[nearest[1]])
-    )
+    first_lot = jnp.stack([arrived[k][:rows] for k in order[:TEAM]])
+    *held_back, first_lot = lax.optimization_barrier((sent[order[-2]], sent[order[-1]], first_lot))
     for k, array in zip(order[-2:], held_back):
         arrived[k] = partner(array, k)
-    first_lot = jnp.stack([arrived[k][:rows] for k in order[:TEAM]])
     queries = jnp.stack([arrived[k][rows:] for k in range(H)])
     lots = [first_lot, jnp.stack([arrived[k][:rows] for k in order[TEAM:]])]
     keys = jnp.concatenate(lots)
@@ -356,23 +356,16 @@
             tables(others, 1 - group), other_queries, far_keys, bf16, near_theirs
         )
         theirs = seq_flip(theirs, 1)
-        team_b = attend_call(
-            tables(mine[TEAM:], 1 - group), queries[TEAM:], far_keys, f32, near_ours[TEAM:]
-        )
-        attention_b = (team_b + theirs[TEAM:].astype(f32)).astype(bf16)
-        attention_b, near_a = lax.optimization_barrier((attention_b, near_ours[:TEAM]))
-        attention_a = attend_call(
-            tables(mine[:TEAM], 1 - group), queries[:TEAM], far_keys, bf16, near_a, theirs[:TEAM]
-        )
+        ours = attend_call(tables(mine, 1 - group), queries, far_keys, f32, near_ours)
+        attention = (ours + theirs.astype(f32)).astype(bf16)
     else:
         everything = lax.all_gather(keys, "seq", axis=0, tiled=True)
         index = jnp.arange(blocks, dtype=jnp.int32)
         slot = index // head_size * H + place_of[jnp.bitwise_xor(index % head_size, me)]
         tables = (start, 1.0 / length, mine, index[::TEAM], slot)
         attention = attend_call(tables, queries, everything, bf16)
-        attention_a, attention_b = attention[:TEAM], attention[TEAM:]
         gating = gating_of(tokens)
-    returned = exchange(attention_a, partner(attention_b, TEAM))
+    returned = exchange(attention[:TEAM], partner(attention[TEAM:], TEAM))
     return pl.pallas_call(
         finish,
         out_shape=jax.ShapeDtypeStruct((rows, width), bf16),

time: 60.9 us -> 62.9 us (1.033); the launches traced: 60.1 us -> 62.8 us
  waiting for transfers between devices: 15.1 us -> 19.8 us
  Pallas kernels: 20.5 us -> 19.1 us
  local copies, waits for them, and re-layouts: 2.1 us -> 0.96 us
    ppermute x11, waiting for transfers between devices: 14.1 us -> 19.8 us  [partner(): return lax.ppermute(array, ('seq', 'head'), pairs)]
    ppermute x4, starting transfers between devices: 1.08 us -> 5.34 us  [seq_flip(): return lax.ppermute(array, 'seq', [(s, s ^ bit) for s in range(seq_size)])]
    ppermute x11, starting transfers between devices: 20.2 us -> 16.5 us  [partner(): return lax.ppermute(array, ('seq', 'head'), pairs)]
    pallas_call x5 -> x4, Pallas kernels: 16.2 us -> 14.5 us  [attend_call(): pl.pallas_call(attend, grid_spec=pltpu.PrefetchScalarGridSpec(num_scalar_...]
    unnamed x32 -> x27, local copies, waits for them, and re-layouts: 1.21 us -> 0.21 us
    ppermute x4, waiting for transfers between devices: 1 us -> 0.01 us  [seq_flip(): return lax.ppermute(array, 'seq', [(s, s ^ bit) for s in range(seq_size)])]
  transfers between devices with their start and end apart: 15 -> 15, of which waited for: 8 -> 5; matrix products, arithmetic and copies ran while one was open for 3% -> 2% of each run, Pallas kernels for 21% -> 20%
where the time goes in v7:
time: 62.9 us; the launch traced here: 62.8 us
  starting transfers between devices  21.8 us (35%)
  waiting for transfers between devices  19.8 us (31%)
  Pallas kernels  19.1 us (30%)
  local copies, waits for them, and re-layouts  0.96 us (2%)
  other arithmetic  0.63 us (1%)
    ppermute x11, waiting for transfers between devices, partner(): return lax.ppermute(array, ('seq', 'head'), pairs)  19.8 us
    ppermute x11, starting transfers between devices, partner(): return lax.ppermute(array, ('seq', 'head'), pairs)  16.5 us
    pallas_call x4, Pallas kernels, attend_call(): pl.pallas_call(attend, grid_spec=pltpu.PrefetchScalarGridSpec(num_scalar_...  14.5 us
    ppermute x4, starting transfers between devices, seq_flip(): return lax.ppermute(array, 'seq', [(s, s ^ bit) for s in range(seq_size)])  5.34 us
    pallas_call x1, Pallas kernels, per_device(): pl.pallas_call(project, out_shape=[jax.ShapeDtypeStruct((rows + half, LAN...  2.58 us
    pallas_call x1, Pallas kernels, per_device(): pl.pallas_call(finish, out_shape=jax.ShapeDtypeStruct((rows, width), bf16...  1.42 us
  transfers between devices with their start and end apart: 15, of which 5 were waited for; matrix products, arithmetic and copies ran while one was open for 2% of the time, Pallas kernels for 20%

profile of v7, /device:TPU:4, one launch (start us, length us, event | category | flops | bytes accessed | tf_op | source)
XLA Modules:
  0.0 62.8 jit_solution(11156781957393707166)
XLA Ops:
  0.0 2.6 %project.1 = (bf16[384,128]{1,0:T(8,128)(2,1)S(1)}, bf16[384,128]{1,0:T(8,128)(2,1)S(1)}, bf16[384,128]{1,0:T(8,128)(2,1)S(1)}, bf16[384,128]{1,0:T(8,128)(2,1)S...) custom-call(s32[1]{0:T(128)} %bitcast.me_ref, ...), custom_call_target="tpu_custom_call" | custom-call | tf_op jit(solution)/shard_map/project/pallas_call | solution.py:282
  2.6 1.6 %collective-permute-start = (bf16[384,128]{1,0:T(8,128)(2,1)S(1)}, bf16[384,128]{1,0:T(8,128)(2,1)S(1)}, u32[]{:S(2)}, u32[]{:S(2)}) collective-permute-start(bf16[384,128]{1,0:T(8,128)(2,1)S(1)} %get-tuple-element.22), channel_id=1, source_target_pairs={{0,1},{1,0},{2,3},{3,2},{4,5},{5,4},{6,7},{7,6},{8,9},{9,8},{10,11... | collective-permute-start | bytes 294920 | tf_op jit(solution)/shard_map/ppermute | solution.py:277
  4.2 2.6 %collective-permute-start.1 = (bf16[384,128]{1,0:T(8,128)(2,1)S(1)}, bf16[384,128]{1,0:T(8,128)(2,1)S(1)}, u32[]{:S(2)}, u32[]{:S(2)}) collective-permute-start(bf16[384,128]{1,0:T(8,128)(2,1)S(1)} %get-tuple-element.23), channel_id=1, source_target_pairs={{0,2},{1,3},{2,0},{3,1},{4,6},{5,7},{6,4},{7,5},{8,10},{9,11},{10,... | collective-permute-start | bytes 294920 | tf_op jit(solution)/shard_map/ppermute | solution.py:277
  7.0 1.5 %collective-permute-start.3 = (bf16[384,128]{1,0:T(8,128)(2,1)S(1)}, bf16[384,128]{1,0:T(8,128)(2,1)S(1)}, u32[]{:S(2)}, u32[]{:S(2)}) collective-permute-start(bf16[384,128]{1,0:T(8,128)(2,1)S(1)} %get-tuple-element.25), channel_id=1, source_target_pairs={{0,8},{1,9},{2,10},{3,11},{4,12},{5,13},{6,14},{7,15},{8,0},{9,1},... | collective-permute-start | bytes 294920 | tf_op jit(solution)/shard_map/ppermute | solution.py:277
  8.5 0.6 %collective-permute-start.4 = (bf16[384,128]{1,0:T(8,128)(2,1)S(1)}, bf16[384,128]{1,0:T(8,128)(2,1)S(1)}, u32[]{:S(2)}, u32[]{:S(2)}) collective-permute-start(bf16[384,128]{1,0:T(8,128)(2,1)S(1)} %get-tuple-element.26), channel_id=1, source_target_pairs={{0,9},{1,8},{2,11},{3,10},{4,13},{5,12},{6,15},{7,14},{8,1},{9,0},... | collective-permute-start | bytes 294920 | tf_op jit(solution)/shard_map/ppermute | solution.py:277
  9.7 0.6 %gather_fusion = s32[8]{0:T(128)S(1)} fusion(s32[8]{0:T(128)S(1)} %copy-done.3, s32[1024]{0:T(1024)S(1)} %pad_clamp_fusion), kind=kCustom, calls=%fused_computation | custom fusion | bytes 96 | tf_op jit(solution)/shard_map/gather | solution.py:347
  10.4 2.3 %collective-permute-done.3 = bf16[384,128]{1,0:T(8,128)(2,1)S(1)} collective-permute-done((bf16[384,128]{1,0:T(8,128)(2,1)S(1)}, bf16[384,128]{1,0:T(8,128)(2,1)S(1)}, u32[]{:S(2)}, u32[]{:S(2)}) %collective-permute-start.3) | collective-permute-done | bytes 98336 | tf_op jit(solution)/shard_map/ppermute | solution.py:277
  12.7 3.3 %collective-permute-done.4 = bf16[384,128]{1,0:T(8,128)(2,1)S(1)} collective-permute-done((bf16[384,128]{1,0:T(8,128)(2,1)S(1)}, bf16[384,128]{1,0:T(8,128)(2,1)S(1)}, u32[]{:S(2)}, u32[]{:S(2)}) %collective-permute-start.4) | collective-permute-done | bytes 98336 | tf_op jit(solution)/shard_map/ppermute | solution.py:277
  16.1 1.0 %collective-permute-start.5 = (bf16[384,128]{1,0:T(8,128)(2,1)S(1)}, bf16[384,128]{1,0:T(8,128)(2,1)S(1)}, u32[]{:S(2)}, u32[]{:S(2)}) collective-permute-start(bf16[384,128]{1,0:T(8,128)(2,1)S(1)} %get-tuple-element.29), channel_id=1, source_target_pairs={{0,10},{1,11},{2,8},{3,9},{4,14},{5,15},{6,12},{7,13},{8,2},{9,3},... | collective-permute-start | bytes 294920 | tf_op jit(solution)/shard_map/ppermute | solution.py:277
  17.1 2.5 %collective-permute-start.6 = (bf16[384,128]{1,0:T(8,128)(2,1)S(1)}, bf16[384,128]{1,0:T(8,128)(2,1)S(1)}, u32[]{:S(2)}, u32[]{:S(2)}) collective-permute-start(bf16[384,128]{1,0:T(8,128)(2,1)S(1)} %get-tuple-element.30), channel_id=1, source_target_pairs={{0,11},{1,10},{2,9},{3,8},{4,15},{5,14},{6,13},{7,12},{8,3},{9,2},... | collective-permute-start | bytes 294920 | tf_op jit(solution)/shard_map/ppermute | solution.py:277
  20.3 5.4 %collective-permute-done.5 = bf16[384,128]{1,0:T(8,128)(2,1)S(1)} collective-permute-done((bf16[384,128]{1,0:T(8,128)(2,1)S(1)}, bf16[384,128]{1,0:T(8,128)(2,1)S(1)}, u32[]{:S(2)}, u32[]{:S(2)}) %collective-permute-start.5) | collective-permute-done | bytes 98336 | tf_op jit(solution)/shard_map/ppermute | solution.py:277
  26.5 5.2 %attend.5.refs_0_ = f32[8,128,128]{2,1,0:T(8,128)S(1)} custom-call(s32[64]{0:T(128)S(1)} %convert_reduce_fusion.1.start_ref, f32[64]{0:T(128)S(1)} %multiply_divide_fusion.inverse_ref, s32[8]{0:T(128)S(1)} %get-tuple-element.45.block_ref, s32[2]{0:T(128)S(1)} %multiply_add_fusion.team_ref, s32[8]{0:T(128)S(1)} %gather_fusion, ...), custom_call_target="tpu_custom_call" | custom-call | flops 4000000000 | bytes 4000000 | tf_op jit(solution)/shard_map/attend/pallas_call | solution.py:204
  31.8 2.5 %attend.4.refs_0_ = f32[8,128,128]{2,1,0:T(8,128)S(1)} custom-call(s32[64]{0:T(128)S(1)} %convert_reduce_fusion.1.start_ref, f32[64]{0:T(128)S(1)} %multiply_divide_fusion.inverse_ref, s32[8]{0:T(128)S(1)} %get-tuple-element.44.block_ref, s32[2]{0:T(128)S(1)} %multiply_add_fusion.team_ref, s32[8]{0:T(128)S(1)} %gather_fusion, ...), custom_call_target="tpu_custom_call" | custom-call | flops 4000000000 | bytes 4000000 | tf_op jit(solution)/shard_map/attend/pallas_call | solution.py:204
  34.3 0.6 project_gating.1.gating_ref
  35.0 2.7 %attend.7 = bf16[8,128,128]{2,1,0:T(8,128)(2,1)S(1)} custom-call(s32[64]{0:T(128)S(1)} %convert_reduce_fusion.1.start_ref, f32[64]{0:T(128)S(1)} %multiply_divide_fusion.inverse_ref, s32[8]{0:T(128)S(1)} %get-tuple-element.44.block_ref, s32[2]{0:T(128)S(1)} %multiply_add_fusion.2.team_ref, s32[8]{0:T(128)S(1)} %gather_fusion, ...), custom_call_target="tpu_custom_call" | custom-call | flops 4000000000 | bytes 4000000 | tf_op jit(solution)/shard_map/attend/pallas_call | solution.py:204
  37.8 4.2 %collective-permute-start.10 = (bf16[8,128,128]{2,1,0:T(8,128)(2,1)S(1)}, bf16[8,128,128]{2,1,0:T(8,128)(2,1)S(1)}, u32[]{:S(2)}, u32[]{:S(2)}) collective-permute-start(bf16[8,128,128]{2,1,0:T(8,128)(2,1)S(1)} %attend.7), channel_id=1, source_target_pairs={{0,4},{4,0},{8,12},{12,8},{16,20},{20,16},{24,28},{28,24},{1,5},{5... | collective-permute-start | bytes 786440 | tf_op jit(solution)/shard_map/ppermute | solution.py:280
  42.0 4.1 %attend.6 = f32[8,128,128]{2,1,0:T(8,128)S(1)} custom-call(s32[64]{0:T(128)S(1)} %convert_reduce_fusion.1.start_ref, f32[64]{0:T(128)S(1)} %multiply_divide_fusion.inverse_ref, s32[8]{0:T(128)S(1)} %get-tuple-element.45.block_ref, s32[2]{0:T(128)S(1)} %multiply_add_fusion.2.team_ref, s32[8]{0:T(128)S(1)} %gather_fusion, ...), custom_call_target="tpu_custom_call" | custom-call | flops 4000000000 | bytes 4000000 | tf_op jit(solution)/shard_map/attend/pallas_call | solution.py:204
  46.2 1.4 %collective-permute-start.11 = (bf16[4,128,128]{2,1,0:T(8,128)(2,1)S(1)}, bf16[4,128,128]{2,1,0:T(8,128)(2,1)S(1)}, u32[]{:S(2)}, u32[]{:S(2)}) collective-permute-start(bf16[4,128,128]{2,1,0:T(8,128)(2,1)S(1)} %slice.147), channel_id=1, source_target_pairs={{0,8},{1,9},{2,10},{3,11},{4,12},{5,13},{6,14},{7,15},{8,0},{9,1},... | collective-permute-start | bytes 393224 | tf_op jit(solution)/shard_map/ppermute | solution.py:277
  47.5 4.1 %collective-permute-done.11 = bf16[4,128,128]{2,1,0:T(8,128)(2,1)S(1)} collective-permute-done((bf16[4,128,128]{2,1,0:T(8,128)(2,1)S(1)}, bf16[4,128,128]{2,1,0:T(8,128)(2,1)S(1)}, u32[]{:S(2)}, u32[]{:S(2)}) %collective-permute-start.11) | collective-permute-done | bytes 131104 | tf_op jit(solution)/shard_map/ppermute | solution.py:277
  51.6 1.6 %collective-permute-start.12 = (bf16[2,128,128]{2,1,0:T(8,128)(2,1)S(1)}, bf16[2,128,128]{2,1,0:T(8,128)(2,1)S(1)}, u32[]{:S(2)}, u32[]{:S(2)}) collective-permute-start(bf16[2,128,128]{2,1,0:T(8,128)(2,1)S(1)} %pad_maximum_fusion.3), channel_id=1, source_target_pairs={{0,1},{1,0},{2,3},{3,2},{4,5},{5,4},{6,7},{7,6},{8,9},{9,8},{10,11... | collective-permute-start | bytes 196616 | tf_op jit(solution)/shard_map/ppermute | solution.py:277
  53.3 1.9 %collective-permute-start.13 = (bf16[2,128,128]{2,1,0:T(8,128)(2,1)S(1)}, bf16[2,128,128]{2,1,0:T(8,128)(2,1)S(1)}, u32[]{:S(2)}, u32[]{:S(2)}) collective-permute-start(bf16[2,128,128]{2,1,0:T(8,128)(2,1)S(1)} %pad_maximum_fusion.4), channel_id=1, source_target_pairs={{0,2},{1,3},{2,0},{3,1},{4,6},{5,7},{6,4},{7,5},{8,10},{9,11},{10,... | collective-permute-start | bytes 196616 | tf_op jit(solution)/shard_map/ppermute | solution.py:277
  55.1 1.5 %collective-permute-start.14 = (bf16[2,128,128]{2,1,0:T(8,128)(2,1)S(1)}, bf16[2,128,128]{2,1,0:T(8,128)(2,1)S(1)}, u32[]{:S(2)}, u32[]{:S(2)}) collective-permute-start(bf16[2,128,128]{2,1,0:T(8,128)(2,1)S(1)} %pad_maximum_fusion.5), channel_id=1, source_target_pairs={{0,3},{1,2},{2,1},{3,0},{4,7},{5,6},{6,5},{7,4},{8,11},{9,10},{10,... | collective-permute-start | bytes 196616 | tf_op jit(solution)/shard_map/ppermute | solution.py:277
  56.7 4.6 %collective-permute-done.13 = bf16[2,128,128]{2,1,0:T(8,128)(2,1)S(1)} collective-permute-done((bf16[2,128,128]{2,1,0:T(8,128)(2,1)S(1)}, bf16[2,128,128]{2,1,0:T(8,128)(2,1)S(1)}, u32[]{:S(2)}, u32[]{:S(2)}) %collective-permute-start.13) | collective-permute-done | bytes 65568 | tf_op jit(solution)/shard_map/ppermute | solution.py:277
  61.4 1.4 %finish.1 = bf16[256,512]{1,0:T(8,128)(2,1)} custom-call(s32[1]{0:T(128)} %bitcast.me_ref, bf16[256,512]{1,0:T(8,128)(2,1)S(1)} %copy-done.1, bf16[8,128,128]{2,1,0:T(8,128)(2,1)S(1)} %constant_dynamic-update-slice_fusion.13.attention_ref, bf16[256,512]{1,0:T(8,128)(2,1)S(1)} %project_gating.1.gating_ref, bf16[512,512]{1,0:T(8,128)(2,1)S(1)} %copy-done.2), custom_call_target="tpu_custom_call" | custom-call | tf_op jit(solution)/shard_map/finish/pallas_call | solution.py:369
  (70 shorter events, 2.4 us)
Async XLA Ops:
  0.0 9.7 %copy-start.3 = (s32[8]{0:T(128)S(1)}, s32[8]{0:T(128)}, u32[]{:S(2)}) copy-start(s32[8]{0:T(128)} %constant.122.clone) | copy-start | bytes 100
  0.0 9.2 %copy-start.4 = (s32[64]{0:T(128)S(1)}, s32[64]{0:T(128)}, u32[]{:S(2)}) copy-start(s32[64]{0:T(128)} %param.8) | copy-start | bytes 772
  2.6 7.8 %collective-permute-start = (bf16[384,128]{1,0:T(8,128)(2,1)S(1)}, bf16[384,128]{1,0:T(8,128)(2,1)S(1)}, u32[]{:S(2)}, u32[]{:S(2)}) collective-permute-start(bf16[384,128]{1,0:T(8,128)(2,1)S(1)} %get-tuple-element.22), channel_id=1, source_target_pairs={{0,1},{1,0},{2,3},{3,2},{4,5},{5,4},{6,7},{7,6},{8,9},{9,8},{10,11... | collective-permute-start | bytes 294920 | tf_op jit(solution)/shard_map/ppermute | solution.py:277
  4.2 15.9 %collective-permute-start.1 = (bf16[384,128]{1,0:T(8,128)(2,1)S(1)}, bf16[384,128]{1,0:T(8,128)(2,1)S(1)}, u32[]{:S(2)}, u32[]{:S(2)}) collective-permute-start(bf16[384,128]{1,0:T(8,128)(2,1)S(1)} %get-tuple-element.23), channel_id=1, source_target_pairs={{0,2},{1,3},{2,0},{3,1},{4,6},{5,7},{6,4},{7,5},{8,10},{9,11},{10,... | collective-permute-start | bytes 294920 | tf_op jit(solution)/shard_map/ppermute | solution.py:277
  6.8 13.4 %collective-permute-start.2 = (bf16[384,128]{1,0:T(8,128)(2,1)S(1)}, bf16[384,128]{1,0:T(8,128)(2,1)S(1)}, u32[]{:S(2)}, u32[]{:S(2)}) collective-permute-start(bf16[384,128]{1,0:T(8,128)(2,1)S(1)} %get-tuple-element.24), channel_id=1, source_target_pairs={{0,3},{1,2},{2,1},{3,0},{4,7},{5,6},{6,5},{7,4},{8,11},{9,10},{10,... | collective-permute-start | bytes 294920 | tf_op jit(solution)/shard_map/ppermute | solution.py:277
  7.0 5.7 %collective-permute-start.3 = (bf16[384,128]{1,0:T(8,128)(2,1)S(1)}, bf16[384,128]{1,0:T(8,128)(2,1)S(1)}, u32[]{:S(2)}, u32[]{:S(2)}) collective-permute-start(bf16[384,128]{1,0:T(8,128)(2,1)S(1)} %get-tuple-element.25), channel_id=1, source_target_pairs={{0,8},{1,9},{2,10},{3,11},{4,12},{5,13},{6,14},{7,15},{8,0},{9,1},... | collective-permute-start | bytes 294920 | tf_op jit(solution)/shard_map/ppermute | solution.py:277
  8.5 7.5 %collective-permute-start.4 = (bf16[384,128]{1,0:T(8,128)(2,1)S(1)}, bf16[384,128]{1,0:T(8,128)(2,1)S(1)}, u32[]{:S(2)}, u32[]{:S(2)}) collective-permute-start(bf16[384,128]{1,0:T(8,128)(2,1)S(1)} %get-tuple-element.26), channel_id=1, source_target_pairs={{0,9},{1,8},{2,11},{3,10},{4,13},{5,12},{6,15},{7,14},{8,1},{9,0},... | collective-permute-start | bytes 294920 | tf_op jit(solution)/shard_map/ppermute | solution.py:277
  16.1 9.6 %collective-permute-start.5 = (bf16[384,128]{1,0:T(8,128)(2,1)S(1)}, bf16[384,128]{1,0:T(8,128)(2,1)S(1)}, u32[]{:S(2)}, u32[]{:S(2)}) collective-permute-start(bf16[384,128]{1,0:T(8,128)(2,1)S(1)} %get-tuple-element.29), channel_id=1, source_target_pairs={{0,10},{1,11},{2,8},{3,9},{4,14},{5,15},{6,12},{7,13},{8,2},{9,3},... | collective-permute-start | bytes 294920 | tf_op jit(solution)/shard_map/ppermute | solution.py:277
  17.1 8.7 %collective-permute-start.6 = (bf16[384,128]{1,0:T(8,128)(2,1)S(1)}, bf16[384,128]{1,0:T(8,128)(2,1)S(1)}, u32[]{:S(2)}, u32[]{:S(2)}) collective-permute-start(bf16[384,128]{1,0:T(8,128)(2,1)S(1)} %get-tuple-element.30), channel_id=1, source_target_pairs={{0,11},{1,10},{2,9},{3,8},{4,15},{5,14},{6,13},{7,12},{8,3},{9,2},... | collective-permute-start | bytes 294920 | tf_op jit(solution)/shard_map/ppermute | solution.py:277
  19.6 15.3 %collective-permute-start.7 = (bf16[4,256,128]{2,1,0:T(8,128)(2,1)S(1)}, bf16[4,256,128]{2,1,0:T(8,128)(2,1)S(1)}, u32[]{:S(2)}, u32[]{:S(2)}) collective-permute-start(bf16[4,256,128]{2,1,0:T(8,128)(2,1)S(1)} %pad_maximum_fusion.1), channel_id=1, source_target_pairs={{0,16},{4,20},{8,24},{12,28},{16,0},{20,4},{24,8},{28,12},{1,17},{... | collective-permute-start | bytes 786440 | tf_op jit(solution)/shard_map/ppermute | solution.py:280
  25.8 6.0 %collective-permute-start.9 = (bf16[8,128,128]{2,1,0:T(8,128)(2,1)S(1)}, bf16[8,128,128]{2,1,0:T(8,128)(2,1)S(1)}, u32[]{:S(2)}, u32[]{:S(2)}) collective-permute-start(bf16[8,128,128]{2,1,0:T(8,128)(2,1)S(1)} %constant_dynamic-update-slice_fusion.queries_ref), channel_id=1, source_target_pairs={{0,4},{4,0},{8,12},{12,8},{16,20},{20,16},{24,28},{28,24},{1,5},{5... | collective-permute-start | bytes 786440 | tf_op jit(solution)/shard_map/ppermute | solution.py:280
  25.9 9.0 %collective-permute-start.8 = (bf16[4,256,128]{2,1,0:T(8,128)(2,1)S(1)}, bf16[4,256,128]{2,1,0:T(8,128)(2,1)S(1)}, u32[]{:S(2)}, u32[]{:S(2)}) collective-permute-start(bf16[4,256,128]{2,1,0:T(8,128)(2,1)S(1)} %pad_maximum_fusion.2), channel_id=1, source_target_pairs={{0,16},{4,20},{8,24},{12,28},{16,0},{20,4},{24,8},{28,12},{1,17},{... | collective-permute-start | bytes 786440 | tf_op jit(solution)/shard_map/ppermute | solution.py:280
  31.8 2.5 %copy-start = (bf16[512,2048]{1,0:T(8,128)(2,1)S(1)}, bf16[512,2048]{1,0:T(8,128)(2,1)}, u32[]{:S(2)}) copy-start(bf16[512,2048]{1,0:T(8,128)(2,1)} %weights_ref.4) | copy-start | bytes 6291460
  31.8 2.5 %copy-start.1 = (bf16[256,512]{1,0:T(8,128)(2,1)S(1)}, bf16[256,512]{1,0:T(8,128)(2,1)}, u32[]{:S(2)}) copy-start(bf16[256,512]{1,0:T(8,128)(2,1)} %tokens_ref.4) | copy-start | bytes 786436
  37.8 8.3 %collective-permute-start.10 = (bf16[8,128,128]{2,1,0:T(8,128)(2,1)S(1)}, bf16[8,128,128]{2,1,0:T(8,128)(2,1)S(1)}, u32[]{:S(2)}, u32[]{:S(2)}) collective-permute-start(bf16[8,128,128]{2,1,0:T(8,128)(2,1)S(1)} %attend.7), channel_id=1, source_target_pairs={{0,4},{4,0},{8,12},{12,8},{16,20},{20,16},{24,28},{28,24},{1,5},{5... | collective-permute-start | bytes 786440 | tf_op jit(solution)/shard_map/ppermute | solution.py:280
  46.0 15.3 %copy-start.2 = (bf16[512,512]{1,0:T(8,128)(2,1)S(1)}, bf16[512,512]{1,0:T(8,128)(2,1)}, u32[]{:S(2)}) copy-start(bf16[512,512]{1,0:T(8,128)(2,1)} %weights_ref.5) | copy-start | bytes 1572868
  46.2 5.4 %collective-permute-start.11 = (bf16[4,128,128]{2,1,0:T(8,128)(2,1)S(1)}, bf16[4,128,128]{2,1,0:T(8,128)(2,1)S(1)}, u32[]{:S(2)}, u32[]{:S(2)}) collective-permute-start(bf16[4,128,128]{2,1,0:T(8,128)(2,1)S(1)} %slice.147), channel_id=1, source_target_pairs={{0,8},{1,9},{2,10},{3,11},{4,12},{5,13},{6,14},{7,15},{8,0},{9,1},... | collective-permute-start | bytes 393224 | tf_op jit(solution)/shard_map/ppermute | solution.py:277
  51.6 5.0 %collective-permute-start.12 = (bf16[2,128,128]{2,1,0:T(8,128)(2,1)S(1)}, bf16[2,128,128]{2,1,0:T(8,128)(2,1)S(1)}, u32[]{:S(2)}, u32[]{:S(2)}) collective-permute-start(bf16[2,128,128]{2,1,0:T(8,128)(2,1)S(1)} %pad_maximum_fusion.3), channel_id=1, source_target_pairs={{0,1},{1,0},{2,3},{3,2},{4,5},{5,4},{6,7},{7,6},{8,9},{9,8},{10,11... | collective-permute-start | bytes 196616 | tf_op jit(solution)/shard_map/ppermute | solution.py:277
  53.3 8.0 %collective-permute-start.13 = (bf16[2,128,128]{2,1,0:T(8,128)(2,1)S(1)}, bf16[2,128,128]{2,1,0:T(8,128)(2,1)S(1)}, u32[]{:S(2)}, u32[]{:S(2)}) collective-permute-start(bf16[2,128,128]{2,1,0:T(8,128)(2,1)S(1)} %pad_maximum_fusion.4), channel_id=1, source_target_pairs={{0,2},{1,3},{2,0},{3,1},{4,6},{5,7},{6,4},{7,5},{8,10},{9,11},{10,... | collective-permute-start | bytes 196616 | tf_op jit(solution)/shard_map/ppermute | solution.py:277
  55.1 6.2 %collective-permute-start.14 = (bf16[2,128,128]{2,1,0:T(8,128)(2,1)S(1)}, bf16[2,128,128]{2,1,0:T(8,128)(2,1)S(1)}, u32[]{:S(2)}, u32[]{:S(2)}) collective-permute-start(bf16[2,128,128]{2,1,0:T(8,128)(2,1)S(1)} %pad_maximum_fusion.5), channel_id=1, source_target_pairs={{0,3},{1,2},{2,1},{3,0},{4,7},{5,6},{6,5},{7,4},{8,11},{9,10},{10,... | collective-permute-start | bytes 196616 | tf_op jit(solution)/shard_map/ppermute | solution.py:277
